TPU v7x, 32 devices: a whole 2x2x4 slice. The times are simulated.
32 devices in a mesh: seq: 16 (over z, y, x), head: 2 (over core).
Axes of the slice: x: 2, y: 2, z: 4, core: 2. Of those that a mesh axis runs over, the one named last changes fastest.
Arguments:
- tokens: bfloat16 [2, 2048, 512], P(None, 'seq'), may hold values from -6 to 6
- cotangent: bfloat16 [2, 2048, 512], P(None, 'seq'), may hold values from -6 to 6
- lengths: int32 [2, 1], replicated, may hold values from 2048 to 2048, as said below
- order: int32 [2, 32], replicated, may hold values from 0 to 31, as said below
- mix_gain: float32 [512], replicated, may hold values from 0.5 to 1.5
- in_value: bfloat16 [512, 1024], P('seq', 'head'), may hold values from -0.25 to 0.25
- in_gate: bfloat16 [512, 1024], P('seq', 'head'), may hold values from -0.25 to 0.25
- in_state: bfloat16 [512, 64], P('seq', 'head'), may hold values from -0.25 to 0.25
- in_rate: bfloat16 [512, 16], P('seq', 'head'), may hold values from -0.25 to 0.25
- rate_bias: float32 [16], P('head'), may hold values from -8 to -2
- decay_log: float32 [16], P('head'), may hold values from -0.7 to 0.7
- conv_taps: float32 [4, 1024], P(None, 'head'), may hold values from -3 to 3
- conv_bias: float32 [1024], P('head'), may hold values from -0.5 to 0.5
- skip_gain: float32 [1024], P('head'), may hold values from 0.5 to 1.5
- mix_out: bfloat16 [1024, 512], P('head', 'seq'), may hold values from -0.1875 to 0.1875
- att_gain: float32 [512], replicated, may hold values from 0.5 to 1.5
- qkv_proj: bfloat16 [512, 3, 512], P('seq', None, 'head'), may hold values from -0.25 to 0.25
- att_out: bfloat16 [512, 512], P('head', 'seq'), may hold values from -12 to 12
- mlp_gain: float32 [512], replicated, may hold values from 0.5 to 1.5
- mlp_up: bfloat16 [512, 2048], P('seq', 'head'), may hold values from -0.25 to 0.25
- mlp_down: bfloat16 [2048, 512], P('head', 'seq'), may hold values from -0.125 to 0.125
Outputs:
- layer_out: bfloat16 [2, 2048, 512], P(None, 'seq')
- tokens_grad: bfloat16 [2, 2048, 512], P(None, 'seq')
- mixgain_grad: float32 [512], replicated
- invalue_grad: float32 [512, 1024], P('seq', 'head')
- ingate_grad: float32 [512, 1024], P('seq', 'head')
- instate_grad: float32 [512, 64], P('seq', 'head')
- inrate_grad: float32 [512, 16], P('seq', 'head')
- ratebias_grad: float32 [16], P('head')
- decaylog_grad: float32 [16], P('head')
- convtaps_grad: float32 [4, 1024], P(None, 'head')
- convbias_grad: float32 [1024], P('head')
- skipgain_grad: float32 [1024], P('head')
- mixout_grad: float32 [1024, 512], P('head', 'seq')
- attgain_grad: float32 [512], replicated
- qkvproj_grad: float32 [512, 3, 512], P('seq', None, 'head')
- attout_grad: float32 [512, 512], P('head', 'seq')
- mlpgain_grad: float32 [512], replicated
- mlpup_grad: float32 [512, 2048], P('seq', 'head')
- mlpdown_grad: float32 [2048, 512], P('head', 'seq')
Inputs may be any that keep to these rules, and one draw needn't show every extreme that they name: Row b holds the lengths of the 1 sequence packed in micro-batch b, in stream order; they sum to 2048, and one of them is exactly 2048. `order`: row b is a permutation of the 32 stream blocks. One sequence of each micro-batch has places in the blocks held at positions 0, 16 and 31 of row b.
All inputs are finite; a program needn't handle non-finite values.
Results may differ from a plain program's by a relative error of at most 0.04.
Values may be sent and summed in bfloat16 or wider, within the bound.
No kernel may reach another device: no remote copies, remote signals or barrier semaphores. Data moves between devices by JAX's collectives and lax.ppermute only.
A program may use at most 256 MiB of HBM per device.

v0:
```python
import functools
import math

import jax
import jax.numpy as jnp
from jax import lax
from jax.experimental import pallas as pl
from jax.experimental.pallas import tpu as pltpu
from jax.sharding import PartitionSpec as P

NSTATE = 16
CONV = 4
AHEAD_DIM = 64


epsilon = 1e-05
highest = lax.Precision.HIGHEST


def rms_norm(values, gain_row):
    return (
        values * lax.rsqrt(jnp.mean(values * values, axis=-1, keepdims=True) + epsilon) * gain_row
    )


def gelu_tanh(values):
    return jax.nn.gelu(values, approximate=True)


def segment_of(position, seq_ends):
    bounds = seq_ends[:-1]
    return jnp.sum((jnp.asarray(position)[..., None] >= bounds).astype(jnp.int32), axis=-1)


def tap_valid(position, lag_rows, seq_ends):
    source = position - lag_rows
    return (
        (source >= 0) & (segment_of(source, seq_ends) == segment_of(position, seq_ends))
    ).astype(jnp.float32)


def slot_position(order_row, row_ids, half_rows):
    slot = row_ids // half_rows
    slot_table = jnp.arange(order_row.shape[0], dtype=jnp.int32)
    block = jnp.sum(jnp.where(slot[:, None] == slot_table[None, :], order_row[None, :], 0), axis=1)
    return block * half_rows + row_ids % half_rows


def stream_slots(order_row):
    slot_table = jnp.arange(order_row.shape[0], dtype=jnp.int32)
    return jnp.sum(
        jnp.where(order_row[None, :] == slot_table[:, None], slot_table[None, :], 0), axis=1
    )


def matmul(left_op, right_op):
    return jnp.dot(left_op, right_op, preferred_element_type=jnp.float32)


def transposed(left_op, right_op):
    return lax.dot_general(
        left_op, right_op, (((1,), (1,)), ((), ())), preferred_element_type=jnp.float32
    )


def left_gram(left_op, right_op):
    return lax.dot_general(
        left_op, right_op, (((0,), (0,)), ((), ())), preferred_element_type=jnp.float32
    )


def transposed_exact(left_op, right_op):
    return lax.dot_general(
        left_op,
        right_op,
        (((1,), (1,)), ((), ())),
        preferred_element_type=jnp.float32,
        precision=highest,
    )


def left_gram_exact(left_op, right_op):
    return lax.dot_general(
        left_op,
        right_op,
        (((0,), (0,)), ((), ())),
        preferred_element_type=jnp.float32,
        precision=highest,
    )


def keep_same(current):
    return current


def head_total(partial_rows):
    return lax.psum(partial_rows, "head")


def collect(in_value, in_gate, in_state, in_rate, qkv_proj, mlp_up, mix_out, att_out, mlp_down):
    return (
        lax.all_gather(in_value, "seq", axis=0, tiled=True),
        lax.all_gather(in_gate, "seq", axis=0, tiled=True),
        lax.all_gather(in_state, "seq", axis=0, tiled=True),
        lax.all_gather(in_rate, "seq", axis=0, tiled=True),
        lax.all_gather(qkv_proj, "seq", axis=0, tiled=True),
        lax.all_gather(mlp_up, "seq", axis=0, tiled=True),
        lax.all_gather(mix_out, "seq", axis=1, tiled=True),
        lax.all_gather(att_out, "seq", axis=1, tiled=True),
        lax.all_gather(mlp_down, "seq", axis=1, tiled=True),
    )


def reduce_grads(grad_parts):
    return (
        lax.psum_scatter(grad_parts[0], "seq", scatter_dimension=0, tiled=True),
        lax.psum_scatter(grad_parts[1], "seq", scatter_dimension=0, tiled=True),
        lax.psum_scatter(grad_parts[2], "seq", scatter_dimension=0, tiled=True),
        lax.psum_scatter(grad_parts[3], "seq", scatter_dimension=0, tiled=True),
        lax.psum_scatter(grad_parts[4], "seq", scatter_dimension=0, tiled=True),
        lax.psum_scatter(grad_parts[5], "seq", scatter_dimension=0, tiled=True),
        lax.psum_scatter(grad_parts[6], "seq", scatter_dimension=1, tiled=True),
        lax.psum_scatter(grad_parts[7], "seq", scatter_dimension=1, tiled=True),
        lax.psum_scatter(grad_parts[8], "seq", scatter_dimension=1, tiled=True),
    )


def fold_blocks(fold_fn, initial, arrays, block_rows):
    blocks_n = arrays[0].shape[0] // block_rows

    def one_step(block_index, current):
        offset = block_index * block_rows
        shards = tuple(
            (lax.dynamic_slice_in_dim(member, offset, block_rows, 0) for member in arrays)
        )
        return fold_fn(current, shards, offset)

    return lax.fori_loop(0, blocks_n, one_step, initial)


def add_parts(left_op, right_op):
    if left_op is None:
        return right_op
    return tuple((first_part + second_part for first_part, second_part in zip(left_op, right_op)))


def combine_state(earlier, later):
    return (earlier[0] * later[0], later[0][..., None, None] * earlier[1] + later[1])


def attention_probs(
    query_rows, key_rows, query_pos, key_pos, query_seg, key_seg, log_total, scaling
):
    allowed = ((key_pos[None, :] <= query_pos[:, None]) & (key_seg[None, :] == query_seg[:, None]))[
        :, None, :
    ]
    scores = (
        jnp.einsum("qhd,khd->qhk", query_rows, key_rows, preferred_element_type=jnp.float32)
        * scaling
    )
    return jnp.where(allowed, jnp.exp(jnp.where(allowed, scores - log_total[:, :, None], 0.0)), 0.0)


def scan_terms(mixed_x, step_size, bc_rows, decay_log, segment, seg_before):
    rows_n, heads_n = step_size.shape
    log_decay = -step_size * jnp.exp(decay_log)
    cumulative = jnp.cumsum(log_decay, axis=0)
    driving = step_size[:, :, None] * mixed_x.reshape(rows_n, heads_n, -1)
    tail_weight = (
        jnp.exp(cumulative[-1][None, :] - cumulative)
        * (segment == segment[-1]).astype(jnp.float32)[:, None]
    )
    local_state = jnp.einsum(
        "sh,shp,sn->hpn", tail_weight, driving, bc_rows[:, :NSTATE], precision=highest
    )
    through = jnp.exp(cumulative[-1]) * (segment[-1] == seg_before).astype(jnp.float32)
    return (cumulative, driving, through, local_state)


def scan_output(cumulative, driving, bc_rows, incoming, segment, seg_before):
    rows_n = cumulative.shape[0]
    row_ids = jnp.arange(rows_n, dtype=jnp.int32)
    allowed = ((row_ids[:, None] >= row_ids[None, :]) & (segment[:, None] == segment[None, :]))[
        :, :, None
    ]
    decays = jnp.where(
        allowed,
        jnp.exp(jnp.where(allowed, cumulative[:, None, :] - cumulative[None, :, :], 0.0)),
        0.0,
    )
    inner_cb = jnp.dot(bc_rows[:, NSTATE:], bc_rows[:, :NSTATE].T, precision=highest)
    output = jnp.einsum("tsh,shp->thp", decays * inner_cb[:, :, None], driving, precision=highest)
    inflow = jnp.exp(cumulative) * (segment == seg_before).astype(jnp.float32)[:, None]
    output = output + inflow[:, :, None] * jnp.einsum(
        "tn,hpn->thp", bc_rows[:, NSTATE:], incoming, precision=highest
    )
    return output.reshape(rows_n, -1)


def scan_whole(mixed_x, step_size, bc_rows, decay_log, incoming, segment, seg_before):
    cumulative, driving, through, local_state = scan_terms(
        mixed_x, step_size, bc_rows, decay_log, segment, seg_before
    )
    output = scan_output(cumulative, driving, bc_rows, incoming, segment, seg_before)
    return (output, through[:, None, None] * incoming + local_state)


def on_device(
    tokens,
    cotangent,
    lengths,
    order,
    mix_gain,
    in_value,
    in_gate,
    in_state,
    in_rate,
    rate_bias,
    decay_log,
    conv_taps,
    conv_bias,
    skip_gain,
    mix_out,
    att_gain,
    qkv_proj,
    att_out,
    mlp_gain,
    mlp_up,
    mlp_down,
):
    rows_n = tokens.shape[1]
    half_rows = rows_n // 2
    slots_n = 2 * lax.axis_size("seq")
    my_slot = 2 * lax.axis_index("seq")
    total_rows = rows_n * lax.axis_size("seq")
    block_rows = math.gcd(total_rows, 1024)
    scaling = AHEAD_DIM ** (-0.5)
    local_ids = jnp.arange(half_rows, dtype=jnp.int32)
    ext_ids = jnp.arange(half_rows + CONV - 1, dtype=jnp.int32)
    terms_all = jax.vmap(scan_terms, in_axes=(0, 0, 0, None, 0, 0))
    output_all = jax.vmap(scan_output, in_axes=(0, 0, 0, 0, 0, 0))
    whole_all = jax.vmap(scan_whole, in_axes=(0, 0, 0, None, 0, 0, 0))
    layer_list = []
    input_list = []
    big_sums = None
    small_sums = None
    for batch_index in range(tokens.shape[0]):
        (
            value_full,
            gate_full,
            state_full,
            rate_full,
            qkv_full,
            up_full,
            mixout_full,
            attout_full,
            down_full,
        ) = collect(
            in_value, in_gate, in_state, in_rate, qkv_proj, mlp_up, mix_out, att_out, mlp_down
        )
        seq_ends = jnp.cumsum(lengths[batch_index])
        order_row = order[batch_index]
        inverse = stream_slots(order_row)
        my_blocks = lax.dynamic_slice_in_dim(order_row, my_slot, 2)
        position = (my_blocks[:, None] * half_rows + local_ids[None, :]).reshape(rows_n)
        segment = segment_of(position, seq_ends)
        seg_blocks = segment.reshape(2, half_rows)
        seg_before = segment_of(my_blocks * half_rows - 1, seq_ends)
        hidden_in = tokens[batch_index].astype(jnp.float32)
        normed_one = rms_norm(hidden_in, mix_gain).astype(jnp.bfloat16)
        x_in = matmul(normed_one, value_full).astype(jnp.bfloat16)
        gate_in = matmul(normed_one, gate_full)
        bc_rows = matmul(normed_one, state_full)
        rate_in = matmul(normed_one, rate_full)
        step_size = jax.nn.softplus(rate_in + rate_bias)
        x_blocks = x_in.reshape(2, half_rows, -1)
        all_tails = lax.all_gather(x_blocks[:, half_rows - (CONV - 1) :], "seq", axis=0, tiled=True)
        pick_prev = (order_row[None, :] == my_blocks[:, None] - 1).astype(jnp.bfloat16)
        edge_rows = jnp.einsum(
            "bs,srd->brd", pick_prev, all_tails, preferred_element_type=jnp.float32
        )
        extended = jnp.concatenate([edge_rows, x_blocks.astype(jnp.float32)], axis=1)
        valid_taps = [
            tap_valid(position, CONV - 1 - tap_index, seq_ends).reshape(2, half_rows)
            for tap_index in range(CONV)
        ]
        conv_blocks = jnp.zeros(x_blocks.shape, jnp.float32) + conv_bias
        for tap_index in range(CONV):
            conv_blocks = (
                conv_blocks
                + conv_taps[tap_index]
                * extended[:, tap_index : tap_index + half_rows]
                * valid_taps[tap_index][:, :, None]
            )
        conv_sum = conv_blocks.reshape(rows_n, -1)
        mixed_x = jax.nn.silu(conv_sum)
        mixed_b = mixed_x.reshape(2, half_rows, -1)
        step_b = step_size.reshape(2, half_rows, -1)
        bc_b = bc_rows.reshape(2, half_rows, -1)
        cumulative, driving, through, local_state = terms_all(
            mixed_b, step_b, bc_b, decay_log, seg_blocks, seg_before
        )
        all_through, all_state = (
            lax.all_gather(through, "seq", axis=0, tiled=True),
            lax.all_gather(local_state, "seq", axis=0, tiled=True),
        )
        through_stream = all_through[inverse]
        state_stream = all_state[inverse]
        acc_through, acc_state = lax.associative_scan(
            combine_state, (through_stream, state_stream), axis=0
        )
        before = my_blocks - 1
        incoming = (
            acc_state[jnp.maximum(before, 0)]
            * (before >= 0).astype(jnp.float32)[:, None, None, None]
        )
        ssm_out = output_all(cumulative, driving, bc_b, incoming, seg_blocks, seg_before).reshape(
            rows_n, -1
        )
        full_y = ssm_out + skip_gain * mixed_x
        gating = jax.nn.silu(gate_in)
        gated_low = (full_y * gating).astype(jnp.bfloat16)
        hidden_one = hidden_in + head_total(matmul(gated_low, mixout_full))
        normed_two = rms_norm(hidden_one, att_gain).astype(jnp.bfloat16)
        qkv_rows = jnp.einsum(
            "rd,dcn->rcn", normed_two, qkv_full, preferred_element_type=jnp.float32
        ).astype(jnp.bfloat16)
        heads_att = qkv_rows.shape[2] // AHEAD_DIM
        queries = qkv_rows[:, 0].reshape(rows_n, heads_att, AHEAD_DIM)
        key_heads = qkv_rows[:, 1].reshape(rows_n, heads_att, AHEAD_DIM)
        value_heads = qkv_rows[:, 2].reshape(rows_n, heads_att, AHEAD_DIM)

        def forward_fold(totals, shards, offset):
            key_rows, value_rows = shards
            key_pos = slot_position(
                order_row, offset + jnp.arange(key_rows.shape[0], dtype=jnp.int32), half_rows
            )
            allowed = (
                (key_pos[None, :] <= position[:, None])
                & (segment_of(key_pos, seq_ends)[None, :] == segment[:, None])
            )[:, None, :]

            def forward_compute(current):
                running_max, running_sum, weighted = current
                scores = (
                    jnp.einsum(
                        "qhd,khd->qhk", queries, key_rows, preferred_element_type=jnp.float32
                    )
                    * scaling
                )
                scores = jnp.where(allowed, scores, -jnp.inf)
                new_max = jnp.maximum(running_max, jnp.max(scores, axis=-1))
                safe_max = jnp.where(new_max == -jnp.inf, 0.0, new_max)
                exp_scores = jnp.exp(scores - safe_max[:, :, None])
                factor = jnp.exp(running_max - safe_max)
                running_sum = running_sum * factor + jnp.sum(exp_scores, axis=-1)
                weighted = weighted * factor[:, :, None] + jnp.einsum(
                    "qhk,khd->qhd",
                    exp_scores.astype(jnp.bfloat16),
                    value_rows,
                    preferred_element_type=jnp.float32,
                )
                return (new_max, running_sum, weighted)

            return lax.cond(jnp.any(allowed), forward_compute, keep_same, totals)

        init_fwd = (
            jnp.full((rows_n, heads_att), -jnp.inf, jnp.float32),
            jnp.zeros((rows_n, heads_att), jnp.float32),
            jnp.zeros((rows_n, heads_att, AHEAD_DIM), jnp.float32),
        )
        all_keys, all_values = (
            lax.all_gather(key_heads, "seq", axis=0, tiled=True),
            lax.all_gather(value_heads, "seq", axis=0, tiled=True),
        )
        running_max, running_sum, weighted = fold_blocks(
            forward_fold, init_fwd, (all_keys, all_values), block_rows
        )
        attended = weighted / running_sum[:, :, None]
        log_total = running_max + jnp.log(running_sum)
        att_low = attended.reshape(rows_n, -1).astype(jnp.bfloat16)
        hidden_two = hidden_one + head_total(matmul(att_low, attout_full))
        normed_three = rms_norm(hidden_two, mlp_gain).astype(jnp.bfloat16)
        up_rows = matmul(normed_three, up_full)
        act_low = gelu_tanh(up_rows).astype(jnp.bfloat16)
        layer_rows = hidden_two + head_total(matmul(act_low, down_full))
        layer_list.append(layer_rows.astype(jnp.bfloat16))
        cot_low = cotangent[batch_index]
        down_wgrad = left_gram(act_low, cot_low)
        act_grad = transposed(cot_low, down_full)
        up_grad = jax.vjp(gelu_tanh, up_rows)[1](act_grad)[0].astype(jnp.bfloat16)
        up_wgrad = left_gram(normed_three, up_grad)
        three_grad = head_total(transposed(up_grad, up_full))
        hidden_part, mlpgain_part = jax.vjp(rms_norm, hidden_two, mlp_gain)[1](three_grad)
        hidden_two_grad = cot_low.astype(jnp.float32) + hidden_part
        branch_low = hidden_two_grad.astype(jnp.bfloat16)
        attout_wgrad = left_gram(att_low, branch_low)
        attended_grad = (
            transposed(branch_low, attout_full)
            .astype(jnp.bfloat16)
            .reshape(rows_n, heads_att, AHEAD_DIM)
        )
        delta_rows = jnp.sum(attended_grad.astype(jnp.float32) * attended, axis=-1)

        def query_fold(totals, shards, offset):
            key_rows, value_rows = shards
            key_pos = slot_position(
                order_row, offset + jnp.arange(key_rows.shape[0], dtype=jnp.int32), half_rows
            )
            key_seg = segment_of(key_pos, seq_ends)
            any_allowed = jnp.any(
                (key_pos[None, :] <= position[:, None]) & (key_seg[None, :] == segment[:, None])
            )

            def query_compute(current):
                probabilities = attention_probs(
                    queries, key_rows, position, key_pos, segment, key_seg, log_total, scaling
                )
                prob_grad = jnp.einsum(
                    "qhd,khd->qhk", attended_grad, value_rows, preferred_element_type=jnp.float32
                )
                score_grad = (probabilities * (prob_grad - delta_rows[:, :, None])).astype(
                    jnp.bfloat16
                )
                return current + jnp.einsum(
                    "qhk,khd->qhd", score_grad, key_rows, preferred_element_type=jnp.float32
                )

            return lax.cond(any_allowed, query_compute, keep_same, totals)

        zero_heads = jnp.zeros((rows_n, heads_att, AHEAD_DIM), jnp.float32)
        query_sum = fold_blocks(query_fold, zero_heads, (all_keys, all_values), block_rows)
        query_rows = lax.all_gather(queries.astype(jnp.float32), "seq", axis=0, tiled=True)
        grad_rows = lax.all_gather(attended_grad.astype(jnp.float32), "seq", axis=0, tiled=True)
        log_rows = lax.all_gather(log_total, "seq", axis=0, tiled=True)
        delta_part = lax.all_gather(delta_rows, "seq", axis=0, tiled=True)
        query_pos = slot_position(
            order_row, jnp.arange(query_rows.shape[0], dtype=jnp.int32), half_rows
        )
        query_seg = segment_of(query_pos, seq_ends)
        key_any_allowed = jnp.any(
            (position[None, :] <= query_pos[:, None]) & (segment[None, :] == query_seg[:, None])
        )

        def key_compute(current):
            query_low = query_rows.astype(jnp.bfloat16)
            grad_low = grad_rows.astype(jnp.bfloat16)
            probabilities = attention_probs(
                query_low, key_heads, query_pos, position, query_seg, segment, log_rows, scaling
            )
            value_grad = jnp.einsum(
                "qhk,qhd->khd",
                probabilities.astype(jnp.bfloat16),
                grad_low,
                preferred_element_type=jnp.float32,
            )
            prob_grad = jnp.einsum(
                "qhd,khd->qhk", grad_low, value_heads, preferred_element_type=jnp.float32
            )
            score_grad = (probabilities * (prob_grad - delta_part[:, :, None])).astype(jnp.bfloat16)
            key_grad = jnp.einsum(
                "qhk,qhd->khd", score_grad, query_low, preferred_element_type=jnp.float32
            )
            return (key_grad, value_grad)

        key_sum, value_sum = lax.cond(
            key_any_allowed, key_compute, keep_same, (zero_heads, zero_heads)
        )
        qkv_grad = jnp.stack(
            [
                (query_sum * scaling).astype(jnp.bfloat16),
                (key_sum * scaling).astype(jnp.bfloat16),
                value_sum.astype(jnp.bfloat16),
            ],
            axis=1,
        ).reshape(rows_n, 3, -1)
        qkv_wgrad = jnp.einsum(
            "rd,rcn->dcn", normed_two, qkv_grad, preferred_element_type=jnp.float32
        )
        two_grad = head_total(
            jnp.einsum("rcn,dcn->rd", qkv_grad, qkv_full, preferred_element_type=jnp.float32)
        )
        hidden_part, attgain_part = jax.vjp(rms_norm, hidden_one, att_gain)[1](two_grad)
        hidden_one_grad = hidden_two_grad + hidden_part
        mix_low = hidden_one_grad.astype(jnp.bfloat16)
        mixout_wgrad = left_gram(gated_low, mix_low)
        gated_grad = transposed(mix_low, mixout_full)
        y_grad = gated_grad * gating
        gate_grad = jax.vjp(jax.nn.silu, gate_in)[1](gated_grad * full_y)[0].astype(jnp.bfloat16)
        skip_part = jnp.sum(y_grad * mixed_x, axis=0)
        heads_mix = step_size.shape[1]
        y_blocks = y_grad.reshape(2, half_rows, -1)
        inflow = (
            jnp.exp(cumulative)
            * (seg_blocks == seg_before[:, None]).astype(jnp.float32)[:, :, None]
        )
        back_local = jnp.einsum(
            "bth,bthp,btn->bhpn",
            inflow,
            y_blocks.reshape(2, half_rows, heads_mix, -1),
            bc_b[:, :, NSTATE:],
            precision=highest,
        )
        all_back = lax.all_gather(back_local, "seq", axis=0, tiled=True)
        back_stream = all_back[inverse]
        rev_through, rev_state = lax.associative_scan(
            combine_state, (through_stream[::-1], back_stream[::-1]), axis=0
        )
        after_index = slots_n - 2 - my_blocks
        outgoing_grad = (
            rev_state[jnp.maximum(after_index, 0)]
            * (after_index >= 0).astype(jnp.float32)[:, None, None, None]
        )

        def scan_call(mixed_arg, step_arg, bc_arg, decay_arg, incoming_arg):
            return whole_all(
                mixed_arg, step_arg, bc_arg, decay_arg, incoming_arg, seg_blocks, seg_before
            )

        scan_pull = jax.vjp(scan_call, mixed_b, step_b, bc_b, decay_log, incoming)[1]
        x_scan_grad, step_grad, bc_grad, decay_part, incoming_grad = scan_pull(
            (y_blocks, outgoing_grad)
        )
        mixed_grad = y_grad * skip_gain + x_scan_grad.reshape(rows_n, -1)
        conv_grad = jax.vjp(jax.nn.silu, conv_sum)[1](mixed_grad)[0]
        conv_grad_b = conv_grad.reshape(2, half_rows, -1)
        convbias_part = jnp.sum(conv_grad, axis=0)
        convtaps_part = jnp.stack(
            [
                jnp.sum(
                    extended[:, tap_index : tap_index + half_rows]
                    * valid_taps[tap_index][:, :, None]
                    * conv_grad_b,
                    axis=(0, 1),
                )
                for tap_index in range(CONV)
            ]
        )
        all_heads = lax.all_gather(conv_grad_b[:, : CONV - 1], "seq", axis=0, tiled=True)
        pick_next = (order_row[None, :] == my_blocks[:, None] + 1).astype(jnp.float32)
        next_rows = jnp.einsum("bs,srd->brd", pick_next, all_heads, precision=highest)
        grad_ext = jnp.concatenate([conv_grad_b, next_rows], axis=1)
        position_ext = (my_blocks[:, None] * half_rows + ext_ids[None, :]).reshape(-1)
        x_blocks_grad = jnp.zeros(conv_grad_b.shape, jnp.float32)
        for tap_index in range(CONV):
            lag_rows = CONV - 1 - tap_index
            masked_grad = (
                grad_ext
                * tap_valid(position_ext, lag_rows, seq_ends).reshape(2, half_rows + CONV - 1)[
                    :, :, None
                ]
            )
            x_blocks_grad = (
                x_blocks_grad
                + conv_taps[tap_index] * masked_grad[:, lag_rows : lag_rows + half_rows]
            )
        x_low = x_blocks_grad.reshape(rows_n, -1).astype(jnp.bfloat16)
        rate_grad = step_grad.reshape(rows_n, -1) * jax.nn.sigmoid(rate_in + rate_bias)
        ratebias_part = jnp.sum(rate_grad, axis=0)
        bc_flat = bc_grad.reshape(rows_n, -1)
        normed_wide = normed_one.astype(jnp.float32)
        value_wgrad = left_gram(normed_one, x_low)
        gate_wgrad = left_gram(normed_one, gate_grad)
        state_wgrad = left_gram_exact(normed_wide, bc_flat)
        rate_wgrad = left_gram_exact(normed_wide, rate_grad)
        one_grad = head_total(
            transposed(x_low, value_full)
            + transposed(gate_grad, gate_full)
            + transposed_exact(bc_flat, state_full.astype(jnp.float32))
            + transposed_exact(rate_grad, rate_full.astype(jnp.float32))
        )
        hidden_part, mixgain_part = jax.vjp(rms_norm, hidden_in, mix_gain)[1](one_grad)
        input_list.append((hidden_one_grad + hidden_part).astype(jnp.bfloat16))
        big_part = (
            value_wgrad,
            gate_wgrad,
            state_wgrad,
            rate_wgrad,
            qkv_wgrad,
            up_wgrad,
            mixout_wgrad,
            attout_wgrad,
            down_wgrad,
        )
        small_part = (
            mixgain_part,
            attgain_part,
            mlpgain_part,
            ratebias_part,
            decay_part,
            convtaps_part,
            convbias_part,
            skip_part,
        )
        big_part = reduce_grads(big_part)
        big_sums = add_parts(big_sums, big_part)
        small_sums = add_parts(small_sums, small_part)
    small_total = lax.psum(
        (
            small_sums[0],
            small_sums[1],
            small_sums[2],
            small_sums[3],
            small_sums[4],
            small_sums[5],
            small_sums[6],
            small_sums[7],
        ),
        "seq",
    )
    return (
        jnp.stack(layer_list),
        jnp.stack(input_list),
        small_total[0],
        big_sums[0],
        big_sums[1],
        big_sums[2],
        big_sums[3],
        small_total[3],
        small_total[4],
        small_total[5],
        small_total[6],
        small_total[7],
        big_sums[6],
        small_total[1],
        big_sums[4],
        big_sums[7],
        small_total[2],
        big_sums[5],
        big_sums[8],
    )


f32 = jnp.float32
bf16 = jnp.bfloat16
HALF = 64
TAIL = 16
EXT = HALF + TAIL
ROWS = 2 * HALF
HCH = 512
LANES = 128
RATE_AT = 32
HPG = 8
TILE_ROWS = 32
SMALL_ROWS = 16
TAIL_COLS = slice(2 * HCH + LANES, 2 * HCH + 2 * LANES)
QKV_ROWS = HALF + HALF // 2
VMEM_LIMIT = 56 * 1024 * 1024


def mm(left_op, right_op):
    return jnp.dot(left_op, right_op, preferred_element_type=f32)


def two_parts(values):
    coarse = values.astype(bf16)
    return coarse, (values - coarse.astype(f32)).astype(bf16)


def mm_onehot(values, onehot):
    coarse, fine = two_parts(values)
    return mm(coarse, onehot) + mm(fine, onehot)


def nt(left_op, right_op):
    return lax.dot_general(
        left_op, right_op, (((1,), (1,)), ((), ())), preferred_element_type=f32
    )


def nt_onehot(values, onehot):
    coarse, fine = two_parts(values)
    return nt(coarse, onehot) + nt(fine, onehot)


def onehot_mm(onehot, values):
    coarse, fine = two_parts(values)
    return mm(onehot, coarse) + mm(onehot, fine)


def tn(left_op, right_op):
    return lax.dot_general(
        left_op, right_op, (((0,), (0,)), ((), ())), preferred_element_type=f32
    )


def iota(shape, axis):
    return lax.broadcasted_iota(jnp.int32, shape, axis)


def sigmoid(values):
    return 1.0 / (1.0 + jnp.exp(-values))


def softplus(values):
    return jnp.maximum(values, 0.0) + jnp.log1p(jnp.exp(-jnp.abs(values)))


def rms_rows(values):
    return lax.rsqrt(jnp.mean(values * values, axis=-1, keepdims=True) + epsilon)


def rms_back(values, gain_row, grad):
    scale = rms_rows(values)
    inner = grad * gain_row
    dot = jnp.mean(inner * values, axis=-1, keepdims=True)
    part = scale * (inner - values * (scale * scale) * dot)
    return part, jnp.sum(grad * (values * scale), axis=0, keepdims=True)


def same_block(rows_idx, cols_idx):
    return (rows_idx // HALF) == (cols_idx // HALF)


def lower_mask():
    rows_idx, cols_idx = iota((ROWS, ROWS), 0), iota((ROWS, ROWS), 1)
    return same_block(rows_idx, cols_idx) & (rows_idx >= cols_idx)


def spread_matrix():
    return (iota((LANES, HCH), 0) - RATE_AT == iota((LANES, HCH), 1) // HALF).astype(f32).astype(bf16)


def per_block(values_0, values_1, shape):
    return jnp.where(iota(shape, 0) < HALF, values_0, values_1)


def step_terms(state_rate, params):
    lane = iota((1, LANES), 1)
    is_rate = (lane >= RATE_AT) & (lane < RATE_AT + HPG)
    shifted = state_rate + params[6:7, 0:LANES]
    step = jnp.where(is_rate, softplus(shifted), 0.0)
    rates = jnp.where(is_rate, jnp.exp(params[7:8, 0:LANES]), 0.0)
    log_decay = -step * rates
    cumulative = onehot_mm(lower_mask().astype(f32).astype(bf16), log_decay)
    return shifted, step, rates, log_decay, cumulative


def tail_decay(cum_wide):
    last = per_block(cum_wide[HALF - 1 : HALF], cum_wide[ROWS - 1 : ROWS], cum_wide.shape)
    return jnp.exp(last - cum_wide)


def decay_matrix(cumulative, cumulative_t, head, mask):
    at = RATE_AT + head
    gap = cumulative[:, at : at + 1] - cumulative_t[at : at + 1, :]
    return jnp.where(mask, jnp.exp(jnp.where(mask, gap, 0.0)), 0.0)


def silu_parts(values):
    gate = sigmoid(values)
    return values * gate, gate * (1.0 + values * (1.0 - gate))


def put_state(msg_ref, batch, group, state):
    for lane_block in range(4):
        for state_half in range(2):
            msg_ref[batch * 16 + group * 8 + lane_block * 2 + state_half, 0:8, :] = state[
                state_half * 8 : (state_half + 1) * 8,
                lane_block * LANES : (lane_block + 1) * LANES,
            ]


def get_state(msg_ref, batch, group):
    base = batch * 16 + group * 8
    return jnp.concatenate(
        [
            jnp.concatenate(
                [
                    msg_ref[base + lane_block * 2 + state_half, 0:8, :]
                    for lane_block in range(4)
                ],
                axis=1,
            )
            for state_half in range(2)
        ],
        axis=0,
    )


def my_rows(core):
    return pl.ds(pl.multiple_of(core * HALF, HALF), HALF)


def in_kernel(
    ids_ref, order_ref, tok_ref, gain_ref, own_ref, other_ref, par_own_ref, par_other_ref,
    ext_ref, normed_ref, x_ref, conv_ref, gate_ref, sr_ref, cum_ref, inner_ref, local_ref,
    msg_ref, deal_ref, gains_ref, x_scr, tail_scr,
):
    chip, core = ids_ref[0], ids_ref[1]
    width = tok_ref.shape[2]
    place = iota((1, width), 1)
    block = place // TILE_ROWS
    source = (chip ^ (block // 4 + 4 * (block % 4))) * TILE_ROWS + place % TILE_ROWS
    deal = (iota((width, width), 0) == source).astype(f32)
    deal_low = deal.astype(bf16)
    deal_ref[...] = deal_low
    gains = mm_onehot(gain_ref[...], deal_low)
    gains_ref[...] = gains
    ext_list = []
    for batch in range(2):
        my_block = order_ref[batch, 2 * chip + core]
        before = jnp.int32(0)
        for slot in range(order_ref.shape[1]):
            before = jnp.where(order_ref[batch, slot] == my_block - 1, slot, before)
        apart = chip ^ (before // 2)
        tail_at = ((apart % 4) * 4 + apart // 4) * TILE_ROWS
        rows = pl.ds(pl.multiple_of(tail_at, TILE_ROWS), TILE_ROWS)

        @pl.when(core == batch)
        def _():
            tail_scr[batch] = own_ref[rows, TAIL_COLS].astype(f32)

        @pl.when(core != batch)
        def _():
            tail_scr[batch] = other_ref[rows, TAIL_COLS].astype(f32)

        tile = jnp.where(before % 2 == 0, tail_scr[batch, 0:12], tail_scr[batch, 12:24])
        tile = jnp.where(my_block == 0, 0.0, tile)
        tails = [
            jnp.concatenate([tile[4 * k + j : 4 * k + j + 1] for j in range(4)], axis=1)
            for k in range(CONV - 1)
        ]
        lead = jnp.zeros((TAIL - (CONV - 1), width), f32)
        ext_list.append(jnp.concatenate([lead] + tails, axis=0).astype(bf16))
        ext_list.append(tok_ref[batch, my_rows(core), :])
    ext_rows = mm(jnp.concatenate(ext_list, axis=0), deal_low).astype(bf16)
    ext_ref[...] = ext_rows
    hidden = ext_rows.astype(f32)
    normed = (hidden * rms_rows(hidden) * gains[0:1]).astype(bf16)
    normed_ref[...] = normed
    real = jnp.concatenate([normed[TAIL:EXT], normed[EXT + TAIL :]], axis=0)
    mask = lower_mask()
    spread = spread_matrix()
    for half, (w_ref, par_ref) in enumerate(
        ((own_ref, par_own_ref), (other_ref, par_other_ref))
    ):
        at = half * HCH
        params = par_ref[...]
        x_low = mm(normed, w_ref[:, 0:HCH]).astype(bf16)
        x_ref[:, at : at + HCH] = x_low
        x_scr[...] = x_low.astype(f32)
        gate_ref[:, at : at + HCH] = mm(real, w_ref[:, HCH : 2 * HCH])
        state_rate = mm(real, w_ref[:, 2 * HCH : 2 * HCH + LANES])
        sr_ref[:, half * LANES : (half + 1) * LANES] = state_rate
        conv_list = []
        for batch in range(2):
            conv = jnp.zeros((HALF, HCH), f32) + params[4:5]
            for tap in range(CONV):
                first = batch * EXT + TAIL - (CONV - 1) + tap
                conv = conv + params[tap : tap + 1] * x_scr[first : first + HALF, :]
            conv_list.append(conv)
        conv = jnp.concatenate(conv_list, axis=0)
        conv_ref[:, at : at + HCH] = conv
        mixed = conv * sigmoid(conv)
        _, step, _, _, cumulative = step_terms(state_rate, params)
        cum_wide = mm_onehot(cumulative, spread)
        cum_ref[:, at : at + HCH] = cum_wide
        driving = mm_onehot(step, spread) * mixed
        weighted = (driving * tail_decay(cum_wide)).astype(bf16)
        driving = driving.astype(bf16)
        b_rows = state_rate[:, 0:NSTATE].astype(bf16)
        c_rows = state_rate[:, NSTATE : 2 * NSTATE].astype(bf16)
        group = half ^ core
        for batch in range(2):
            rows = slice(batch * HALF, (batch + 1) * HALF)
            state = tn(b_rows[rows], weighted[rows])
            local_ref[batch, half] = state
            last_row = (batch + 1) * HALF - 1
            total = jnp.broadcast_to(cum_wide[last_row : last_row + 1], (4, HCH))
            coarse = total.astype(bf16).astype(f32)
            for state_half in range(2):
                block = jnp.concatenate(
                    [state[state_half * 8 : (state_half + 1) * 8], coarse, total - coarse], axis=0
                ).astype(bf16)
                for lane_block in range(4):
                    msg_ref[batch * 16 + group * 8 + lane_block * 2 + state_half] = block[
                        :, lane_block * LANES : (lane_block + 1) * LANES
                    ]
        inner_cb = nt(c_rows, b_rows)
        cumulative_t = cumulative.T
        first_head = iota((ROWS, LANES), 1) < HALF
        for pair in range(4):
            pair_rows = driving[:, pair * LANES : (pair + 1) * LANES]
            parts = [
                mm(
                    (decay_matrix(cumulative, cumulative_t, 2 * pair + k, mask) * inner_cb).astype(
                        bf16
                    ),
                    pair_rows,
                )
                for k in range(2)
            ]
            inner_ref[:, at + pair * LANES : at + (pair + 1) * LANES] = jnp.where(
                first_head, parts[0], parts[1]
            )


def invert_order(ids_ref, order_ref, slots_scr):
    slots_n = order_ref.shape[1]
    batch = (2 * ids_ref[0] + ids_ref[1]) // (slots_n // 2)
    for slot in range(slots_n):
        slots_scr[order_ref[batch, slot]] = slot


def block_decay(block):
    return jnp.exp(block[8:9] + block[12:13])


def forward_scan_kernel(ids_ref, order_ref, in_ref, out_ref, slots_scr):
    invert_order(ids_ref, order_ref, slots_scr)
    state = jnp.zeros((8, LANES), f32)
    for place in range(order_ref.shape[1]):
        slot = slots_scr[place]
        out_ref[slot] = state
        block = in_ref[slot].astype(f32)
        state = state * block_decay(block) + block[0:8]


def backward_scan_kernel(ids_ref, order_ref, decay_ref, in_ref, out_ref, slots_scr):
    invert_order(ids_ref, order_ref, slots_scr)
    state = jnp.zeros((8, LANES), f32)
    for place in reversed(range(order_ref.shape[1])):
        slot = slots_scr[place]
        out_ref[slot] = state
        state = state * block_decay(decay_ref[slot].astype(f32)) + in_ref[slot]


def mix_kernel(
    ids_ref, tok_ref, state_ref, sr_ref, cum_ref, inner_ref, conv_ref, gate_ref,
    par_own_ref, par_other_ref, own_ref, other_ref, gain_ref,
    full_ref, gated_ref, hidden_ref, normed_ref, msg_ref,
):
    core = ids_ref[1]
    hidden = tok_ref[...].astype(f32)
    hidden = jnp.concatenate([hidden[TAIL:EXT], hidden[EXT + TAIL :]], axis=0)
    for half, (w_ref, par_ref) in enumerate(
        ((own_ref, par_own_ref), (other_ref, par_other_ref))
    ):
        cols = slice(half * HCH, (half + 1) * HCH)
        c_rows = sr_ref[:, half * LANES + NSTATE : half * LANES + 2 * NSTATE].astype(bf16)
        carried = jnp.concatenate(
            [
                mm(
                    c_rows[batch * HALF : (batch + 1) * HALF],
                    get_state(state_ref, batch, half ^ core).astype(bf16),
                )
                for batch in range(2)
            ],
            axis=0,
        )
        conv = conv_ref[:, cols]
        mixed = conv * sigmoid(conv)
        full = inner_ref[:, cols] + jnp.exp(cum_ref[:, cols]) * carried + par_ref[5:6] * mixed
        full_ref[:, cols] = full
        gate = gate_ref[:, cols]
        gated = (full * (gate * sigmoid(gate))).astype(bf16)
        gated_ref[:, cols] = gated
        hidden = hidden + nt(gated, w_ref[:, 0:HCH])
    hidden_ref[...] = hidden
    normed = (hidden * rms_rows(hidden) * gain_ref[1:2]).astype(bf16)
    normed_ref[...] = normed
    for half, w_ref in enumerate((own_ref, other_ref)):
        rows_qkv = mm(normed, w_ref[:, HCH : HCH + 768]).astype(bf16)
        for batch in range(2):
            rows = slice(batch * HALF, (batch + 1) * HALF)
            for head in range(4):
                put_qkv(
                    msg_ref,
                    batch * 8 + (half ^ core) * 4 + head,
                    [
                        rows_qkv[rows, at : at + AHEAD_DIM]
                        for at in range(head * AHEAD_DIM, 768, 256)
                    ],
                )


def put_qkv(ref, at, members):
    ref[at, 0:HALF, 0:AHEAD_DIM] = members[0]
    ref[at, 0:HALF, AHEAD_DIM:LANES] = members[1]
    ref[at, HALF:QKV_ROWS, 0:AHEAD_DIM] = members[2][0 : HALF // 2]
    ref[at, HALF:QKV_ROWS, AHEAD_DIM:LANES] = members[2][HALF // 2 :]


def get_qkv(ref, at):
    return [
        ref[at, 0:HALF, 0:AHEAD_DIM],
        ref[at, 0:HALF, AHEAD_DIM:LANES],
        jnp.concatenate(
            [ref[at, HALF:QKV_ROWS, 0:AHEAD_DIM], ref[at, HALF:QKV_ROWS, AHEAD_DIM:LANES]], axis=0
        ),
    ]


def unpack_qkv(own_ref, other_ref, query_scr, key_scr, value_scr):
    for k, ref in enumerate((own_ref, other_ref)):
        for at in range(ref.shape[0]):
            rows = slice(at * HALF, (at + 1) * HALF)
            queries, keys, values = get_qkv(ref, at)
            if k == 0:
                query_scr[rows, :] = queries
            key_scr[k, rows, :] = keys
            value_scr[k, rows, :] = values


def put_rows(ref, at, member):
    ref[at, :, 0:AHEAD_DIM] = member[0 : HALF // 2]
    ref[at, :, AHEAD_DIM:LANES] = member[HALF // 2 :]


def get_rows(ref, at):
    return jnp.concatenate([ref[at, :, 0:AHEAD_DIM], ref[at, :, AHEAD_DIM:LANES]], axis=0)


QTILE = 256


def block_place(ids_ref, order_ref, block, other):
    chip, core = ids_ref[0], ids_ref[1]
    batch = chip // (order_ref.shape[1] // 4)
    return order_ref[batch, 2 * block + (core ^ other)] * HALF


def query_places(ids_ref, order_ref, tile):
    parts = [
        iota((HALF, 1), 0) + block_place(ids_ref, order_ref, tile * (QTILE // HALF) + k, 0)
        for k in range(QTILE // HALF)
    ]
    return jnp.concatenate(parts, axis=0)


def key_places(ids_ref, order_ref, other):
    lane = iota((1, LANES), 1)
    parts = []
    for pair in range(order_ref.shape[1] // 4):
        first = block_place(ids_ref, order_ref, 2 * pair, other)
        second = block_place(ids_ref, order_ref, 2 * pair + 1, other)
        parts.append(lane + jnp.where(lane < HALF, first, second - HALF))
    return jnp.concatenate(parts, axis=1)


def attend_kernel(
    ids_ref, order_ref, own_ref, other_ref, out_ref, log_ref, full_ref, query_scr, key_scr,
    value_scr,
):
    places = [key_places(ids_ref, order_ref, k) for k in range(2)]
    unpack_qkv(own_ref, other_ref, query_scr, key_scr, value_scr)
    scaling = AHEAD_DIM ** (-0.5)
    for tile in range(query_scr.shape[0] // QTILE):
        rows = slice(tile * QTILE, (tile + 1) * QTILE)
        place = query_places(ids_ref, order_ref, tile)
        queries = (query_scr[rows, :].astype(f32) * scaling).astype(bf16)
        scores = [
            jnp.where(
                places[k] <= place, nt(queries, key_scr[k]), -jnp.inf
            )
            for k in range(2)
        ]
        most = jnp.maximum(
            jnp.max(scores[0], axis=-1, keepdims=True), jnp.max(scores[1], axis=-1, keepdims=True)
        )
        exps = [jnp.exp(member - most) for member in scores]
        total = jnp.sum(exps[0], axis=-1, keepdims=True) + jnp.sum(exps[1], axis=-1, keepdims=True)
        mixed = mm(exps[0].astype(bf16), value_scr[0]) + mm(exps[1].astype(bf16), value_scr[1])
        mixed = mixed / total
        full_ref[rows, :] = mixed
        mixed = mixed.astype(bf16)
        for k in range(QTILE // HALF):
            put_rows(out_ref, tile * (QTILE // HALF) + k, mixed[k * HALF : (k + 1) * HALF])
        log_ref[rows, :] = most + jnp.log(total)


def attend_back_kernel(
    ids_ref, order_ref, own_ref, other_ref, grad_ref, log_ref, full_ref, mine_ref, theirs_ref,
    query_scr, key_scr, value_scr, query_sum, key_sum, value_sum,
):
    places = [key_places(ids_ref, order_ref, k) for k in range(2)]
    unpack_qkv(own_ref, other_ref, query_scr, key_scr, value_scr)
    scaling = AHEAD_DIM ** (-0.5)
    key_sum[...] = jnp.zeros(key_sum.shape, f32)
    value_sum[...] = jnp.zeros(value_sum.shape, f32)
    for tile in range(query_scr.shape[0] // QTILE):
        rows = slice(tile * QTILE, (tile + 1) * QTILE)
        place = query_places(ids_ref, order_ref, tile)
        queries = query_scr[rows, :]
        scaled = (queries.astype(f32) * scaling).astype(bf16)
        grad = jnp.concatenate(
            [get_rows(grad_ref, tile * (QTILE // HALF) + k) for k in range(QTILE // HALF)],
            axis=0,
        )
        log_total = log_ref[rows, :]
        probs = []
        prob_grads = []
        for k in range(2):
            scores = nt(scaled, key_scr[k]) - log_total
            probs.append(jnp.exp(jnp.where(places[k] <= place, scores, -jnp.inf)))
            prob_grads.append(nt(grad, value_scr[k]))
        delta = jnp.sum(grad.astype(f32) * full_ref[rows, :], axis=-1, keepdims=True)
        query_grad = jnp.zeros((QTILE, AHEAD_DIM), f32)
        for k in range(2):
            score_grad = (probs[k] * (prob_grads[k] - delta)).astype(bf16)
            value_sum[k] += tn(probs[k].astype(bf16), grad)
            key_sum[k] += tn(score_grad, queries)
            query_grad = query_grad + mm(score_grad, key_scr[k])
        query_sum[rows, :] = query_grad * scaling
    for at in range(mine_ref.shape[0]):
        rows = slice(at * HALF, (at + 1) * HALF)
        put_qkv(
            mine_ref, at, [query_sum[rows, :], key_sum[0, rows, :] * scaling, value_sum[0, rows, :]]
        )
        put_qkv(
            theirs_ref,
            at,
            [
                jnp.zeros((HALF, AHEAD_DIM), bf16),
                (key_sum[1, rows, :] * scaling).astype(bf16),
                value_sum[1, rows, :].astype(bf16),
            ],
        )


GELU_RATE = math.sqrt(2.0 / math.pi)
GELU_CUBE = 0.044715


def mlp_kernel(
    ids_ref, att_ref, hidden_ref, cot_ref, deal_ref, gain_ref, own_ref, other_ref,
    out_ref, hidden_two_ref, cot_both_ref, mine_ref, theirs_ref, hidden_grad_ref, gain_grad_ref,
    msg_ref,
    att_scr, result_scr,
):
    core = ids_ref[1]
    weights = (own_ref, other_ref)
    packs = (mine_ref, theirs_ref)
    up_cols, down_cols, att_cols = slice(0, 1024), slice(1024, 2048), slice(2048, 2304)
    cot_both = mm(
        jnp.concatenate(
            [cot_ref[batch, my_rows(side), :] for side in (core, 1 - core) for batch in range(2)],
            axis=0,
        ),
        deal_ref[...],
    ).astype(bf16)
    cot_both_ref[...] = cot_both
    cot = cot_both[0:ROWS]
    hidden = hidden_ref[...]
    for half in range(2):
        for batch in range(2):
            for head in range(4):
                att_scr[
                    half,
                    batch * HALF : (batch + 1) * HALF,
                    head * AHEAD_DIM : (head + 1) * AHEAD_DIM,
                ] = get_rows(att_ref, batch * 8 + (half ^ core) * 4 + head)
        packs[half][:, att_cols] = att_scr[half]
        hidden = hidden + nt(att_scr[half], weights[half][:, att_cols])
    gain = gain_ref[2:3]
    normed = (hidden * rms_rows(hidden) * gain).astype(bf16)
    normed_grad = jnp.zeros(hidden.shape, f32)
    for half in range(2):
        up_rows = mm(normed, weights[half][:, up_cols])
        squares = up_rows * up_rows
        bent = jnp.tanh(GELU_RATE * (up_rows + GELU_CUBE * squares * up_rows))
        act = (0.5 * up_rows * (1.0 + bent)).astype(bf16)
        slope = 0.5 * (1.0 + bent) + 0.5 * up_rows * (1.0 - bent * bent) * (
            GELU_RATE * (1.0 + 3.0 * GELU_CUBE * squares)
        )
        result_scr[half] = nt(act, weights[half][:, down_cols])
        packs[half][:, down_cols] = act
        up_grad = (mm(cot, weights[half][:, down_cols]) * slope).astype(bf16)
        packs[half][:, up_cols] = up_grad
        normed_grad = normed_grad + nt(up_grad, weights[half][:, up_cols])
        packs[half][:, 2304 : 2304 + 512] = normed
    hidden_two_ref[...] = hidden
    out_ref[...] = result_scr[0] + result_scr[1]
    part, gain_grad = rms_back(hidden, gain, normed_grad)
    gain_grad_ref[...] = gain_grad
    hidden_grad = cot.astype(f32) + part
    hidden_grad_ref[...] = hidden_grad
    branch = hidden_grad.astype(bf16)
    for half in range(2):
        packs[half][:, 2816 : 2816 + 512] = branch
        att_grad = mm(branch, weights[half][:, att_cols]).astype(bf16)
        for batch in range(2):
            for head in range(4):
                put_rows(
                    msg_ref,
                    batch * 8 + (half ^ core) * 4 + head,
                    att_grad[
                        batch * HALF : (batch + 1) * HALF,
                        head * AHEAD_DIM : (head + 1) * AHEAD_DIM,
                    ],
                )


def both_rows(mine_ref, theirs_ref, cols):
    return jnp.concatenate([mine_ref[:, cols], theirs_ref[:, cols]], axis=0)


def put_pieces(piece_refs, cols, values):
    rows_n = piece_refs[0].shape[0]
    for k, piece_ref in enumerate(piece_refs):
        piece_ref[:, cols] = values[k * rows_n : (k + 1) * rows_n].astype(bf16)


def third_grad_kernel(mine_ref, theirs_ref, cot_ref, *piece_refs):
    up_cols, down_cols, att_cols = slice(0, 1024), slice(1024, 2048), slice(2048, 2304)

    def both(cols):
        return both_rows(mine_ref, theirs_ref, cols)

    put_pieces(piece_refs, up_cols, tn(both(slice(2304, 2816)), both(up_cols)))
    put_pieces(piece_refs, down_cols, tn(cot_ref[...], both(down_cols)))
    put_pieces(piece_refs, att_cols, tn(both(slice(2816, 3328)), both(att_cols)))


def second_grad_kernel(mine_ref, theirs_ref, *piece_refs):
    def both(cols):
        return both_rows(mine_ref, theirs_ref, cols)

    for cols, base in ((slice(0, 512), 2304), (slice(512, 1280), 1792), (slice(1280, 1792), 2816)):
        put_pieces(piece_refs, cols, tn(both(slice(base, base + 512)), both(cols)))


def first_grad_kernel(ids_ref, mine_ref, theirs_ref, msg_ref, *piece_refs):
    cols = slice(0, HCH + LANES)
    rows = slice(0, 2 * EXT)
    packs = (mine_ref, theirs_ref)
    put_pieces(
        piece_refs,
        cols,
        tn(
            jnp.concatenate([ref[rows, HCH + LANES : 2 * HCH + LANES] for ref in packs], axis=0),
            jnp.concatenate([ref[rows, cols] for ref in packs], axis=0),
        ),
    )
    rows = slice(2 * EXT, 2 * EXT + SMALL_ROWS)
    small = mine_ref[rows, 0:HCH].astype(f32) + theirs_ref[rows, 0:HCH].astype(f32)
    tails = [ref[rows, HCH : 2 * HCH].astype(f32) for ref in packs]
    ordered = [jnp.where(ids_ref[1] == k, tails[0], tails[1]) for k in range(2)]
    tails = jnp.concatenate(
        [ordered[0][0:6], ordered[1][0:6], jnp.zeros((SMALL_ROWS - 12, HCH), f32)], axis=0
    )
    block = jnp.concatenate([small, tails], axis=1).astype(bf16)
    for k in range(msg_ref.shape[0]):
        msg_ref[k] = block


def sum_kernel(*refs):
    total = refs[0][...].astype(f32)
    for ref in refs[1:4]:
        total = total + ref[...].astype(f32)
    put_pieces(refs[4:], slice(0, total.shape[1]), total)


def sum_both_kernel(*refs):
    at = 0
    for group in (refs[0:4], refs[4:8]):
        total = group[0][...].astype(f32)
        for ref in group[1:]:
            total = total + ref[...].astype(f32)
        put_pieces(refs[8:], slice(at, at + total.shape[1]), total)
        at += total.shape[1]


def early_out_kernel(*refs):
    total = refs[0][...].astype(f32)
    for ref in refs[1:4]:
        total = total + ref[...].astype(f32)
    value_ref, state_ref, rate_ref, mix_ref, qkv_ref, gate_ref = refs[4:]
    value_ref[...] = total[:, 0:HCH]
    state_ref[...] = total[:, HCH : HCH + 32]
    rate_ref[...] = total[:, HCH : HCH + LANES].T[RATE_AT : RATE_AT + HPG]
    base = HCH + LANES
    mix_ref[...] = total[:, base : base + HCH]
    for kind in range(3):
        qkv_ref[kind] = total[:, base + HCH + kind * 256 : base + HCH + (kind + 1) * 256]
    gate_ref[...] = total[:, base + HCH + 768 :]


def mix_back_kernel(
    ids_ref, qkv_ref, first_ref, normed_ref, hidden_ref, hidden_grad_ref, gain_ref, own_ref,
    other_ref, gated_ref, gate_ref, full_ref, conv_ref, cum_ref, sr_ref,
    mine_ref, theirs_ref, y_grad_ref, gate_grad_ref, one_grad_ref, gain_grad_ref, skip_grad_ref,
    msg_ref, qkv_scr,
):
    core = ids_ref[1]
    weights = (own_ref, other_ref)
    packs = (mine_ref, theirs_ref)
    mix_cols, qkv_cols, gate_cols = slice(0, 512), slice(512, 1280), slice(1280, 1792)
    first = jnp.concatenate([first_ref[TAIL:EXT], first_ref[EXT + TAIL :]], axis=0)
    normed_grad = jnp.zeros(hidden_ref.shape, f32)
    for half in range(2):
        for batch in range(2):
            for head in range(4):
                members = get_qkv(qkv_ref, batch * 8 + (half ^ core) * 4 + head)
                for kind, member in enumerate(members):
                    at = kind * 256 + head * AHEAD_DIM
                    qkv_scr[batch * HALF : (batch + 1) * HALF, at : at + AHEAD_DIM] = member
        rows_grad = qkv_scr[...]
        packs[half][:, qkv_cols] = rows_grad
        normed_grad = normed_grad + nt(rows_grad, weights[half][:, qkv_cols])
    part, gain_grad = rms_back(hidden_ref[...], gain_ref[1:2], normed_grad)
    gain_grad_ref[...] = gain_grad
    one_grad = hidden_grad_ref[...] + part
    one_grad_ref[...] = one_grad
    branch = one_grad.astype(bf16)
    for half in range(2):
        cols = slice(half * HCH, (half + 1) * HCH)
        packs[half][:, mix_cols] = gated_ref[:, cols]
        packs[half][:, 1792:2304] = normed_ref[...]
        packs[half][:, 2304:2816] = branch
        packs[half][:, 2816:3328] = first
        gated_grad = mm(branch, weights[half][:, mix_cols])
        silu, slope = silu_parts(gate_ref[:, cols])
        y_grad = gated_grad * silu
        y_grad_ref[:, cols] = y_grad
        gate_grad = (gated_grad * full_ref[:, cols] * slope).astype(bf16)
        gate_grad_ref[:, cols] = gate_grad
        packs[half][:, gate_cols] = gate_grad
        conv = conv_ref[:, cols]
        skip_grad_ref[:, cols] = jnp.sum(y_grad * (conv * sigmoid(conv)), axis=0, keepdims=True)
        carried = (jnp.exp(cum_ref[:, cols]) * y_grad).astype(bf16)
        c_rows = sr_ref[:, half * LANES + NSTATE : half * LANES + 2 * NSTATE].astype(bf16)
        for batch in range(2):
            rows = slice(batch * HALF, (batch + 1) * HALF)
            put_state(msg_ref, batch, half ^ core, tn(c_rows[rows], carried[rows]))


def in_back_kernel(
    ids_ref, later_ref, state_ref, local_ref, sr_ref, cum_ref, conv_ref, x_ref, y_grad_ref,
    gate_grad_ref, normed_ref, tok_ref, gain_ref, one_grad_ref, own_ref, other_ref,
    par_own_ref, par_other_ref, deal_ref, skip_grad_ref, attgain_ref, mlpgain_ref,
    mine_ref, theirs_ref, hidden_grad_ref,
    x_scr, grad_scr, sr_scr, gate_scr,
):
    core = ids_ref[1]
    mask = lower_mask()
    spread = spread_matrix()
    normed = normed_ref[...]
    ext_grad = jnp.zeros((2 * EXT, normed.shape[1]), f32)
    lower_t = (
        same_block(iota((ROWS, ROWS), 0), iota((ROWS, ROWS), 1))
        & (iota((ROWS, ROWS), 0) <= iota((ROWS, ROWS), 1))
    ).astype(f32).astype(bf16)
    lane = iota((1, LANES), 1)
    small_list = []
    for half, (w_ref, par_ref, pack_ref) in enumerate(
        ((own_ref, par_own_ref, mine_ref), (other_ref, par_other_ref, theirs_ref))
    ):
        cols = slice(half * HCH, (half + 1) * HCH)
        group = half ^ core
        params = par_ref[...]
        state_rate = sr_ref[:, half * LANES : (half + 1) * LANES]
        shifted, step, rates, log_decay, cumulative = step_terms(state_rate, params)
        cumulative_t = cumulative.T
        cum_wide = cum_ref[:, cols]
        step_wide = mm_onehot(step, spread)
        conv = conv_ref[:, cols]
        mixed, conv_slope = silu_parts(conv)
        driving = step_wide * mixed
        tail = tail_decay(cum_wide)
        inflow = jnp.exp(cum_wide)
        y_grad = y_grad_ref[:, cols]
        y_low = y_grad.astype(bf16)
        driving_low = driving.astype(bf16)
        b_rows = state_rate[:, 0:NSTATE].astype(bf16)
        c_rows = state_rate[:, NSTATE : 2 * NSTATE].astype(bf16)
        inner_cb = nt(c_rows, b_rows)
        weighted = (driving * tail).astype(bf16)
        carried_grad = (inflow * y_grad).astype(bf16)
        through_list = []
        tail_list = []
        flow_list = []
        b_list = []
        c_list = []
        for batch in range(2):
            rows = slice(batch * HALF, (batch + 1) * HALF)
            incoming = get_state(state_ref, batch, group)
            later = get_state(later_ref, batch, group)
            total = cum_wide[(batch + 1) * HALF - 1 : (batch + 1) * HALF, :]
            outgoing = jnp.exp(total) * incoming + local_ref[batch, half]
            through_list.append(jnp.sum(later * outgoing, axis=0, keepdims=True))
            incoming = incoming.astype(bf16)
            later = later.astype(bf16)
            tail_list.append(mm(b_rows[rows], later))
            flow_list.append(mm(c_rows[rows], incoming))
            b_list.append(nt(weighted[rows], later))
            c_list.append(nt(carried_grad[rows], incoming))
        tail_part = tail * jnp.concatenate(tail_list, axis=0)
        flow_part = inflow * jnp.concatenate(flow_list, axis=0)
        first_head = iota((ROWS, LANES), 1) < HALF
        inner_grad = jnp.zeros((ROWS, ROWS), f32)
        row_sums = jnp.zeros((ROWS, LANES), f32)
        col_list = []
        drive_list = []
        for pair in range(4):
            lanes = slice(pair * LANES, (pair + 1) * LANES)
            y_pair = y_low[:, lanes]
            u_pair = driving_low[:, lanes]
            parts = []
            for k in range(2):
                head = 2 * pair + k
                mine = first_head if k == 0 else ~first_head
                decay = decay_matrix(cumulative, cumulative_t, head, mask)
                product = nt(jnp.where(mine, y_pair, jnp.zeros_like(y_pair)), u_pair)
                decayed = decay * product
                inner_grad = inner_grad + decayed
                both = decayed * inner_cb
                row_sums = row_sums + jnp.where(
                    lane == RATE_AT + head, jnp.sum(both, axis=1, keepdims=True), 0.0
                )
                col_list.append(jnp.sum(both, axis=0, keepdims=True))
                parts.append(tn((decay * inner_cb).astype(bf16), y_pair))
            drive_list.append(jnp.where(first_head, parts[0], parts[1]))
        drive_grad = jnp.concatenate(drive_list, axis=1) + tail_part
        col_rows = jnp.concatenate(
            [jnp.zeros((RATE_AT, ROWS), f32)]
            + col_list
            + [jnp.zeros((LANES - RATE_AT - HPG, ROWS), f32)],
            axis=0,
        )
        cum_grad = (
            row_sums
            - col_rows.T
            + nt_onehot(y_grad * flow_part - driving * tail_part, spread)
        )
        through_rows = nt_onehot(
            jnp.concatenate(through_list + [jnp.zeros((6, HCH), f32)], axis=0), spread
        )
        decay_grad = onehot_mm(lower_t, cum_grad) + per_block(
            through_rows[0:1], through_rows[1:2], (ROWS, LANES)
        )
        step_grad = nt_onehot(mixed * drive_grad, spread) - decay_grad * rates
        rate_grad = step_grad * sigmoid(shifted)
        inner_low = inner_grad.astype(bf16)
        b_grad = tn(inner_low, c_rows) + jnp.concatenate(b_list, axis=0)
        c_grad = mm(inner_low, b_rows) + jnp.concatenate(c_list, axis=0)
        is_rate = (lane >= RATE_AT) & (lane < RATE_AT + HPG)
        rate_grad = jnp.where(is_rate, rate_grad, 0.0)
        sr_grad = jnp.concatenate(
            [b_grad, c_grad, rate_grad[:, RATE_AT:LANES]], axis=1
        ).astype(bf16)
        mixed_grad = step_wide * drive_grad + params[5:6] * y_grad
        conv_grad = mixed_grad * conv_slope
        x_scr[...] = x_ref[:, cols].astype(f32)
        grad_scr[...] = jnp.zeros(grad_scr.shape, f32)
        sr_scr[...] = jnp.zeros(sr_scr.shape, bf16)
        gate_scr[...] = jnp.zeros(gate_scr.shape, bf16)
        gate_grad = gate_grad_ref[:, cols]
        for batch in range(2):
            rows = slice(batch * HALF, (batch + 1) * HALF)
            ext_rows = slice(batch * EXT + TAIL, (batch + 1) * EXT)
            grad_scr[batch, TAIL:EXT, :] = conv_grad[rows]
            sr_scr[ext_rows, :] = sr_grad[rows]
            gate_scr[ext_rows, :] = gate_grad[rows]
        x_list = []
        tap_list = [jnp.zeros((1, HCH), f32) for _ in range(CONV)]
        for batch in range(2):
            x_grad = jnp.zeros((EXT, HCH), f32)
            for tap in range(CONV):
                lag = CONV - 1 - tap
                x_grad = x_grad + params[tap : tap + 1] * grad_scr[batch, lag : lag + EXT, :]
                first = batch * EXT + TAIL - lag
                tap_list[tap] = tap_list[tap] + jnp.sum(
                    x_scr[first : first + HALF, :] * grad_scr[batch, TAIL:EXT, :],
                    axis=0,
                    keepdims=True,
                )
            x_list.append(x_grad)
        x_low = jnp.concatenate(x_list, axis=0).astype(bf16)
        small_list.append(
            jnp.concatenate(
                tap_list
                + [
                    jnp.sum(conv_grad, axis=0, keepdims=True),
                    skip_grad_ref[:, cols],
                    jnp.concatenate(
                        [
                            jnp.sum(rate_grad, axis=0, keepdims=True),
                            jnp.sum(decay_grad * log_decay, axis=0, keepdims=True),
                            jnp.zeros((1, HCH - 2 * LANES), f32),
                        ],
                        axis=1,
                    ),
                ],
                axis=0,
            )
        )
        pack_ref[0 : 2 * EXT, 0:HCH] = x_low
        pack_ref[0 : 2 * EXT, HCH : HCH + LANES] = sr_scr[...]
        pack_ref[0 : 2 * EXT, HCH + LANES : 2 * HCH + LANES] = normed
        ext_grad = (
            ext_grad
            + nt(x_low, w_ref[:, 0:HCH])
            + nt(gate_scr[...], w_ref[:, HCH : 2 * HCH])
            + nt(sr_scr[...], w_ref[:, 2 * HCH : 2 * HCH + LANES])
        )
    hidden = tok_ref[...].astype(f32)
    part, gain_grad = rms_back(hidden, gain_ref[0:1], ext_grad)
    deal = deal_ref[...]
    gain_grads = nt_onehot(
        jnp.concatenate([gain_grad, attgain_ref[...], mlpgain_ref[...]], axis=0), deal
    )
    tails = nt(
        jnp.concatenate([part[TAIL - 3 : TAIL], part[EXT + TAIL - 3 : EXT + TAIL]], axis=0).astype(
            bf16
        ),
        deal,
    )
    tails = jnp.concatenate([tails, jnp.zeros((SMALL_ROWS - 6, HCH), f32)], axis=0)
    for small, pack_ref in zip(small_list, (mine_ref, theirs_ref)):
        rows = slice(2 * EXT, 2 * EXT + SMALL_ROWS)
        pack_ref[rows, 0:HCH] = jnp.concatenate(
            [small, gain_grads, jnp.zeros((SMALL_ROWS - 10, HCH), f32)], axis=0
        ).astype(bf16)
        pack_ref[rows, HCH : 2 * HCH] = tails.astype(bf16)
        pack_ref[rows, 2 * HCH :] = jnp.zeros((SMALL_ROWS, LANES), bf16)
    rows_grad = jnp.concatenate([part[TAIL:EXT], part[EXT + TAIL :]], axis=0) + one_grad_ref[...]
    hidden_grad_ref[...] = nt(rows_grad.astype(bf16), deal)


SMEM_SPEC = pl.BlockSpec(memory_space=pltpu.SMEM)
VMEM_SPEC = pl.BlockSpec(memory_space=pltpu.VMEM)
ANY_SPEC = pl.BlockSpec(memory_space=pl.ANY)


def run_kernel(kernel, out_shapes, scalars_n, args, scratch=(), after=(), pieces=None, at=0):
    args_n = len(args)
    pieces = [] if pieces is None else list(pieces[0]) + list(pieces[1])
    scratch = list(scratch)
    if pieces:
        rows_n, cols = pieces[0].shape
        scratch += [pltpu.VMEM((4 * rows_n, cols), bf16)] * 2
        scratch.append(pltpu.SemaphoreType.DMA((8,)))

    def body(*refs):
        ins, rest = list(refs[:args_n]), list(refs[args_n + len(pieces) + len(after) :])
        if pieces:
            *rest, own_scr, other_scr, sems = rest
            copies = [
                pltpu.make_async_copy(
                    refs[args_n + k],
                    (own_scr, other_scr)[k // 4].at[pl.ds((k % 4) * rows_n, rows_n), :],
                    sems.at[k],
                )
                for k in range(8)
            ]
            for copy in copies:
                copy.start()
            for copy in copies:
                copy.wait()
            ins[at:at] = [own_scr, other_scr]
        kernel(*ins, *rest)

    return pl.pallas_call(
        body,
        out_shape=[jax.ShapeDtypeStruct(shape, kind) for shape, kind in out_shapes],
        in_specs=[SMEM_SPEC] * scalars_n
        + [VMEM_SPEC] * (args_n - scalars_n)
        + [ANY_SPEC] * (len(pieces) + len(after)),
        out_specs=[VMEM_SPEC] * len(out_shapes),
        scratch_shapes=scratch,
        compiler_params=pltpu.CompilerParams(vmem_limit_bytes=VMEM_LIMIT),
        name=kernel.__name__,
        cost_estimate=pl.CostEstimate(flops=0, transcendentals=0, bytes_accessed=0),
    )(*args, *pieces, *after)


def hold(values, *after):
    def body(*refs):
        pass

    return pl.pallas_call(
        body,
        out_shape=jax.ShapeDtypeStruct(values.shape, values.dtype),
        in_specs=[ANY_SPEC] * (1 + len(after)),
        out_specs=ANY_SPEC,
        input_output_aliases={0: 0},
    )(values, *after)


def flip(bits, ranks):
    return [(index, index ^ bits) for index in range(ranks)]


def swap_cores(values):
    return lax.ppermute(values, "head", [(0, 1), (1, 0)])


def permute_three(pieces, step, ranks):
    return [
        lax.ppermute(piece, "seq", flip(step * (k + 1), ranks)) for k, piece in enumerate(pieces)
    ]


def sum_pieces(mine, moved, after=()):
    rows_n, cols = mine.shape
    return run_kernel(
        sum_kernel, [((rows_n // 4, cols), bf16)] * 4, 0, [mine] + moved, (), after
    )


def exchange(values, axes):
    return lax.all_to_all(values, axes, 0, 0, tiled=True)


def dealt_device(
    tokens, cotangent, lengths, order, mix_gain, in_value, in_gate, in_state, in_rate,
    rate_bias, decay_log, conv_taps, conv_bias, skip_gain, mix_out, att_gain, qkv_proj,
    att_out, mlp_gain, mlp_up, mlp_down,
):
    ranks = lax.axis_size("seq")
    both = ("seq", "head")
    chip = lax.axis_index("seq")
    core = lax.axis_index("head")
    ids = jnp.stack([chip, core]).astype(jnp.int32)
    my_slot = 2 * chip + core
    width = tokens.shape[2]
    slots_n = 2 * ranks
    shard_rows = width // ranks
    slots_scratch = (pltpu.SMEM((slots_n,), jnp.int32),)

    tail_rows = tokens.reshape(2, 2, HALF, width)[:, :, HALF - (CONV - 1) :]
    tail_rows = jnp.where(core == 0, tail_rows[0], tail_rows[1]).reshape(-1, LANES)
    tail_rows = jnp.pad(tail_rows, ((0, shard_rows - tail_rows.shape[0]), (0, 0)))
    first_shard = jnp.concatenate(
        [
            in_value, in_gate, in_state, in_rate, jnp.zeros((shard_rows, LANES - 40), bf16),
            tail_rows,
        ],
        axis=1,
    )
    first_cols = first_shard.shape[1]
    second_cols, third_cols = HCH + 768, 2304
    early_shard = jnp.concatenate(
        [first_shard, mix_out.T, qkv_proj.reshape(shard_rows, -1)], axis=1
    )
    third_shard = jnp.concatenate([mlp_up, mlp_down.T, att_out.T], axis=1)
    early_pieces = [early_shard] + permute_three([early_shard] * 3, 4, ranks)
    first_stack = jnp.concatenate([piece[:, :first_cols] for piece in early_pieces], axis=0)
    third_shard = hold(third_shard, first_stack)
    third_z = [third_shard] + permute_three([third_shard] * 3, 4, ranks)
    third_stack = jnp.concatenate(third_z, axis=0)
    first_own = [first_stack] + permute_three([first_stack] * 3, 1, ranks)
    first_own[3] = hold(first_own[3], *third_z[1:])
    first_pieces = (first_own, [swap_cores(piece) for piece in first_own])
    second_stack = jnp.concatenate([piece[:, first_cols:] for piece in early_pieces], axis=0)
    second_own = [second_stack] + permute_three([second_stack] * 3, 1, ranks)
    second_pieces = (second_own, [swap_cores(piece) for piece in second_own])

    par_own = jnp.concatenate(
        [
            conv_taps,
            conv_bias[None],
            skip_gain[None],
            jnp.pad(rate_bias, (RATE_AT, HCH - RATE_AT - HPG))[None],
            jnp.pad(decay_log, (RATE_AT, HCH - RATE_AT - HPG))[None],
        ],
        axis=0,
    )
    par_other = swap_cores(par_own)
    gains = jnp.stack([mix_gain, att_gain, mlp_gain])

    channels = 2 * HCH
    (
        ext_rows, normed_one, x_in, conv_sum, gate_in, state_rate, cum_wide, inner_y,
        local_state, msg, deal_low, gains,
    ) = run_kernel(
        in_kernel,
        [
            ((2 * EXT, width), bf16),
            ((2 * EXT, width), bf16),
            ((2 * EXT, channels), bf16),
            ((ROWS, channels), f32),
            ((ROWS, channels), f32),
            ((ROWS, 2 * LANES), f32),
            ((ROWS, channels), f32),
            ((ROWS, channels), f32),
            ((2, 2, NSTATE, HCH), f32),
            ((slots_n, 16, LANES), bf16),
            ((width, width), bf16),
            ((3, width), f32),
        ],
        2,
        (ids, order, tokens, gains, par_own, par_other),
        (pltpu.VMEM((2 * EXT, HCH), f32), pltpu.VMEM((2, TILE_ROWS, LANES), f32)),
        pieces=first_pieces,
        at=4,
    )

    states = exchange(hold(msg, *second_own[1:3]), both)
    (incoming,) = run_kernel(
        forward_scan_kernel,
        [((slots_n, 8, LANES), f32)],
        2,
        (ids, order, states),
        slots_scratch,
        after=second_own[3:],
    )
    incoming = exchange(incoming, both)

    full_y, gated, hidden_one, normed_two, msg = run_kernel(
        mix_kernel,
        [
            ((ROWS, channels), f32),
            ((ROWS, channels), bf16),
            ((ROWS, width), f32),
            ((ROWS, width), bf16),
            ((ranks, QKV_ROWS, LANES), bf16),
        ],
        1,
        (
            ids, ext_rows, incoming, state_rate, cum_wide, inner_y, conv_sum, gate_in,
            par_own, par_other, gains,
        ),
        after=[third_stack],
        pieces=second_pieces,
        at=10,
    )
    third_own = [third_stack] + permute_three([third_stack] * 3, 1, ranks)
    att_rows = ranks * HALF
    qkv_scratch = (
        pltpu.VMEM((att_rows, AHEAD_DIM), bf16),
        pltpu.VMEM((2, att_rows, AHEAD_DIM), bf16),
        pltpu.VMEM((2, att_rows, AHEAD_DIM), bf16),
    )
    qkv_own = exchange(hold(msg, *third_own[1:3]), "seq")
    qkv_other = swap_cores(qkv_own)
    attended, log_total, att_full = run_kernel(
        attend_kernel,
        [((ranks, HALF // 2, LANES), bf16), ((att_rows, 1), f32), ((att_rows, AHEAD_DIM), f32)],
        2,
        (ids, order, qkv_own, qkv_other),
        qkv_scratch,
    )
    third_own[3] = hold(third_own[3], log_total)
    third_pieces = (third_own, [swap_cores(piece) for piece in third_own])
    attended = exchange(attended, "seq")

    pack_cols = 3328
    (
        down_rows, hidden_two, cot_both, mine, theirs, two_grad, mlpgain_part, msg,
    ) = run_kernel(
        mlp_kernel,
        [
            ((ROWS, width), f32),
            ((ROWS, width), f32),
            ((2 * ROWS, width), bf16),
            ((ROWS, pack_cols), bf16),
            ((ROWS, pack_cols), bf16),
            ((ROWS, width), f32),
            ((1, width), f32),
            ((ranks, HALF // 2, LANES), bf16),
        ],
        1,
        (ids, attended, hidden_one, cotangent, deal_low, gains),
        (pltpu.VMEM((2, ROWS, 256), bf16), pltpu.VMEM((2, ROWS, width), f32)),
        pieces=third_pieces,
        at=6,
    )
    att_grad = exchange(msg, "seq")
    third_grads = run_kernel(
        third_grad_kernel,
        [((width // 4, third_cols), bf16)] * 4,
        0,
        (mine, swap_cores(theirs), cot_both),
    )
    mine, theirs = run_kernel(
        attend_back_kernel,
        [((ranks, QKV_ROWS, LANES), f32), ((ranks, QKV_ROWS, LANES), bf16)],
        2,
        (ids, order, qkv_own, qkv_other, att_grad, log_total, att_full),
        qkv_scratch
        + (
            pltpu.VMEM((att_rows, AHEAD_DIM), f32),
            pltpu.VMEM((2, att_rows, AHEAD_DIM), f32),
            pltpu.VMEM((2, att_rows, AHEAD_DIM), f32),
        ),
        after=third_grads[:1],
    )
    qkv_grad = (mine + swap_cores(theirs).astype(f32)).astype(bf16)
    qkv_grad = exchange(qkv_grad, "seq")
    third_moved = permute_three(third_grads[1:], 1, ranks)

    mine, theirs, y_grad, gate_grad, one_grad, attgain_part, skip_part, msg = run_kernel(
        mix_back_kernel,
        [
            ((ROWS, pack_cols), bf16),
            ((ROWS, pack_cols), bf16),
            ((ROWS, channels), f32),
            ((ROWS, channels), bf16),
            ((ROWS, width), f32),
            ((1, width), f32),
            ((1, channels), f32),
            ((slots_n, 8, LANES), f32),
        ],
        1,
        (
            ids, qkv_grad, normed_one, normed_two, hidden_one, two_grad, gains, gated, gate_in,
            full_y, conv_sum, cum_wide, state_rate,
        ),
        (pltpu.VMEM((ROWS, 768), bf16),),
        pieces=second_pieces,
        at=7,
        after=third_moved[:2],
    )
    back_states = exchange(msg, both)
    second_grads = run_kernel(
        second_grad_kernel,
        [((width // 4, second_cols + HCH), bf16)] * 4,
        0,
        (mine, swap_cores(theirs)),
    )
    (later,) = run_kernel(
        backward_scan_kernel,
        [((slots_n, 8, LANES), f32)],
        2,
        (ids, order, states, back_states),
        slots_scratch,
        after=[second_grads[0], third_moved[2]],
    )
    third_parts = sum_pieces(third_grads[0], third_moved, (later,))
    third_moved = permute_three(third_parts[1:], 4, ranks)
    second_moved = permute_three(second_grads[1:], 1, ranks)
    later = exchange(later, both)

    grad_cols = HCH + LANES
    pack_shape = (2 * EXT + SMALL_ROWS, grad_cols + width)
    mine, theirs, tokens_grad = run_kernel(
        in_back_kernel,
        [(pack_shape, bf16), (pack_shape, bf16), ((ROWS, width), f32)],
        1,
        (
            ids, later, incoming, local_state, state_rate, cum_wide, conv_sum, x_in, y_grad,
            gate_grad, normed_one, ext_rows, gains, one_grad, par_own, par_other, deal_low,
            skip_part, attgain_part, mlpgain_part,
        ),
        (
            pltpu.VMEM((2 * EXT, HCH), f32),
            pltpu.VMEM((2, EXT + TAIL, HCH), f32),
            pltpu.VMEM((2 * EXT, LANES), bf16),
            pltpu.VMEM((2 * EXT, HCH), bf16),
        ),
        after=[third_parts[0]],
        pieces=first_pieces,
        at=14,
    )
    last_msg, *first_grads = run_kernel(
        first_grad_kernel,
        [((ranks, SMALL_ROWS, 2 * HCH), bf16)] + [((width // 4, grad_cols), bf16)] * 4,
        1,
        (ids, mine, swap_cores(theirs)),
        after=second_moved,
    )
    first_moved = permute_three(first_grads[1:], 1, ranks)
    last = exchange(hold(last_msg, *first_moved), "seq")
    early_parts = run_kernel(
        sum_both_kernel,
        [((width // 16, grad_cols + second_cols + HCH), bf16)] * 4,
        0,
        [first_grads[0]] + first_moved + [second_grads[0]] + second_moved,
    )
    third_total = third_parts[0].astype(f32)
    for piece in third_moved:
        third_total = third_total + piece.astype(f32)
    early_outs = run_kernel(
        early_out_kernel,
        [
            (shape, f32)
            for shape in (
                in_value.shape,
                in_state.shape,
                in_rate.shape[::-1],
                mix_out.shape[::-1],
                (qkv_proj.shape[1], qkv_proj.shape[0], qkv_proj.shape[2]),
                in_gate.shape,
            )
        ],
        0,
        [early_parts[0]] + permute_three(early_parts[1:], 4, ranks),
    )

    my_blocks = jnp.sum(
        jnp.where(jnp.arange(slots_n)[None, :] == my_slot, order, 0), axis=1
    )
    last = last.astype(f32)
    small_total = jnp.sum(last[:, 0:10, 0:HCH], axis=0)
    next_tails = last[:, 0:12, HCH:].reshape(ranks, 2, 2, CONV - 1, width).transpose(2, 0, 1, 3, 4)
    next_tails = next_tails.reshape(2, slots_n, CONV - 1, width)
    pick_next = (order == my_blocks[:, None] + 1).astype(f32)
    tail_add = jnp.sum(pick_next[:, :, None, None] * next_tails, axis=1)
    tokens_grad = tokens_grad.reshape(2, HALF, width)
    tokens_grad = jnp.concatenate(
        [tokens_grad[:, : HALF - (CONV - 1)], tokens_grad[:, HALF - (CONV - 1) :] + tail_add],
        axis=1,
    ).astype(bf16)
    layer_rows = nt((hidden_two + down_rows).astype(bf16), deal_low).astype(bf16)
    outs = jnp.stack([layer_rows.reshape(2, HALF, width), tokens_grad])
    outs_other = swap_cores(outs)
    outs = jnp.where(
        core == 0,
        jnp.concatenate([outs, outs_other], axis=2),
        jnp.concatenate([outs_other, outs], axis=2),
    )
    return (
        outs[0],
        outs[1],
        small_total[7],
        early_outs[0],
        early_outs[5],
        early_outs[1],
        early_outs[2].T,
        small_total[6, RATE_AT : RATE_AT + HPG],
        small_total[6, LANES + RATE_AT : LANES + RATE_AT + HPG],
        small_total[0:4],
        small_total[4],
        small_total[5],
        early_outs[3].T,
        small_total[8],
        early_outs[4].transpose(1, 0, 2),
        third_total[:, 2048:2304].T,
        small_total[9],
        third_total[:, 0:1024],
        third_total[:, 1024:2048].T,
    )


def layer(*args):
    tokens, lengths = args[0], args[2]
    fits = lax.axis_size("seq") == 16 and lax.axis_size("head") == 2
    fits = fits and lengths.shape == (2, 1) and tokens.shape[1] == ROWS
    return dealt_device(*args) if fits else on_device(*args)


def solution(mesh):
    return jax.shard_map(
        layer,
        mesh=mesh,
        in_specs=(
            P(None, "seq", None),
            P(None, "seq", None),
            P(),
            P(),
            P(),
            P("seq", "head"),
            P("seq", "head"),
            P("seq", "head"),
            P("seq", "head"),
            P("head"),
            P("head"),
            P(None, "head"),
            P("head"),
            P("head"),
            P("head", "seq"),
            P(),
            P("seq", None, "head"),
            P("head", "seq"),
            P(),
            P("seq", "head"),
            P("head", "seq"),
        ),
        out_specs=(
            P(None, "seq", None),
            P(None, "seq", None),
            P(),
            P("seq", "head"),
            P("seq", "head"),
            P("seq", "head"),
            P("seq", "head"),
            P("head"),
            P("head"),
            P(None, "head"),
            P("head"),
            P("head"),
            P("head", "seq"),
            P(),
            P("seq", None, "head"),
            P("head", "seq"),
            P(),
            P("seq", "head"),
            P("head", "seq"),
        ),
        check_vma=False,
    )
```

profile of v0, /device:TPU:1, one launch (start us, length us, event | category | flops | bytes accessed | tf_op | source)
XLA Modules:
  0.0 305.4 jit_solution(2414165929069556647)
XLA Ops:
  12.9 6.1 %collective-permute-done.3 = bf16[32,2560]{1,0:T(8,128)(2,1)S(1)} collective-permute-done((bf16[32,2560]{1,0:T(8,128)(2,1)S(1)}, bf16[32,2560]{1,0:T(8,128)(2,1)S(1)}, u32[]{:S(2)}, u32[]{:S(2)}) %collective-permute-start.3) | collective-permute-done | bytes 163872 | tf_op jit(solution)/shard_map/ppermute | solution.py:1592
  22.1 3.8 %collective-permute-start.7 = (bf16[32,2304]{1,0:T(8,128)(2,1)}, bf16[32,2304]{1,0:T(8,128)(2,1)S(1)}, u32[]{:S(2)}, u32[]{:S(2)}) collective-permute-start(bf16[32,2304]{1,0:T(8,128)(2,1)} %shard_map.339), channel_id=1, source_target_pairs={{0,8},{2,10},{4,12},{6,14},{8,0},{10,2},{12,4},{14,6},{16,24},{18,... | collective-permute-start | bytes 442376 | tf_op jit(solution)/shard_map/ppermute | solution.py:1592
  31.3 5.1 %collective-permute-done.9.refs_3_ = bf16[32,2304]{1,0:T(8,128)(2,1)S(1)} collective-permute-done((bf16[32,2304]{1,0:T(8,128)(2,1)}, bf16[32,2304]{1,0:T(8,128)(2,1)S(1)}, u32[]{:S(2)}, u32[]{:S(2)}) %collective-permute-start.9) | collective-permute-done | bytes 147488 | tf_op jit(solution)/shard_map/ppermute | solution.py:1592
  36.4 5.3 %collective-permute-start.10 = (bf16[128,1280]{1,0:T(8,128)(2,1)}, bf16[128,1280]{1,0:T(8,128)(2,1)}, u32[]{:S(2)}, u32[]{:S(2)}) collective-permute-start(bf16[128,1280]{1,0:T(8,128)(2,1)} %copy-done.2), channel_id=1, source_target_pairs={{0,1},{1,0},{2,3},{3,2},{4,5},{5,4},{6,7},{7,6},{8,9},{9,8},{10,11... | collective-permute-start | bytes 983048 | tf_op jit(solution)/shard_map/ppermute | solution.py:1587
  45.4 5.3 %collective-permute-start.17 = (bf16[128,1280]{1,0:T(8,128)(2,1)S(1)}, bf16[128,1280]{1,0:T(8,128)(2,1)S(1)}, u32[]{:S(2)}, u32[]{:S(2)}) collective-permute-start(bf16[128,1280]{1,0:T(8,128)(2,1)S(1)} %pad_maximum_fusion.2.refs_11_.refs_13_), channel_id=1, source_target_pairs={{0,1},{1,0},{2,3},{3,2},{4,5},{5,4},{6,7},{7,6},{8,9},{9,8},{10,11... | collective-permute-start | bytes 983048 | tf_op jit(solution)/shard_map/ppermute | solution.py:1587
  56.7 6.7 %in_kernel.1 = (bf16[160,512]{1,0:T(8,128)(2,1)}, bf16[160,512]{1,0:T(8,128)(2,1)}, bf16[160,1024]{1,0:T(8,128)(2,1)}, f32[128,1024]{1,0:T(8,128)}, f32[128,1024...) custom-call(s32[2]{0:T(128)} %pad_add_fusion.refs_0_, ...), custom_call_target="tpu_custom_call" | custom-call | tf_op jit(solution)/shard_map/in_kernel/pallas_call | solution.py:1555
  64.2 4.7 %all-to-all-start = ((bf16[32,16,128]{2,1,0:T(8,128)(2,1)}), bf16[32,16,128]{2,1,0:T(8,128)(2,1)S(1)}, u32[]{:S(2)}, u32[]{:S(2)}) async-start(bf16[32,16,128]{2,1,0:T(8,128)(2,1)} %shard_map.341), calls=%async_computation | async-start | bytes 262144 | tf_op jit(solution)/shard_map/all_to_all | solution.py:1604
  69.7 7.3 %all-to-all-done.refs_2_ = bf16[32,16,128]{2,1,0:T(8,128)(2,1)S(1)} async-done(((bf16[32,16,128]{2,1,0:T(8,128)(2,1)}), bf16[32,16,128]{2,1,0:T(8,128)(2,1)S(1)}, u32[]{:S(2)}, u32[]{:S(2)}) %all-to-all-start) | async-done | bytes 131104 | tf_op jit(solution)/shard_map/all_to_all | solution.py:1604
  81.9 8.3 %all-to-all-done.1.refs_2_ = f32[32,8,128]{2,1,0:T(8,128)S(1)} async-done(((f32[32,8,128]{2,1,0:T(8,128)}), f32[32,8,128]{2,1,0:T(8,128)S(1)}, u32[]{:S(2)}, u32[]{:S(2)}) %all-to-all-start.1) | async-done | bytes 131104 | tf_op jit(solution)/shard_map/all_to_all | solution.py:1604
  90.9 5.5 %mix_kernel.1 = (f32[128,1024]{1,0:T(8,128)}, bf16[128,1024]{1,0:T(8,128)(2,1)}, f32[128,512]{1,0:T(8,128)}, bf16[128,512]{1,0:T(8,128)(2,1)}, bf16[16,96,128]{2,1,0:T(8,128)(2,1)}) custom-call(s32[2]{0:T(128)} %pad_add_fusion.refs_0_, bf16[160,512]{1,0:T(8,128)(2,1)} %get-tuple-element.87.refs_1_.refs_11_, f32[32,8,128]{2,1,0:T(8,128)} %copy-done.32, ...), custom_call_target="tpu_custom_call" | custom-call | tf_op jit(solution)/shard_map/mix_kernel/pallas_call | solution.py:1555
  97.4 3.7 %all-to-all-start.2 = ((bf16[16,96,128]{2,1,0:T(8,128)(2,1)}), bf16[16,96,128]{2,1,0:T(8,128)(2,1)S(1)}, u32[]{:S(2)}, u32[]{:S(2)}) async-start(bf16[16,96,128]{2,1,0:T(8,128)(2,1)} %shard_map.342), calls=%async_computation.2 | async-start | bytes 786432 | tf_op jit(solution)/shard_map/all_to_all | solution.py:1604
  103.3 8.6 %all-to-all-done.2.refs_2_ = bf16[16,96,128]{2,1,0:T(8,128)(2,1)S(1)} async-done(((bf16[16,96,128]{2,1,0:T(8,128)(2,1)}), bf16[16,96,128]{2,1,0:T(8,128)(2,1)S(1)}, u32[]{:S(2)}, u32[]{:S(2)}) %all-to-all-start.2) | async-done | bytes 393248 | tf_op jit(solution)/shard_map/all_to_all | solution.py:1604
  116.8 6.4 %attend_kernel.1 = (bf16[16,32,128]{2,1,0:T(8,128)(2,1)}, f32[1024,1]{1,0:T(8,128)}, f32[1024,64]{1,0:T(8,128)}) custom-call(s32[2]{0:T(128)} %pad_add_fusion.refs_0_, s32[2,32]{1,0:T(2,128)} %refs_1_.9, bf16[16,96,128]{2,1,0:T(8,128)(2,1)} %copy-done.4, bf16[16,96,128]{2,1,0:T(8,128)(2,1)} %copy-done.21), custom_call_target="tpu_custom_call" | custom-call | tf_op jit(solution)/shard_map/attend_kernel/pallas_call | solution.py:1555
  124.5 3.7 %all-to-all-start.3 = ((bf16[16,32,128]{2,1,0:T(8,128)(2,1)}), bf16[16,32,128]{2,1,0:T(8,128)(2,1)S(1)}, u32[]{:S(2)}, u32[]{:S(2)}) async-start(bf16[16,32,128]{2,1,0:T(8,128)(2,1)} %get-tuple-element.96), calls=%async_computation.3 | async-start | bytes 262144 | tf_op jit(solution)/shard_map/all_to_all | solution.py:1604
  128.3 6.4 %all-to-all-done.3.refs_1_ = bf16[16,32,128]{2,1,0:T(8,128)(2,1)S(1)} async-done(((bf16[16,32,128]{2,1,0:T(8,128)(2,1)}), bf16[16,32,128]{2,1,0:T(8,128)(2,1)S(1)}, u32[]{:S(2)}, u32[]{:S(2)}) %all-to-all-start.3) | async-done | bytes 131104 | tf_op jit(solution)/shard_map/all_to_all | solution.py:1604
  135.6 7.8 %mlp_kernel.1 = (f32[128,512]{1,0:T(8,128)}, f32[128,512]{1,0:T(8,128)}, bf16[256,512]{1,0:T(8,128)(2,1)}, bf16[128,3328]{1,0:T(8,128)(2,1)}, bf16[128,3328]{1,0...) custom-call(s32[2]{0:T(128)} %pad_add_fusion.refs_0_, ...), custom_call_target="tpu_custom_call" | custom-call | tf_op jit(solution)/shard_map/mlp_kernel/pallas_call | solution.py:1555
  145.1 3.5 %all-to-all-start.4 = ((bf16[16,32,128]{2,1,0:T(8,128)(2,1)}), bf16[16,32,128]{2,1,0:T(8,128)(2,1)S(1)}, u32[]{:S(2)}, u32[]{:S(2)}) async-start(bf16[16,32,128]{2,1,0:T(8,128)(2,1)} %get-tuple-element.102), calls=%async_computation.4 | async-start | bytes 262144 | tf_op jit(solution)/shard_map/all_to_all | solution.py:1604
  149.6 3.6 %third_grad_kernel.1 = (bf16[128,2304]{1,0:T(8,128)(2,1)}, bf16[128,2304]{1,0:T(8,128)(2,1)}, bf16[128,2304]{1,0:T(8,128)(2,1)}, bf16[128,2304]{1,0:T(8,128)(2,1)}) custom-call(bf16[128,3328]{1,0:T(8,128)(2,1)} %get-tuple-element.104.refs_0_, bf16[128,3328]{1,0:T(8,128)(2,1)} %copy-done.34, bf16[256,512]{1,0:T(8,128)(2,1)} %get-tuple-element.106.refs_2_), custom_call_target="tpu_custom_call" | custom-call | tf_op jit(solution)/shard_map/third_grad_kernel/pallas_call | solution.py:1555
  156.5 9.2 %attend_back_kernel.1 = (f32[16,96,128]{2,1,0:T(8,128)}, bf16[16,96,128]{2,1,0:T(8,128)(2,1)}) custom-call(s32[2]{0:T(128)} %pad_add_fusion.refs_0_, s32[2,32]{1,0:T(2,128)} %refs_1_.9, bf16[16,96,128]{2,1,0:T(8,128)(2,1)} %copy-done.4, bf16[16,96,128]{2,1,0:T(8,128)(2,1)} %copy-done.21, bf16[16,32,128]{2,1,0:T(8,128)(2,1)} %copy-done.47, ...), custom_call_target="tpu_custom_call" | custom-call | tf_op jit(solution)/shard_map/attend_back_kernel/pallas_call | solution.py:1555
  170.4 3.8 %all-to-all-start.5 = ((bf16[16,96,128]{2,1,0:T(8,128)(2,1)}), bf16[16,96,128]{2,1,0:T(8,128)(2,1)S(1)}, u32[]{:S(2)}, u32[]{:S(2)}) async-start(bf16[16,96,128]{2,1,0:T(8,128)(2,1)} %add_convert_fusion), calls=%async_computation.5 | async-start | bytes 786432 | tf_op jit(solution)/shard_map/all_to_all | solution.py:1604
  176.4 16.2 %collective-permute-done.31.refs_21_.refs_1_ = bf16[128,2304]{1,0:T(8,128)(2,1)S(1)} collective-permute-done((bf16[128,2304]{1,0:T(8,128)(2,1)S(1)}, bf16[128,2304]{1,0:T(8,128)(2,1)S(1)}, u32[]{:S(2)}, u32[]{:S(2)}) %collective-permute-start.31) | collective-permute-done | bytes 589856 | tf_op jit(solution)/shard_map/ppermute | solution.py:1592
  194.8 6.9 %mix_back_kernel.1 = (bf16[128,3328]{1,0:T(8,128)(2,1)}, bf16[128,3328]{1,0:T(8,128)(2,1)}, f32[128,1024]{1,0:T(8,128)}, bf16[128,1024]{1,0:T(8,128)(2,1)}, f32[...) custom-call(s32[2]{0:T(128)} %pad_add_fusion.refs_0_, ...), custom_call_target="tpu_custom_call" | custom-call | tf_op jit(solution)/shard_map/mix_back_kernel/pallas_call | solution.py:1555
  203.5 4.7 %all-to-all-start.6 = ((f32[32,8,128]{2,1,0:T(8,128)}), f32[32,8,128]{2,1,0:T(8,128)S(1)}, u32[]{:S(2)}, u32[]{:S(2)}) async-start(f32[32,8,128]{2,1,0:T(8,128)} %get-tuple-element.117), calls=%async_computation.6 | async-start | bytes 262144 | tf_op jit(solution)/shard_map/all_to_all | solution.py:1604
  212.4 6.9 %collective-permute-done.34.refs_5_.refs_3_ = bf16[128,2304]{1,0:T(8,128)(2,1)S(1)} collective-permute-done((bf16[128,2304]{1,0:T(8,128)(2,1)S(1)}, bf16[128,2304]{1,0:T(8,128)(2,1)S(1)}, u32[]{:S(2)}, u32[]{:S(2)}) %collective-permute-start.34) | collective-permute-done | bytes 589856 | tf_op jit(solution)/shard_map/ppermute | solution.py:1592
  222.4 4.6 %all-to-all-start.7 = ((f32[32,8,128]{2,1,0:T(8,128)}), f32[32,8,128]{2,1,0:T(8,128)S(1)}, u32[]{:S(2)}, u32[]{:S(2)}) async-start(f32[32,8,128]{2,1,0:T(8,128)} %backward_scan_kernel.1.refs_4_), calls=%async_computation.7 | async-start | bytes 262144 | tf_op jit(solution)/shard_map/all_to_all | solution.py:1604
  235.9 8.6 %in_back_kernel.1 = (bf16[176,1152]{1,0:T(8,128)(2,1)}, bf16[176,1152]{1,0:T(8,128)(2,1)}, f32[128,512]{1,0:T(8,128)}) custom-call(s32[2]{0:T(128)} %pad_add_fusion.refs_0_, f32[32,8,128]{2,1,0:T(8,128)} %copy-done.48, f32[32,8,128]{2,1,0:T(8,128)} %copy-done.32, f32[2,2,16,512]{3,2,1,0:T(8,128)} %get-tuple-element.122.refs_3_, ...), custom_call_target="tpu_custom_call" | custom-call | tf_op jit(solution)/shard_map/in_back_kernel/pallas_call | solution.py:1555
  245.1 6.1 %collective-permute-done.38.refs_5_.refs_7_ = bf16[128,1792]{1,0:T(8,128)(2,1)S(1)} collective-permute-done((bf16[128,1792]{1,0:T(8,128)(2,1)S(1)}, bf16[128,1792]{1,0:T(8,128)(2,1)S(1)}, u32[]{:S(2)}, u32[]{:S(2)}) %collective-permute-start.38) | collective-permute-done | bytes 458784 | tf_op jit(solution)/shard_map/ppermute | solution.py:1592
  261.8 4.9 %collective-permute-done.40.refs_2_ = bf16[128,640]{1,0:T(8,128)(2,1)S(1)} collective-permute-done((bf16[128,640]{1,0:T(8,128)(2,1)}, bf16[128,640]{1,0:T(8,128)(2,1)S(1)}, u32[]{:S(2)}, u32[]{:S(2)}) %collective-permute-start.40) | collective-permute-done | bytes 163872 | tf_op jit(solution)/shard_map/ppermute | solution.py:1592
  267.5 4.8 %all-to-all-start.8 = ((bf16[16,16,1024]{2,1,0:T(8,128)(2,1)}), bf16[16,16,1024]{2,1,0:T(8,128)(2,1)S(1)}, u32[]{:S(2)}, u32[]{:S(2)}) async-start(bf16[16,16,1024]{2,1,0:T(8,128)(2,1)} %shard_map.344), calls=%async_computation.8 | async-start | bytes 1048576 | tf_op jit(solution)/shard_map/all_to_all | solution.py:1604
  280.0 5.4 %collective-permute-done.43.refs_1_ = bf16[32,2432]{1,0:T(8,128)(2,1)S(1)} collective-permute-done((bf16[32,2432]{1,0:T(8,128)(2,1)}, bf16[32,2432]{1,0:T(8,128)(2,1)S(1)}, u32[]{:S(2)}, u32[]{:S(2)}) %collective-permute-start.43) | collective-permute-done | bytes 155680 | tf_op jit(solution)/shard_map/ppermute | solution.py:1592
  285.4 6.5 %collective-permute-done.44.refs_2_ = bf16[32,2432]{1,0:T(8,128)(2,1)S(1)} collective-permute-done((bf16[32,2432]{1,0:T(8,128)(2,1)}, bf16[32,2432]{1,0:T(8,128)(2,1)S(1)}, u32[]{:S(2)}, u32[]{:S(2)}) %collective-permute-start.44) | collective-permute-done | bytes 155680 | tf_op jit(solution)/shard_map/ppermute | solution.py:1592
  295.0 7.4 %collective-permute-start.42 = (bf16[2,2,64,512]{3,2,1,0:T(8,128)(2,1)S(1)}, bf16[2,2,64,512]{3,2,1,0:T(8,128)(2,1)S(1)}, u32[]{:S(2)}, u32[]{:S(2)}) collective-permute-start(bf16[2,2,64,512]{3,2,1,0:T(8,128)(2,1)S(1)} %maximum_maximum_fusion), channel_id=1, source_target_pairs={{0,1},{1,0},{2,3},{3,2},{4,5},{5,4},{6,7},{7,6},{8,9},{9,8},{10,11... | collective-permute-start | bytes 786440 | tf_op jit(solution)/shard_map/ppermute | solution.py:1587
  (299 shorter events, 106.0 us)
Async XLA Ops:
  10.7 31.7 %collective-permute-start = (f32[8,512]{1,0:T(8,128)S(1)}, f32[8,512]{1,0:T(8,128)S(1)}, u32[]{:S(2)}, u32[]{:S(2)}) collective-permute-start(f32[8,512]{1,0:T(8,128)S(1)} %concatenate.46.refs_4_.refs_8_.refs_14_), channel_id=1, source_target_pairs={{0,1},{1,0},{2,3},{3,2},{4,5},{5,4},{6,7},{7,6},{8,9},{9,8},{10,11... | collective-permute-start | bytes 49160 | tf_op jit(solution)/shard_map/ppermute | solution.py:1587
  19.1 22.6 %collective-permute-start.6 = (bf16[128,1280]{1,0:T(8,128)(2,1)S(1)}, bf16[128,1280]{1,0:T(8,128)(2,1)S(1)}, u32[]{:S(2)}, u32[]{:S(2)}) collective-permute-start(bf16[128,1280]{1,0:T(8,128)(2,1)S(1)} %pad_maximum_fusion.1.refs_1_.refs_6_.refs_20_), channel_id=1, source_target_pairs={{0,6},{2,4},{4,2},{6,0},{8,14},{10,12},{12,10},{14,8},{16,22},{18,... | collective-permute-start | bytes 983048 | tf_op jit(solution)/shard_map/ppermute | solution.py:1592
  28.9 14.2 %collective-permute-start.4 = (bf16[128,1280]{1,0:T(8,128)(2,1)}, bf16[128,1280]{1,0:T(8,128)(2,1)S(1)}, u32[]{:S(2)}, u32[]{:S(2)}) collective-permute-start(bf16[128,1280]{1,0:T(8,128)(2,1)} %copy-done.2), channel_id=1, source_target_pairs={{0,2},{2,0},{4,6},{6,4},{8,10},{10,8},{12,14},{14,12},{16,18},{18,... | collective-permute-start | bytes 983048 | tf_op jit(solution)/shard_map/ppermute | solution.py:1592
  31.0 13.3 %collective-permute-start.5 = (bf16[128,1280]{1,0:T(8,128)(2,1)}, bf16[128,1280]{1,0:T(8,128)(2,1)S(1)}, u32[]{:S(2)}, u32[]{:S(2)}) collective-permute-start(bf16[128,1280]{1,0:T(8,128)(2,1)} %copy-done.2), channel_id=1, source_target_pairs={{0,4},{2,6},{4,0},{6,2},{8,12},{10,14},{12,8},{14,10},{16,20},{18,... | collective-permute-start | bytes 983048 | tf_op jit(solution)/shard_map/ppermute | solution.py:1592
  43.1 20.4 %collective-permute-start.15 = (bf16[128,1280]{1,0:T(8,128)(2,1)S(1)}, bf16[128,1280]{1,0:T(8,128)(2,1)S(1)}, u32[]{:S(2)}, u32[]{:S(2)}) collective-permute-start(bf16[128,1280]{1,0:T(8,128)(2,1)S(1)} %pad_maximum_fusion.2.refs_11_.refs_13_), channel_id=1, source_target_pairs={{0,4},{2,6},{4,0},{6,2},{8,12},{10,14},{12,8},{14,10},{16,20},{18,... | collective-permute-start | bytes 983048 | tf_op jit(solution)/shard_map/ppermute | solution.py:1592
  44.3 24.9 %collective-permute-start.16 = (bf16[128,1280]{1,0:T(8,128)(2,1)S(1)}, bf16[128,1280]{1,0:T(8,128)(2,1)S(1)}, u32[]{:S(2)}, u32[]{:S(2)}) collective-permute-start(bf16[128,1280]{1,0:T(8,128)(2,1)S(1)} %pad_maximum_fusion.2.refs_11_.refs_13_), channel_id=1, source_target_pairs={{0,6},{2,4},{4,2},{6,0},{8,14},{10,12},{12,10},{14,8},{16,22},{18,... | collective-permute-start | bytes 983048 | tf_op jit(solution)/shard_map/ppermute | solution.py:1592
  45.4 24.0 %collective-permute-start.17 = (bf16[128,1280]{1,0:T(8,128)(2,1)S(1)}, bf16[128,1280]{1,0:T(8,128)(2,1)S(1)}, u32[]{:S(2)}, u32[]{:S(2)}) collective-permute-start(bf16[128,1280]{1,0:T(8,128)(2,1)S(1)} %pad_maximum_fusion.2.refs_11_.refs_13_), channel_id=1, source_target_pairs={{0,1},{1,0},{2,3},{3,2},{4,5},{5,4},{6,7},{7,6},{8,9},{9,8},{10,11... | collective-permute-start | bytes 983048 | tf_op jit(solution)/shard_map/ppermute | solution.py:1587
  54.2 42.2 %collective-permute-start.21 = (bf16[128,2304]{1,0:T(8,128)(2,1)S(1)}, bf16[128,2304]{1,0:T(8,128)(2,1)S(1)}, u32[]{:S(2)}, u32[]{:S(2)}) collective-permute-start(bf16[128,2304]{1,0:T(8,128)(2,1)S(1)} %pad_maximum_fusion.refs_19_.refs_6_), channel_id=1, source_target_pairs={{0,2},{2,0},{4,6},{6,4},{8,10},{10,8},{12,14},{14,12},{16,18},{18,... | collective-permute-start | bytes 1769480 | tf_op jit(solution)/shard_map/ppermute | solution.py:1592
  54.6 41.7 %collective-permute-start.22 = (bf16[128,2304]{1,0:T(8,128)(2,1)S(1)}, bf16[128,2304]{1,0:T(8,128)(2,1)S(1)}, u32[]{:S(2)}, u32[]{:S(2)}) collective-permute-start(bf16[128,2304]{1,0:T(8,128)(2,1)S(1)} %pad_maximum_fusion.refs_19_.refs_6_), channel_id=1, source_target_pairs={{0,4},{2,6},{4,0},{6,2},{8,12},{10,14},{12,8},{14,10},{16,20},{18,... | collective-permute-start | bytes 1769480 | tf_op jit(solution)/shard_map/ppermute | solution.py:1592
  64.2 12.9 %all-to-all-start = ((bf16[32,16,128]{2,1,0:T(8,128)(2,1)}), bf16[32,16,128]{2,1,0:T(8,128)(2,1)S(1)}, u32[]{:S(2)}, u32[]{:S(2)}) async-start(bf16[32,16,128]{2,1,0:T(8,128)(2,1)} %shard_map.341), calls=%async_computation | async-start | bytes 262144 | tf_op jit(solution)/shard_map/all_to_all | solution.py:1604
  68.9 13.0 %collective-permute-start.18 = (bf16[128,1280]{1,0:T(8,128)(2,1)S(1)}, bf16[128,1280]{1,0:T(8,128)(2,1)S(1)}, u32[]{:S(2)}, u32[]{:S(2)}) collective-permute-start(bf16[128,1280]{1,0:T(8,128)(2,1)S(1)} %copy-done.6), channel_id=1, source_target_pairs={{0,1},{1,0},{2,3},{3,2},{4,5},{5,4},{6,7},{7,6},{8,9},{9,8},{10,11... | collective-permute-start | bytes 983048 | tf_op jit(solution)/shard_map/ppermute | solution.py:1587
  69.2 12.7 %collective-permute-start.19 = (bf16[128,1280]{1,0:T(8,128)(2,1)}, bf16[128,1280]{1,0:T(8,128)(2,1)}, u32[]{:S(2)}, u32[]{:S(2)}) collective-permute-start(bf16[128,1280]{1,0:T(8,128)(2,1)} %copy-done.7), channel_id=1, source_target_pairs={{0,1},{1,0},{2,3},{3,2},{4,5},{5,4},{6,7},{7,6},{8,9},{9,8},{10,11... | collective-permute-start | bytes 983048 | tf_op jit(solution)/shard_map/ppermute | solution.py:1587
  69.5 12.5 %collective-permute-start.20 = (bf16[128,1280]{1,0:T(8,128)(2,1)S(1)}, bf16[128,1280]{1,0:T(8,128)(2,1)S(1)}, u32[]{:S(2)}, u32[]{:S(2)}) collective-permute-start(bf16[128,1280]{1,0:T(8,128)(2,1)S(1)} %collective-permute-done.16.refs_3_.refs_14_.refs_16_), channel_id=1, source_target_pairs={{0,1},{1,0},{2,3},{3,2},{4,5},{5,4},{6,7},{7,6},{8,9},{9,8},{10,11... | collective-permute-start | bytes 983048 | tf_op jit(solution)/shard_map/ppermute | solution.py:1587
  97.4 14.5 %all-to-all-start.2 = ((bf16[16,96,128]{2,1,0:T(8,128)(2,1)}), bf16[16,96,128]{2,1,0:T(8,128)(2,1)S(1)}, u32[]{:S(2)}, u32[]{:S(2)}) async-start(bf16[16,96,128]{2,1,0:T(8,128)(2,1)} %shard_map.342), calls=%async_computation.2 | async-start | bytes 786432 | tf_op jit(solution)/shard_map/all_to_all | solution.py:1604
  101.1 22.1 %collective-permute-start.24 = (bf16[128,2304]{1,0:T(8,128)(2,1)S(1)}, bf16[128,2304]{1,0:T(8,128)(2,1)S(1)}, u32[]{:S(2)}, u32[]{:S(2)}) collective-permute-start(bf16[128,2304]{1,0:T(8,128)(2,1)S(1)} %copy-done.1), channel_id=1, source_target_pairs={{0,6},{2,4},{4,2},{6,0},{8,14},{10,12},{12,10},{14,8},{16,22},{18,... | collective-permute-start | bytes 1769480 | tf_op jit(solution)/shard_map/ppermute | solution.py:1592
  114.7 13.5 %collective-permute-start.25 = (bf16[128,2304]{1,0:T(8,128)(2,1)S(1)}, bf16[128,2304]{1,0:T(8,128)(2,1)S(1)}, u32[]{:S(2)}, u32[]{:S(2)}) collective-permute-start(bf16[128,2304]{1,0:T(8,128)(2,1)S(1)} %copy-done.1), channel_id=1, source_target_pairs={{0,1},{1,0},{2,3},{3,2},{4,5},{5,4},{6,7},{7,6},{8,9},{9,8},{10,11... | collective-permute-start | bytes 1769480 | tf_op jit(solution)/shard_map/ppermute | solution.py:1587
  114.7 13.5 %collective-permute-start.26 = (bf16[128,2304]{1,0:T(8,128)(2,1)}, bf16[128,2304]{1,0:T(8,128)(2,1)S(1)}, u32[]{:S(2)}, u32[]{:S(2)}) collective-permute-start(bf16[128,2304]{1,0:T(8,128)(2,1)} %copy-done.14), channel_id=1, source_target_pairs={{0,1},{1,0},{2,3},{3,2},{4,5},{5,4},{6,7},{7,6},{8,9},{9,8},{10,11... | collective-permute-start | bytes 1769480 | tf_op jit(solution)/shard_map/ppermute | solution.py:1587
  115.2 13.1 %collective-permute-start.27 = (bf16[128,2304]{1,0:T(8,128)(2,1)}, bf16[128,2304]{1,0:T(8,128)(2,1)}, u32[]{:S(2)}, u32[]{:S(2)}) collective-permute-start(bf16[128,2304]{1,0:T(8,128)(2,1)} %copy-done.15), channel_id=1, source_target_pairs={{0,1},{1,0},{2,3},{3,2},{4,5},{5,4},{6,7},{7,6},{8,9},{9,8},{10,11... | collective-permute-start | bytes 1769480 | tf_op jit(solution)/shard_map/ppermute | solution.py:1587
  170.4 23.5 %all-to-all-start.5 = ((bf16[16,96,128]{2,1,0:T(8,128)(2,1)}), bf16[16,96,128]{2,1,0:T(8,128)(2,1)S(1)}, u32[]{:S(2)}, u32[]{:S(2)}) async-start(bf16[16,96,128]{2,1,0:T(8,128)(2,1)} %add_convert_fusion), calls=%async_computation.5 | async-start | bytes 786432 | tf_op jit(solution)/shard_map/all_to_all | solution.py:1604
  174.1 18.5 %collective-permute-start.31 = (bf16[128,2304]{1,0:T(8,128)(2,1)S(1)}, bf16[128,2304]{1,0:T(8,128)(2,1)S(1)}, u32[]{:S(2)}, u32[]{:S(2)}) collective-permute-start(bf16[128,2304]{1,0:T(8,128)(2,1)S(1)} %copy-done.68), channel_id=1, source_target_pairs={{0,2},{2,0},{4,6},{6,4},{8,10},{10,8},{12,14},{14,12},{16,18},{18,... | collective-permute-start | bytes 1769480 | tf_op jit(solution)/shard_map/ppermute | solution.py:1592
  175.2 18.6 %collective-permute-start.32 = (bf16[128,2304]{1,0:T(8,128)(2,1)S(1)}, bf16[128,2304]{1,0:T(8,128)(2,1)S(1)}, u32[]{:S(2)}, u32[]{:S(2)}) collective-permute-start(bf16[128,2304]{1,0:T(8,128)(2,1)S(1)} %copy-done.67), channel_id=1, source_target_pairs={{0,4},{2,6},{4,0},{6,2},{8,12},{10,14},{12,8},{14,10},{16,20},{18,... | collective-permute-start | bytes 1769480 | tf_op jit(solution)/shard_map/ppermute | solution.py:1592
  202.4 16.9 %collective-permute-start.34 = (bf16[128,2304]{1,0:T(8,128)(2,1)S(1)}, bf16[128,2304]{1,0:T(8,128)(2,1)S(1)}, u32[]{:S(2)}, u32[]{:S(2)}) collective-permute-start(bf16[128,2304]{1,0:T(8,128)(2,1)S(1)} %copy-done.66), channel_id=1, source_target_pairs={{0,6},{2,4},{4,2},{6,0},{8,14},{10,12},{12,10},{14,8},{16,22},{18,... | collective-permute-start | bytes 1769480 | tf_op jit(solution)/shard_map/ppermute | solution.py:1592
  203.5 16.5 %all-to-all-start.6 = ((f32[32,8,128]{2,1,0:T(8,128)}), f32[32,8,128]{2,1,0:T(8,128)S(1)}, u32[]{:S(2)}, u32[]{:S(2)}) async-start(f32[32,8,128]{2,1,0:T(8,128)} %get-tuple-element.117), calls=%async_computation.6 | async-start | bytes 262144 | tf_op jit(solution)/shard_map/all_to_all | solution.py:1604
  222.4 12.8 %all-to-all-start.7 = ((f32[32,8,128]{2,1,0:T(8,128)}), f32[32,8,128]{2,1,0:T(8,128)S(1)}, u32[]{:S(2)}, u32[]{:S(2)}) async-start(f32[32,8,128]{2,1,0:T(8,128)} %backward_scan_kernel.1.refs_4_), calls=%async_computation.7 | async-start | bytes 262144 | tf_op jit(solution)/shard_map/all_to_all | solution.py:1604
  227.0 18.1 %collective-permute-start.36 = (bf16[128,1792]{1,0:T(8,128)(2,1)S(1)}, bf16[128,1792]{1,0:T(8,128)(2,1)S(1)}, u32[]{:S(2)}, u32[]{:S(2)}) collective-permute-start(bf16[128,1792]{1,0:T(8,128)(2,1)S(1)} %copy-done.71), channel_id=1, source_target_pairs={{0,2},{2,0},{4,6},{6,4},{8,10},{10,8},{12,14},{14,12},{16,18},{18,... | collective-permute-start | bytes 1376264 | tf_op jit(solution)/shard_map/ppermute | solution.py:1592
  228.5 16.7 %collective-permute-start.37 = (bf16[128,1792]{1,0:T(8,128)(2,1)S(1)}, bf16[128,1792]{1,0:T(8,128)(2,1)S(1)}, u32[]{:S(2)}, u32[]{:S(2)}) collective-permute-start(bf16[128,1792]{1,0:T(8,128)(2,1)S(1)} %copy-done.70), channel_id=1, source_target_pairs={{0,4},{2,6},{4,0},{6,2},{8,12},{10,14},{12,8},{14,10},{16,20},{18,... | collective-permute-start | bytes 1376264 | tf_op jit(solution)/shard_map/ppermute | solution.py:1592
  229.7 21.6 %collective-permute-start.38 = (bf16[128,1792]{1,0:T(8,128)(2,1)S(1)}, bf16[128,1792]{1,0:T(8,128)(2,1)S(1)}, u32[]{:S(2)}, u32[]{:S(2)}) collective-permute-start(bf16[128,1792]{1,0:T(8,128)(2,1)S(1)} %copy-done.69), channel_id=1, source_target_pairs={{0,6},{2,4},{4,2},{6,0},{8,14},{10,12},{12,10},{14,8},{16,22},{18,... | collective-permute-start | bytes 1376264 | tf_op jit(solution)/shard_map/ppermute | solution.py:1592
  256.2 16.0 %collective-permute-start.46 = (bf16[32,2304]{1,0:T(8,128)(2,1)S(1)}, bf16[32,2304]{1,0:T(8,128)(2,1)S(1)}, u32[]{:S(2)}, u32[]{:S(2)}) collective-permute-start(bf16[32,2304]{1,0:T(8,128)(2,1)S(1)} %copy-done.74), channel_id=1, source_target_pairs={{0,8},{2,10},{4,12},{6,14},{8,0},{10,2},{12,4},{14,6},{16,24},{18,... | collective-permute-start | bytes 442376 | tf_op jit(solution)/shard_map/ppermute | solution.py:1592
  257.2 15.0 %collective-permute-start.47 = (bf16[32,2304]{1,0:T(8,128)(2,1)S(1)}, bf16[32,2304]{1,0:T(8,128)(2,1)S(1)}, u32[]{:S(2)}, u32[]{:S(2)}) collective-permute-start(bf16[32,2304]{1,0:T(8,128)(2,1)S(1)} %copy-done.73), channel_id=1, source_target_pairs={{0,16},{2,18},{4,20},{6,22},{8,24},{10,26},{12,28},{14,30},{16,0},... | collective-permute-start | bytes 442376 | tf_op jit(solution)/shard_map/ppermute | solution.py:1592
  258.9 13.3 %collective-permute-start.48 = (bf16[32,2304]{1,0:T(8,128)(2,1)S(1)}, bf16[32,2304]{1,0:T(8,128)(2,1)S(1)}, u32[]{:S(2)}, u32[]{:S(2)}) collective-permute-start(bf16[32,2304]{1,0:T(8,128)(2,1)S(1)} %copy-done.72), channel_id=1, source_target_pairs={{0,24},{2,26},{4,28},{6,30},{8,16},{10,18},{12,20},{14,22},{16,8},... | collective-permute-start | bytes 442376 | tf_op jit(solution)/shard_map/ppermute | solution.py:1592
  267.5 27.1 %all-to-all-start.8 = ((bf16[16,16,1024]{2,1,0:T(8,128)(2,1)}), bf16[16,16,1024]{2,1,0:T(8,128)(2,1)S(1)}, u32[]{:S(2)}, u32[]{:S(2)}) async-start(bf16[16,16,1024]{2,1,0:T(8,128)(2,1)} %shard_map.344), calls=%async_computation.8 | async-start | bytes 1048576 | tf_op jit(solution)/shard_map/all_to_all | solution.py:1604
  277.8 14.2 %collective-permute-start.44 = (bf16[32,2432]{1,0:T(8,128)(2,1)}, bf16[32,2432]{1,0:T(8,128)(2,1)S(1)}, u32[]{:S(2)}, u32[]{:S(2)}) collective-permute-start(bf16[32,2432]{1,0:T(8,128)(2,1)} %get-tuple-element.144), channel_id=1, source_target_pairs={{0,16},{2,18},{4,20},{6,22},{8,24},{10,26},{12,28},{14,30},{16,0},... | collective-permute-start | bytes 466952 | tf_op jit(solution)/shard_map/ppermute | solution.py:1592
  (101 other events, 738.5 us)
where the time goes:
time: 307 us; the launch traced here: 305 us
  starting transfers between devices  101 us (33%)
  waiting for transfers between devices  101 us (33%)
  Pallas kernels  71.4 us (23%)
  local copies, waits for them, and re-layouts  24.1 us (8%)
  other arithmetic  6.59 us (2%)
    pallas_call x15, Pallas kernels, run_kernel(): pl.pallas_call(body, out_shape=[jax.ShapeDtypeStruct(shape, kind) for sha...  71.4 us
    ppermute x30, waiting for transfers between devices, permute_three(): lax.ppermute(piece, 'seq', flip(step * (k + 1), ranks))  61.3 us
    all_to_all x9, waiting for transfers between devices, exchange(): return lax.all_to_all(values, axes, 0, 0, tiled=True)  36.8 us
    ppermute x30, starting transfers between devices, permute_three(): lax.ppermute(piece, 'seq', flip(step * (k + 1), ranks))  35.9 us
    all_to_all x9, starting transfers between devices, exchange(): return lax.all_to_all(values, axes, 0, 0, tiled=True)  35.9 us
    ppermute x19, starting transfers between devices, swap_cores(): return lax.ppermute(values, 'head', [(0, 1), (1, 0)])  29.1 us
    unnamed x151, local copies, waits for them, and re-layouts  14.8 us
  transfers between devices with their start and end apart: 58, of which 22 were waited for; matrix products, arithmetic and copies ran while one was open for 3% of the time, Pallas kernels for 14%

commit v1 on v0

--- a/solution.py
+++ b/solution.py
@@ -1863,23 +1863,6 @@
     third_total = third_parts[0].astype(f32)
     for piece in third_moved:
         third_total = third_total + piece.astype(f32)
-    early_outs = run_kernel(
-        early_out_kernel,
-        [
-            (shape, f32)
-            for shape in (
-                in_value.shape,
-                in_state.shape,
-                in_rate.shape[::-1],
-                mix_out.shape[::-1],
-                (qkv_proj.shape[1], qkv_proj.shape[0], qkv_proj.shape[2]),
-                in_gate.shape,
-            )
-        ],
-        0,
-        [early_parts[0]] + permute_three(early_parts[1:], 4, ranks),
-    )
-
     my_blocks = jnp.sum(
         jnp.where(jnp.arange(slots_n)[None, :] == my_slot, order, 0), axis=1
     )
@@ -1902,24 +1885,51 @@
         jnp.concatenate([outs, outs_other], axis=2),
         jnp.concatenate([outs_other, outs], axis=2),
     )
-    return (
-        outs[0],
-        outs[1],
+    small_outs = [
         small_total[7],
-        early_outs[0],
-        early_outs[5],
-        early_outs[1],
-        early_outs[2].T,
         small_total[6, RATE_AT : RATE_AT + HPG],
         small_total[6, LANES + RATE_AT : LANES + RATE_AT + HPG],
         small_total[0:4],
         small_total[4],
         small_total[5],
+        small_total[8],
+        small_total[9],
+    ]
+    early_outs = run_kernel(
+        early_out_kernel,
+        [
+            (shape, f32)
+            for shape in (
+                in_value.shape,
+                in_state.shape,
+                in_rate.shape[::-1],
+                mix_out.shape[::-1],
+                (qkv_proj.shape[1], qkv_proj.shape[0], qkv_proj.shape[2]),
+                in_gate.shape,
+            )
+        ],
+        0,
+        [early_parts[0]] + permute_three(early_parts[1:], 4, ranks),
+        after=[outs] + small_outs,
+    )
+    return (
+        outs[0],
+        outs[1],
+        small_outs[0],
+        early_outs[0],
+        early_outs[5],
+        early_outs[1],
+        early_outs[2].T,
+        small_outs[1],
+        small_outs[2],
+        small_outs[3],
+        small_outs[4],
+        small_outs[5],
         early_outs[3].T,
-        small_total[8],
+        small_outs[6],
         early_outs[4].transpose(1, 0, 2),
         third_total[:, 2048:2304].T,
-        small_total[9],
+        small_outs[7],
         third_total[:, 0:1024],
         third_total[:, 1024:2048].T,
     )

time: 307 us -> 304 us (level); the launches traced: 305 us -> 299 us
  waiting for transfers between devices: 101 us -> 90.7 us
    ppermute x30, waiting for transfers between devices: 61.3 us -> 49.4 us  [permute_three(): lax.ppermute(piece, 'seq', flip(step * (k + 1), ranks))]
    ppermute x19, starting transfers between devices: 29.1 us -> 32.2 us  [swap_cores(): return lax.ppermute(values, 'head', [(0, 1), (1, 0)])]
    unnamed x151 -> x153, local copies, waits for them, and re-layouts: 14.8 us -> 15 us
  transfers between devices with their start and end apart: 58 -> 58, of which waited for: 22 -> 21; matrix products, arithmetic and copies ran while one was open for 3% -> 4% of each run, Pallas kernels for 14% -> 14%
where the time goes in v1:
time: 304 us; the launch traced here: 299 us
  starting transfers between devices  104 us (34%)
  waiting for transfers between devices  90.7 us (30%)
  Pallas kernels  71.5 us (24%)
  local copies, waits for them, and re-layouts  24.3 us (8%)
  other arithmetic  6.61 us (2%)
    pallas_call x15, Pallas kernels, run_kernel(): pl.pallas_call(body, out_shape=[jax.ShapeDtypeStruct(shape, kind) for sha...  71.5 us
    ppermute x30, waiting for transfers between devices, permute_three(): lax.ppermute(piece, 'seq', flip(step * (k + 1), ranks))  49.4 us
    all_to_all x9, waiting for transfers between devices, exchange(): return lax.all_to_all(values, axes, 0, 0, tiled=True)  38.7 us
    ppermute x30, starting transfers between devices, permute_three(): lax.ppermute(piece, 'seq', flip(step * (k + 1), ranks))  35.9 us
    all_to_all x9, starting transfers between devices, exchange(): return lax.all_to_all(values, axes, 0, 0, tiled=True)  35.8 us
    ppermute x19, starting transfers between devices, swap_cores(): return lax.ppermute(values, 'head', [(0, 1), (1, 0)])  32.2 us
    unnamed x153, local copies, waits for them, and re-layouts  15 us
  transfers between devices with their start and end apart: 58, of which 21 were waited for; matrix products, arithmetic and copies ran while one was open for 4% of the time, Pallas kernels for 14%

profile of v1, /device:TPU:1, one launch (start us, length us, event | category | flops | bytes accessed | tf_op | source)
XLA Modules:
  0.0 298.8 jit_solution(11740761573224807473)
XLA Ops:
  12.9 6.1 %collective-permute-done.3 = bf16[32,2560]{1,0:T(8,128)(2,1)S(1)} collective-permute-done((bf16[32,2560]{1,0:T(8,128)(2,1)S(1)}, bf16[32,2560]{1,0:T(8,128)(2,1)S(1)}, u32[]{:S(2)}, u32[]{:S(2)}) %collective-permute-start.3) | collective-permute-done | bytes 163872 | tf_op jit(solution)/shard_map/ppermute | solution.py:1592
  22.1 3.8 %collective-permute-start.7 = (bf16[32,2304]{1,0:T(8,128)(2,1)}, bf16[32,2304]{1,0:T(8,128)(2,1)S(1)}, u32[]{:S(2)}, u32[]{:S(2)}) collective-permute-start(bf16[32,2304]{1,0:T(8,128)(2,1)} %shard_map.339), channel_id=1, source_target_pairs={{0,8},{2,10},{4,12},{6,14},{8,0},{10,2},{12,4},{14,6},{16,24},{18,... | collective-permute-start | bytes 442376 | tf_op jit(solution)/shard_map/ppermute | solution.py:1592
  31.3 5.1 %collective-permute-done.9.refs_3_ = bf16[32,2304]{1,0:T(8,128)(2,1)S(1)} collective-permute-done((bf16[32,2304]{1,0:T(8,128)(2,1)}, bf16[32,2304]{1,0:T(8,128)(2,1)S(1)}, u32[]{:S(2)}, u32[]{:S(2)}) %collective-permute-start.9) | collective-permute-done | bytes 147488 | tf_op jit(solution)/shard_map/ppermute | solution.py:1592
  36.4 5.3 %collective-permute-start.10 = (bf16[128,1280]{1,0:T(8,128)(2,1)}, bf16[128,1280]{1,0:T(8,128)(2,1)}, u32[]{:S(2)}, u32[]{:S(2)}) collective-permute-start(bf16[128,1280]{1,0:T(8,128)(2,1)} %copy-done.2), channel_id=1, source_target_pairs={{0,1},{1,0},{2,3},{3,2},{4,5},{5,4},{6,7},{7,6},{8,9},{9,8},{10,11... | collective-permute-start | bytes 983048 | tf_op jit(solution)/shard_map/ppermute | solution.py:1587
  45.4 5.3 %collective-permute-start.17 = (bf16[128,1280]{1,0:T(8,128)(2,1)S(1)}, bf16[128,1280]{1,0:T(8,128)(2,1)S(1)}, u32[]{:S(2)}, u32[]{:S(2)}) collective-permute-start(bf16[128,1280]{1,0:T(8,128)(2,1)S(1)} %pad_maximum_fusion.2.refs_11_.refs_13_), channel_id=1, source_target_pairs={{0,1},{1,0},{2,3},{3,2},{4,5},{5,4},{6,7},{7,6},{8,9},{9,8},{10,11... | collective-permute-start | bytes 983048 | tf_op jit(solution)/shard_map/ppermute | solution.py:1587
  56.7 6.7 %in_kernel.1 = (bf16[160,512]{1,0:T(8,128)(2,1)}, bf16[160,512]{1,0:T(8,128)(2,1)}, bf16[160,1024]{1,0:T(8,128)(2,1)}, f32[128,1024]{1,0:T(8,128)}, f32[128,1024...) custom-call(s32[2]{0:T(128)} %pad_add_fusion.refs_0_, ...), custom_call_target="tpu_custom_call" | custom-call | tf_op jit(solution)/shard_map/in_kernel/pallas_call | solution.py:1555
  64.2 4.7 %all-to-all-start = ((bf16[32,16,128]{2,1,0:T(8,128)(2,1)}), bf16[32,16,128]{2,1,0:T(8,128)(2,1)S(1)}, u32[]{:S(2)}, u32[]{:S(2)}) async-start(bf16[32,16,128]{2,1,0:T(8,128)(2,1)} %shard_map.341), calls=%async_computation | async-start | bytes 262144 | tf_op jit(solution)/shard_map/all_to_all | solution.py:1604
  69.7 7.3 %all-to-all-done.refs_2_ = bf16[32,16,128]{2,1,0:T(8,128)(2,1)S(1)} async-done(((bf16[32,16,128]{2,1,0:T(8,128)(2,1)}), bf16[32,16,128]{2,1,0:T(8,128)(2,1)S(1)}, u32[]{:S(2)}, u32[]{:S(2)}) %all-to-all-start) | async-done | bytes 131104 | tf_op jit(solution)/shard_map/all_to_all | solution.py:1604
  82.0 8.3 %all-to-all-done.1.refs_2_ = f32[32,8,128]{2,1,0:T(8,128)S(1)} async-done(((f32[32,8,128]{2,1,0:T(8,128)}), f32[32,8,128]{2,1,0:T(8,128)S(1)}, u32[]{:S(2)}, u32[]{:S(2)}) %all-to-all-start.1) | async-done | bytes 131104 | tf_op jit(solution)/shard_map/all_to_all | solution.py:1604
  90.9 5.5 %mix_kernel.1 = (f32[128,1024]{1,0:T(8,128)}, bf16[128,1024]{1,0:T(8,128)(2,1)}, f32[128,512]{1,0:T(8,128)}, bf16[128,512]{1,0:T(8,128)(2,1)}, bf16[16,96,128]{2,1,0:T(8,128)(2,1)}) custom-call(s32[2]{0:T(128)} %pad_add_fusion.refs_0_, bf16[160,512]{1,0:T(8,128)(2,1)} %get-tuple-element.87.refs_1_.refs_11_, f32[32,8,128]{2,1,0:T(8,128)} %copy-done.33, ...), custom_call_target="tpu_custom_call" | custom-call | tf_op jit(solution)/shard_map/mix_kernel/pallas_call | solution.py:1555
  97.5 3.7 %all-to-all-start.2 = ((bf16[16,96,128]{2,1,0:T(8,128)(2,1)}), bf16[16,96,128]{2,1,0:T(8,128)(2,1)S(1)}, u32[]{:S(2)}, u32[]{:S(2)}) async-start(bf16[16,96,128]{2,1,0:T(8,128)(2,1)} %shard_map.342), calls=%async_computation.2 | async-start | bytes 786432 | tf_op jit(solution)/shard_map/all_to_all | solution.py:1604
  103.4 8.6 %all-to-all-done.2.refs_2_ = bf16[16,96,128]{2,1,0:T(8,128)(2,1)S(1)} async-done(((bf16[16,96,128]{2,1,0:T(8,128)(2,1)}), bf16[16,96,128]{2,1,0:T(8,128)(2,1)S(1)}, u32[]{:S(2)}, u32[]{:S(2)}) %all-to-all-start.2) | async-done | bytes 393248 | tf_op jit(solution)/shard_map/all_to_all | solution.py:1604
  116.9 6.4 %attend_kernel.1 = (bf16[16,32,128]{2,1,0:T(8,128)(2,1)}, f32[1024,1]{1,0:T(8,128)}, f32[1024,64]{1,0:T(8,128)}) custom-call(s32[2]{0:T(128)} %pad_add_fusion.refs_0_, s32[2,32]{1,0:T(2,128)} %refs_1_.9, bf16[16,96,128]{2,1,0:T(8,128)(2,1)} %copy-done.5, bf16[16,96,128]{2,1,0:T(8,128)(2,1)} %copy-done.22), custom_call_target="tpu_custom_call" | custom-call | tf_op jit(solution)/shard_map/attend_kernel/pallas_call | solution.py:1555
  124.6 3.7 %all-to-all-start.3 = ((bf16[16,32,128]{2,1,0:T(8,128)(2,1)}), bf16[16,32,128]{2,1,0:T(8,128)(2,1)S(1)}, u32[]{:S(2)}, u32[]{:S(2)}) async-start(bf16[16,32,128]{2,1,0:T(8,128)(2,1)} %get-tuple-element.96), calls=%async_computation.3 | async-start | bytes 262144 | tf_op jit(solution)/shard_map/all_to_all | solution.py:1604
  128.3 6.4 %all-to-all-done.3.refs_1_ = bf16[16,32,128]{2,1,0:T(8,128)(2,1)S(1)} async-done(((bf16[16,32,128]{2,1,0:T(8,128)(2,1)}), bf16[16,32,128]{2,1,0:T(8,128)(2,1)S(1)}, u32[]{:S(2)}, u32[]{:S(2)}) %all-to-all-start.3) | async-done | bytes 131104 | tf_op jit(solution)/shard_map/all_to_all | solution.py:1604
  135.6 7.8 %mlp_kernel.1 = (f32[128,512]{1,0:T(8,128)}, f32[128,512]{1,0:T(8,128)}, bf16[256,512]{1,0:T(8,128)(2,1)}, bf16[128,3328]{1,0:T(8,128)(2,1)}, bf16[128,3328]{1,0...) custom-call(s32[2]{0:T(128)} %pad_add_fusion.refs_0_, ...), custom_call_target="tpu_custom_call" | custom-call | tf_op jit(solution)/shard_map/mlp_kernel/pallas_call | solution.py:1555
  145.2 3.5 %all-to-all-start.4 = ((bf16[16,32,128]{2,1,0:T(8,128)(2,1)}), bf16[16,32,128]{2,1,0:T(8,128)(2,1)S(1)}, u32[]{:S(2)}, u32[]{:S(2)}) async-start(bf16[16,32,128]{2,1,0:T(8,128)(2,1)} %get-tuple-element.102), calls=%async_computation.4 | async-start | bytes 262144 | tf_op jit(solution)/shard_map/all_to_all | solution.py:1604
  149.7 3.6 %third_grad_kernel.1 = (bf16[128,2304]{1,0:T(8,128)(2,1)}, bf16[128,2304]{1,0:T(8,128)(2,1)}, bf16[128,2304]{1,0:T(8,128)(2,1)}, bf16[128,2304]{1,0:T(8,128)(2,1)}) custom-call(bf16[128,3328]{1,0:T(8,128)(2,1)} %get-tuple-element.104.refs_0_, bf16[128,3328]{1,0:T(8,128)(2,1)} %copy-done.35, bf16[256,512]{1,0:T(8,128)(2,1)} %get-tuple-element.106.refs_2_), custom_call_target="tpu_custom_call" | custom-call | tf_op jit(solution)/shard_map/third_grad_kernel/pallas_call | solution.py:1555
  156.6 9.2 %attend_back_kernel.1 = (f32[16,96,128]{2,1,0:T(8,128)}, bf16[16,96,128]{2,1,0:T(8,128)(2,1)}) custom-call(s32[2]{0:T(128)} %pad_add_fusion.refs_0_, s32[2,32]{1,0:T(2,128)} %refs_1_.9, bf16[16,96,128]{2,1,0:T(8,128)(2,1)} %copy-done.5, bf16[16,96,128]{2,1,0:T(8,128)(2,1)} %copy-done.22, bf16[16,32,128]{2,1,0:T(8,128)(2,1)} %copy-done.48, ...), custom_call_target="tpu_custom_call" | custom-call | tf_op jit(solution)/shard_map/attend_back_kernel/pallas_call | solution.py:1555
  170.5 3.8 %all-to-all-start.5 = ((bf16[16,96,128]{2,1,0:T(8,128)(2,1)}), bf16[16,96,128]{2,1,0:T(8,128)(2,1)S(1)}, u32[]{:S(2)}, u32[]{:S(2)}) async-start(bf16[16,96,128]{2,1,0:T(8,128)(2,1)} %add_convert_fusion), calls=%async_computation.5 | async-start | bytes 786432 | tf_op jit(solution)/shard_map/all_to_all | solution.py:1604
  176.5 16.2 %collective-permute-done.31.refs_21_.refs_1_ = bf16[128,2304]{1,0:T(8,128)(2,1)S(1)} collective-permute-done((bf16[128,2304]{1,0:T(8,128)(2,1)S(1)}, bf16[128,2304]{1,0:T(8,128)(2,1)S(1)}, u32[]{:S(2)}, u32[]{:S(2)}) %collective-permute-start.31) | collective-permute-done | bytes 589856 | tf_op jit(solution)/shard_map/ppermute | solution.py:1592
  194.9 6.9 %mix_back_kernel.1 = (bf16[128,3328]{1,0:T(8,128)(2,1)}, bf16[128,3328]{1,0:T(8,128)(2,1)}, f32[128,1024]{1,0:T(8,128)}, bf16[128,1024]{1,0:T(8,128)(2,1)}, f32[...) custom-call(s32[2]{0:T(128)} %pad_add_fusion.refs_0_, ...), custom_call_target="tpu_custom_call" | custom-call | tf_op jit(solution)/shard_map/mix_back_kernel/pallas_call | solution.py:1555
  203.6 4.7 %all-to-all-start.6 = ((f32[32,8,128]{2,1,0:T(8,128)}), f32[32,8,128]{2,1,0:T(8,128)S(1)}, u32[]{:S(2)}, u32[]{:S(2)}) async-start(f32[32,8,128]{2,1,0:T(8,128)} %get-tuple-element.117), calls=%async_computation.6 | async-start | bytes 262144 | tf_op jit(solution)/shard_map/all_to_all | solution.py:1604
  209.3 3.2 %second_grad_kernel.1 = (bf16[128,1792]{1,0:T(8,128)(2,1)}, bf16[128,1792]{1,0:T(8,128)(2,1)}, bf16[128,1792]{1,0:T(8,128)(2,1)}, bf16[128,1792]{1,0:T(8,128)(2,1)}) custom-call(bf16[128,3328]{1,0:T(8,128)(2,1)} %get-tuple-element.118.refs_0_, bf16[128,3328]{1,0:T(8,128)(2,1)} %copy-done.34), custom_call_target="tpu_custom_call" | custom-call | tf_op jit(solution)/shard_map/second_grad_kernel/pallas_call | solution.py:1555
  212.5 6.9 %collective-permute-done.34.refs_5_.refs_3_ = bf16[128,2304]{1,0:T(8,128)(2,1)S(1)} collective-permute-done((bf16[128,2304]{1,0:T(8,128)(2,1)S(1)}, bf16[128,2304]{1,0:T(8,128)(2,1)S(1)}, u32[]{:S(2)}, u32[]{:S(2)}) %collective-permute-start.34) | collective-permute-done | bytes 589856 | tf_op jit(solution)/shard_map/ppermute | solution.py:1592
  222.5 4.6 %all-to-all-start.7 = ((f32[32,8,128]{2,1,0:T(8,128)}), f32[32,8,128]{2,1,0:T(8,128)S(1)}, u32[]{:S(2)}, u32[]{:S(2)}) async-start(f32[32,8,128]{2,1,0:T(8,128)} %backward_scan_kernel.1.refs_4_), calls=%async_computation.7 | async-start | bytes 262144 | tf_op jit(solution)/shard_map/all_to_all | solution.py:1604
  232.4 2.9 all-to-all-done.7.refs_1_
  236.0 8.6 %in_back_kernel.1 = (bf16[176,1152]{1,0:T(8,128)(2,1)}, bf16[176,1152]{1,0:T(8,128)(2,1)}, f32[128,512]{1,0:T(8,128)}) custom-call(s32[2]{0:T(128)} %pad_add_fusion.refs_0_, f32[32,8,128]{2,1,0:T(8,128)} %copy-done.49, f32[32,8,128]{2,1,0:T(8,128)} %copy-done.33, f32[2,2,16,512]{3,2,1,0:T(8,128)} %get-tuple-element.122.refs_3_, ...), custom_call_target="tpu_custom_call" | custom-call | tf_op jit(solution)/shard_map/in_back_kernel/pallas_call | solution.py:1555
  245.2 6.1 %collective-permute-done.38.refs_5_.refs_7_ = bf16[128,1792]{1,0:T(8,128)(2,1)S(1)} collective-permute-done((bf16[128,1792]{1,0:T(8,128)(2,1)S(1)}, bf16[128,1792]{1,0:T(8,128)(2,1)S(1)}, u32[]{:S(2)}, u32[]{:S(2)}) %collective-permute-start.38) | collective-permute-done | bytes 458784 | tf_op jit(solution)/shard_map/ppermute | solution.py:1592
  261.9 4.9 %collective-permute-done.40.refs_2_ = bf16[128,640]{1,0:T(8,128)(2,1)S(1)} collective-permute-done((bf16[128,640]{1,0:T(8,128)(2,1)}, bf16[128,640]{1,0:T(8,128)(2,1)S(1)}, u32[]{:S(2)}, u32[]{:S(2)}) %collective-permute-start.40) | collective-permute-done | bytes 163872 | tf_op jit(solution)/shard_map/ppermute | solution.py:1592
  267.6 4.8 %all-to-all-start.8 = ((bf16[16,16,1024]{2,1,0:T(8,128)(2,1)}), bf16[16,16,1024]{2,1,0:T(8,128)(2,1)S(1)}, u32[]{:S(2)}, u32[]{:S(2)}) async-start(bf16[16,16,1024]{2,1,0:T(8,128)(2,1)} %shard_map.344), calls=%async_computation.8 | async-start | bytes 1048576 | tf_op jit(solution)/shard_map/all_to_all | solution.py:1604
  282.5 10.5 %collective-permute-start.42 = (bf16[2,2,64,512]{3,2,1,0:T(8,128)(2,1)S(1)}, bf16[2,2,64,512]{3,2,1,0:T(8,128)(2,1)S(1)}, u32[]{:S(2)}, u32[]{:S(2)}) collective-permute-start(bf16[2,2,64,512]{3,2,1,0:T(8,128)(2,1)S(1)} %maximum_maximum_fusion), channel_id=1, source_target_pairs={{0,1},{1,0},{2,3},{3,2},{4,5},{5,4},{6,7},{7,6},{8,9},{9,8},{10,11... | collective-permute-start | bytes 786440 | tf_op jit(solution)/shard_map/ppermute | solution.py:1587
  (301 shorter events, 102.0 us)
Async XLA Ops:
  10.7 31.7 %collective-permute-start = (f32[8,512]{1,0:T(8,128)S(1)}, f32[8,512]{1,0:T(8,128)S(1)}, u32[]{:S(2)}, u32[]{:S(2)}) collective-permute-start(f32[8,512]{1,0:T(8,128)S(1)} %concatenate.46.refs_4_.refs_8_.refs_14_), channel_id=1, source_target_pairs={{0,1},{1,0},{2,3},{3,2},{4,5},{5,4},{6,7},{7,6},{8,9},{9,8},{10,11... | collective-permute-start | bytes 49160 | tf_op jit(solution)/shard_map/ppermute | solution.py:1587
  19.1 22.6 %collective-permute-start.6 = (bf16[128,1280]{1,0:T(8,128)(2,1)S(1)}, bf16[128,1280]{1,0:T(8,128)(2,1)S(1)}, u32[]{:S(2)}, u32[]{:S(2)}) collective-permute-start(bf16[128,1280]{1,0:T(8,128)(2,1)S(1)} %pad_maximum_fusion.1.refs_1_.refs_6_.refs_20_), channel_id=1, source_target_pairs={{0,6},{2,4},{4,2},{6,0},{8,14},{10,12},{12,10},{14,8},{16,22},{18,... | collective-permute-start | bytes 983048 | tf_op jit(solution)/shard_map/ppermute | solution.py:1592
  28.9 14.2 %collective-permute-start.4 = (bf16[128,1280]{1,0:T(8,128)(2,1)}, bf16[128,1280]{1,0:T(8,128)(2,1)S(1)}, u32[]{:S(2)}, u32[]{:S(2)}) collective-permute-start(bf16[128,1280]{1,0:T(8,128)(2,1)} %copy-done.2), channel_id=1, source_target_pairs={{0,2},{2,0},{4,6},{6,4},{8,10},{10,8},{12,14},{14,12},{16,18},{18,... | collective-permute-start | bytes 983048 | tf_op jit(solution)/shard_map/ppermute | solution.py:1592
  31.0 13.3 %collective-permute-start.5 = (bf16[128,1280]{1,0:T(8,128)(2,1)}, bf16[128,1280]{1,0:T(8,128)(2,1)S(1)}, u32[]{:S(2)}, u32[]{:S(2)}) collective-permute-start(bf16[128,1280]{1,0:T(8,128)(2,1)} %copy-done.2), channel_id=1, source_target_pairs={{0,4},{2,6},{4,0},{6,2},{8,12},{10,14},{12,8},{14,10},{16,20},{18,... | collective-permute-start | bytes 983048 | tf_op jit(solution)/shard_map/ppermute | solution.py:1592
  43.1 20.4 %collective-permute-start.15 = (bf16[128,1280]{1,0:T(8,128)(2,1)S(1)}, bf16[128,1280]{1,0:T(8,128)(2,1)S(1)}, u32[]{:S(2)}, u32[]{:S(2)}) collective-permute-start(bf16[128,1280]{1,0:T(8,128)(2,1)S(1)} %pad_maximum_fusion.2.refs_11_.refs_13_), channel_id=1, source_target_pairs={{0,4},{2,6},{4,0},{6,2},{8,12},{10,14},{12,8},{14,10},{16,20},{18,... | collective-permute-start | bytes 983048 | tf_op jit(solution)/shard_map/ppermute | solution.py:1592
  44.3 24.9 %collective-permute-start.16 = (bf16[128,1280]{1,0:T(8,128)(2,1)S(1)}, bf16[128,1280]{1,0:T(8,128)(2,1)S(1)}, u32[]{:S(2)}, u32[]{:S(2)}) collective-permute-start(bf16[128,1280]{1,0:T(8,128)(2,1)S(1)} %pad_maximum_fusion.2.refs_11_.refs_13_), channel_id=1, source_target_pairs={{0,6},{2,4},{4,2},{6,0},{8,14},{10,12},{12,10},{14,8},{16,22},{18,... | collective-permute-start | bytes 983048 | tf_op jit(solution)/shard_map/ppermute | solution.py:1592
  45.4 24.0 %collective-permute-start.17 = (bf16[128,1280]{1,0:T(8,128)(2,1)S(1)}, bf16[128,1280]{1,0:T(8,128)(2,1)S(1)}, u32[]{:S(2)}, u32[]{:S(2)}) collective-permute-start(bf16[128,1280]{1,0:T(8,128)(2,1)S(1)} %pad_maximum_fusion.2.refs_11_.refs_13_), channel_id=1, source_target_pairs={{0,1},{1,0},{2,3},{3,2},{4,5},{5,4},{6,7},{7,6},{8,9},{9,8},{10,11... | collective-permute-start | bytes 983048 | tf_op jit(solution)/shard_map/ppermute | solution.py:1587
  54.2 42.2 %collective-permute-start.21 = (bf16[128,2304]{1,0:T(8,128)(2,1)S(1)}, bf16[128,2304]{1,0:T(8,128)(2,1)S(1)}, u32[]{:S(2)}, u32[]{:S(2)}) collective-permute-start(bf16[128,2304]{1,0:T(8,128)(2,1)S(1)} %pad_maximum_fusion.refs_19_.refs_6_), channel_id=1, source_target_pairs={{0,2},{2,0},{4,6},{6,4},{8,10},{10,8},{12,14},{14,12},{16,18},{18,... | collective-permute-start | bytes 1769480 | tf_op jit(solution)/shard_map/ppermute | solution.py:1592
  54.6 41.8 %collective-permute-start.22 = (bf16[128,2304]{1,0:T(8,128)(2,1)S(1)}, bf16[128,2304]{1,0:T(8,128)(2,1)S(1)}, u32[]{:S(2)}, u32[]{:S(2)}) collective-permute-start(bf16[128,2304]{1,0:T(8,128)(2,1)S(1)} %pad_maximum_fusion.refs_19_.refs_6_), channel_id=1, source_target_pairs={{0,4},{2,6},{4,0},{6,2},{8,12},{10,14},{12,8},{14,10},{16,20},{18,... | collective-permute-start | bytes 1769480 | tf_op jit(solution)/shard_map/ppermute | solution.py:1592
  64.2 12.9 %all-to-all-start = ((bf16[32,16,128]{2,1,0:T(8,128)(2,1)}), bf16[32,16,128]{2,1,0:T(8,128)(2,1)S(1)}, u32[]{:S(2)}, u32[]{:S(2)}) async-start(bf16[32,16,128]{2,1,0:T(8,128)(2,1)} %shard_map.341), calls=%async_computation | async-start | bytes 262144 | tf_op jit(solution)/shard_map/all_to_all | solution.py:1604
  68.9 13.0 %collective-permute-start.18 = (bf16[128,1280]{1,0:T(8,128)(2,1)S(1)}, bf16[128,1280]{1,0:T(8,128)(2,1)S(1)}, u32[]{:S(2)}, u32[]{:S(2)}) collective-permute-start(bf16[128,1280]{1,0:T(8,128)(2,1)S(1)} %copy-done.7), channel_id=1, source_target_pairs={{0,1},{1,0},{2,3},{3,2},{4,5},{5,4},{6,7},{7,6},{8,9},{9,8},{10,11... | collective-permute-start | bytes 983048 | tf_op jit(solution)/shard_map/ppermute | solution.py:1587
  97.5 14.5 %all-to-all-start.2 = ((bf16[16,96,128]{2,1,0:T(8,128)(2,1)}), bf16[16,96,128]{2,1,0:T(8,128)(2,1)S(1)}, u32[]{:S(2)}, u32[]{:S(2)}) async-start(bf16[16,96,128]{2,1,0:T(8,128)(2,1)} %shard_map.342), calls=%async_computation.2 | async-start | bytes 786432 | tf_op jit(solution)/shard_map/all_to_all | solution.py:1604
  101.2 22.1 %collective-permute-start.24 = (bf16[128,2304]{1,0:T(8,128)(2,1)S(1)}, bf16[128,2304]{1,0:T(8,128)(2,1)S(1)}, u32[]{:S(2)}, u32[]{:S(2)}) collective-permute-start(bf16[128,2304]{1,0:T(8,128)(2,1)S(1)} %copy-done.1), channel_id=1, source_target_pairs={{0,6},{2,4},{4,2},{6,0},{8,14},{10,12},{12,10},{14,8},{16,22},{18,... | collective-permute-start | bytes 1769480 | tf_op jit(solution)/shard_map/ppermute | solution.py:1592
  114.8 13.5 %collective-permute-start.25 = (bf16[128,2304]{1,0:T(8,128)(2,1)S(1)}, bf16[128,2304]{1,0:T(8,128)(2,1)S(1)}, u32[]{:S(2)}, u32[]{:S(2)}) collective-permute-start(bf16[128,2304]{1,0:T(8,128)(2,1)S(1)} %copy-done.1), channel_id=1, source_target_pairs={{0,1},{1,0},{2,3},{3,2},{4,5},{5,4},{6,7},{7,6},{8,9},{9,8},{10,11... | collective-permute-start | bytes 1769480 | tf_op jit(solution)/shard_map/ppermute | solution.py:1587
  114.8 13.5 %collective-permute-start.26 = (bf16[128,2304]{1,0:T(8,128)(2,1)}, bf16[128,2304]{1,0:T(8,128)(2,1)S(1)}, u32[]{:S(2)}, u32[]{:S(2)}) collective-permute-start(bf16[128,2304]{1,0:T(8,128)(2,1)} %copy-done.15), channel_id=1, source_target_pairs={{0,1},{1,0},{2,3},{3,2},{4,5},{5,4},{6,7},{7,6},{8,9},{9,8},{10,11... | collective-permute-start | bytes 1769480 | tf_op jit(solution)/shard_map/ppermute | solution.py:1587
  115.3 13.1 %collective-permute-start.27 = (bf16[128,2304]{1,0:T(8,128)(2,1)}, bf16[128,2304]{1,0:T(8,128)(2,1)}, u32[]{:S(2)}, u32[]{:S(2)}) collective-permute-start(bf16[128,2304]{1,0:T(8,128)(2,1)} %copy-done.16), channel_id=1, source_target_pairs={{0,1},{1,0},{2,3},{3,2},{4,5},{5,4},{6,7},{7,6},{8,9},{9,8},{10,11... | collective-permute-start | bytes 1769480 | tf_op jit(solution)/shard_map/ppermute | solution.py:1587
  170.5 23.5 %all-to-all-start.5 = ((bf16[16,96,128]{2,1,0:T(8,128)(2,1)}), bf16[16,96,128]{2,1,0:T(8,128)(2,1)S(1)}, u32[]{:S(2)}, u32[]{:S(2)}) async-start(bf16[16,96,128]{2,1,0:T(8,128)(2,1)} %add_convert_fusion), calls=%async_computation.5 | async-start | bytes 786432 | tf_op jit(solution)/shard_map/all_to_all | solution.py:1604
  174.3 18.5 %collective-permute-start.31 = (bf16[128,2304]{1,0:T(8,128)(2,1)S(1)}, bf16[128,2304]{1,0:T(8,128)(2,1)S(1)}, u32[]{:S(2)}, u32[]{:S(2)}) collective-permute-start(bf16[128,2304]{1,0:T(8,128)(2,1)S(1)} %copy-done.69), channel_id=1, source_target_pairs={{0,2},{2,0},{4,6},{6,4},{8,10},{10,8},{12,14},{14,12},{16,18},{18,... | collective-permute-start | bytes 1769480 | tf_op jit(solution)/shard_map/ppermute | solution.py:1592
  175.3 18.6 %collective-permute-start.32 = (bf16[128,2304]{1,0:T(8,128)(2,1)S(1)}, bf16[128,2304]{1,0:T(8,128)(2,1)S(1)}, u32[]{:S(2)}, u32[]{:S(2)}) collective-permute-start(bf16[128,2304]{1,0:T(8,128)(2,1)S(1)} %copy-done.68), channel_id=1, source_target_pairs={{0,4},{2,6},{4,0},{6,2},{8,12},{10,14},{12,8},{14,10},{16,20},{18,... | collective-permute-start | bytes 1769480 | tf_op jit(solution)/shard_map/ppermute | solution.py:1592
  202.5 16.9 %collective-permute-start.34 = (bf16[128,2304]{1,0:T(8,128)(2,1)S(1)}, bf16[128,2304]{1,0:T(8,128)(2,1)S(1)}, u32[]{:S(2)}, u32[]{:S(2)}) collective-permute-start(bf16[128,2304]{1,0:T(8,128)(2,1)S(1)} %copy-done.67), channel_id=1, source_target_pairs={{0,6},{2,4},{4,2},{6,0},{8,14},{10,12},{12,10},{14,8},{16,22},{18,... | collective-permute-start | bytes 1769480 | tf_op jit(solution)/shard_map/ppermute | solution.py:1592
  203.6 16.5 %all-to-all-start.6 = ((f32[32,8,128]{2,1,0:T(8,128)}), f32[32,8,128]{2,1,0:T(8,128)S(1)}, u32[]{:S(2)}, u32[]{:S(2)}) async-start(f32[32,8,128]{2,1,0:T(8,128)} %get-tuple-element.117), calls=%async_computation.6 | async-start | bytes 262144 | tf_op jit(solution)/shard_map/all_to_all | solution.py:1604
  222.5 12.8 %all-to-all-start.7 = ((f32[32,8,128]{2,1,0:T(8,128)}), f32[32,8,128]{2,1,0:T(8,128)S(1)}, u32[]{:S(2)}, u32[]{:S(2)}) async-start(f32[32,8,128]{2,1,0:T(8,128)} %backward_scan_kernel.1.refs_4_), calls=%async_computation.7 | async-start | bytes 262144 | tf_op jit(solution)/shard_map/all_to_all | solution.py:1604
  227.1 18.1 %collective-permute-start.36 = (bf16[128,1792]{1,0:T(8,128)(2,1)S(1)}, bf16[128,1792]{1,0:T(8,128)(2,1)S(1)}, u32[]{:S(2)}, u32[]{:S(2)}) collective-permute-start(bf16[128,1792]{1,0:T(8,128)(2,1)S(1)} %copy-done.72), channel_id=1, source_target_pairs={{0,2},{2,0},{4,6},{6,4},{8,10},{10,8},{12,14},{14,12},{16,18},{18,... | collective-permute-start | bytes 1376264 | tf_op jit(solution)/shard_map/ppermute | solution.py:1592
  228.6 16.7 %collective-permute-start.37 = (bf16[128,1792]{1,0:T(8,128)(2,1)S(1)}, bf16[128,1792]{1,0:T(8,128)(2,1)S(1)}, u32[]{:S(2)}, u32[]{:S(2)}) collective-permute-start(bf16[128,1792]{1,0:T(8,128)(2,1)S(1)} %copy-done.71), channel_id=1, source_target_pairs={{0,4},{2,6},{4,0},{6,2},{8,12},{10,14},{12,8},{14,10},{16,20},{18,... | collective-permute-start | bytes 1376264 | tf_op jit(solution)/shard_map/ppermute | solution.py:1592
  229.8 21.6 %collective-permute-start.38 = (bf16[128,1792]{1,0:T(8,128)(2,1)S(1)}, bf16[128,1792]{1,0:T(8,128)(2,1)S(1)}, u32[]{:S(2)}, u32[]{:S(2)}) collective-permute-start(bf16[128,1792]{1,0:T(8,128)(2,1)S(1)} %copy-done.70), channel_id=1, source_target_pairs={{0,6},{2,4},{4,2},{6,0},{8,14},{10,12},{12,10},{14,8},{16,22},{18,... | collective-permute-start | bytes 1376264 | tf_op jit(solution)/shard_map/ppermute | solution.py:1592
  256.4 16.0 %collective-permute-start.46 = (bf16[32,2304]{1,0:T(8,128)(2,1)S(1)}, bf16[32,2304]{1,0:T(8,128)(2,1)S(1)}, u32[]{:S(2)}, u32[]{:S(2)}) collective-permute-start(bf16[32,2304]{1,0:T(8,128)(2,1)S(1)} %copy-done.75), channel_id=1, source_target_pairs={{0,8},{2,10},{4,12},{6,14},{8,0},{10,2},{12,4},{14,6},{16,24},{18,... | collective-permute-start | bytes 442376 | tf_op jit(solution)/shard_map/ppermute | solution.py:1592
  257.4 15.0 %collective-permute-start.47 = (bf16[32,2304]{1,0:T(8,128)(2,1)S(1)}, bf16[32,2304]{1,0:T(8,128)(2,1)S(1)}, u32[]{:S(2)}, u32[]{:S(2)}) collective-permute-start(bf16[32,2304]{1,0:T(8,128)(2,1)S(1)} %copy-done.74), channel_id=1, source_target_pairs={{0,16},{2,18},{4,20},{6,22},{8,24},{10,26},{12,28},{14,30},{16,0},... | collective-permute-start | bytes 442376 | tf_op jit(solution)/shard_map/ppermute | solution.py:1592
  259.1 13.3 %collective-permute-start.48 = (bf16[32,2304]{1,0:T(8,128)(2,1)S(1)}, bf16[32,2304]{1,0:T(8,128)(2,1)S(1)}, u32[]{:S(2)}, u32[]{:S(2)}) collective-permute-start(bf16[32,2304]{1,0:T(8,128)(2,1)S(1)} %copy-done.73), channel_id=1, source_target_pairs={{0,24},{2,26},{4,28},{6,30},{8,16},{10,18},{12,20},{14,22},{16,8},... | collective-permute-start | bytes 442376 | tf_op jit(solution)/shard_map/ppermute | solution.py:1592
  267.6 14.5 %all-to-all-start.8 = ((bf16[16,16,1024]{2,1,0:T(8,128)(2,1)}), bf16[16,16,1024]{2,1,0:T(8,128)(2,1)S(1)}, u32[]{:S(2)}, u32[]{:S(2)}) async-start(bf16[16,16,1024]{2,1,0:T(8,128)(2,1)} %shard_map.344), calls=%async_computation.8 | async-start | bytes 1048576 | tf_op jit(solution)/shard_map/all_to_all | solution.py:1604
  276.6 19.5 %collective-permute-start.43 = (bf16[32,2432]{1,0:T(8,128)(2,1)}, bf16[32,2432]{1,0:T(8,128)(2,1)S(1)}, u32[]{:S(2)}, u32[]{:S(2)}) collective-permute-start(bf16[32,2432]{1,0:T(8,128)(2,1)} %get-tuple-element.143), channel_id=1, source_target_pairs={{0,8},{2,10},{4,12},{6,14},{8,0},{10,2},{12,4},{14,6},{16,24},{18,... | collective-permute-start | bytes 466952 | tf_op jit(solution)/shard_map/ppermute | solution.py:1592
  278.0 18.1 %collective-permute-start.44 = (bf16[32,2432]{1,0:T(8,128)(2,1)}, bf16[32,2432]{1,0:T(8,128)(2,1)S(1)}, u32[]{:S(2)}, u32[]{:S(2)}) collective-permute-start(bf16[32,2432]{1,0:T(8,128)(2,1)} %get-tuple-element.144), channel_id=1, source_target_pairs={{0,16},{2,18},{4,20},{6,22},{8,24},{10,26},{12,28},{14,30},{16,0},... | collective-permute-start | bytes 466952 | tf_op jit(solution)/shard_map/ppermute | solution.py:1592
  280.0 16.1 %collective-permute-start.45 = (bf16[32,2432]{1,0:T(8,128)(2,1)}, bf16[32,2432]{1,0:T(8,128)(2,1)S(1)}, u32[]{:S(2)}, u32[]{:S(2)}) collective-permute-start(bf16[32,2432]{1,0:T(8,128)(2,1)} %get-tuple-element.145), channel_id=1, source_target_pairs={{0,24},{2,26},{4,28},{6,30},{8,16},{10,18},{12,20},{14,22},{16,8},... | collective-permute-start | bytes 466952 | tf_op jit(solution)/shard_map/ppermute | solution.py:1592
  (102 other events, 741.1 us)

commit v2 on v1

--- a/solution.py
+++ b/solution.py
@@ -1861,7 +1861,7 @@
         [first_grads[0]] + first_moved + [second_grads[0]] + second_moved,
     )
     third_total = third_parts[0].astype(f32)
-    for piece in third_moved:
+    for piece in [hold(member, early_parts[0]) for member in third_moved]:
         third_total = third_total + piece.astype(f32)
     my_blocks = jnp.sum(
         jnp.where(jnp.arange(slots_n)[None, :] == my_slot, order, 0), axis=1

time: 304 us -> 305 us (level); the launches traced: 299 us -> 304 us
  waiting for transfers between devices: 90.7 us -> 99.4 us
  starting transfers between devices: 104 us -> 97.7 us
    all_to_all x9, waiting for transfers between devices: 38.7 us -> 47.7 us  [exchange(): return lax.all_to_all(values, axes, 0, 0, tiled=True)]
    ppermute x19, starting transfers between devices: 32.2 us -> 24.7 us  [swap_cores(): return lax.ppermute(values, 'head', [(0, 1), (1, 0)])]
    unnamed x153 -> x163, local copies, waits for them, and re-layouts: 15 us -> 16.1 us
  transfers between devices with their start and end apart: 58 -> 58, of which waited for: 21 -> 22; matrix products, arithmetic and copies ran while one was open for 4% -> 4% of each run, Pallas kernels for 14% -> 14%
where the time goes in v2:
time: 305 us; the launch traced here: 304 us
  waiting for transfers between devices  99.4 us (33%)
  starting transfers between devices  97.7 us (32%)
  Pallas kernels  71.5 us (23%)
  local copies, waits for them, and re-layouts  25.4 us (8%)
  other arithmetic  7.65 us (3%)
    pallas_call x15, Pallas kernels, run_kernel(): pl.pallas_call(body, out_shape=[jax.ShapeDtypeStruct(shape, kind) for sha...  71.5 us
    ppermute x30, waiting for transfers between devices, permute_three(): lax.ppermute(piece, 'seq', flip(step * (k + 1), ranks))  49.2 us
    all_to_all x9, waiting for transfers between devices, exchange(): return lax.all_to_all(values, axes, 0, 0, tiled=True)  47.7 us
    ppermute x30, starting transfers between devices, permute_three(): lax.ppermute(piece, 'seq', flip(step * (k + 1), ranks))  38.3 us
    all_to_all x9, starting transfers between devices, exchange(): return lax.all_to_all(values, axes, 0, 0, tiled=True)  34.7 us
    ppermute x19, starting transfers between devices, swap_cores(): return lax.ppermute(values, 'head', [(0, 1), (1, 0)])  24.7 us
    unnamed x163, local copies, waits for them, and re-layouts  16.1 us
  transfers between devices with their start and end apart: 58, of which 22 were waited for; matrix products, arithmetic and copies ran while one was open for 4% of the time, Pallas kernels for 14%

profile of v2, /device:TPU:1, one launch (start us, length us, event | category | flops | bytes accessed | tf_op | source)
XLA Modules:
  0.0 303.5 jit_solution(119046010896705046)
XLA Ops:
  12.9 6.1 %collective-permute-done.3 = bf16[32,2560]{1,0:T(8,128)(2,1)S(1)} collective-permute-done((bf16[32,2560]{1,0:T(8,128)(2,1)S(1)}, bf16[32,2560]{1,0:T(8,128)(2,1)S(1)}, u32[]{:S(2)}, u32[]{:S(2)}) %collective-permute-start.3) | collective-permute-done | bytes 163872 | tf_op jit(solution)/shard_map/ppermute | solution.py:1592
  22.1 3.8 %collective-permute-start.7 = (bf16[32,2304]{1,0:T(8,128)(2,1)}, bf16[32,2304]{1,0:T(8,128)(2,1)S(1)}, u32[]{:S(2)}, u32[]{:S(2)}) collective-permute-start(bf16[32,2304]{1,0:T(8,128)(2,1)} %shard_map.339), channel_id=1, source_target_pairs={{0,8},{2,10},{4,12},{6,14},{8,0},{10,2},{12,4},{14,6},{16,24},{18,... | collective-permute-start | bytes 442376 | tf_op jit(solution)/shard_map/ppermute | solution.py:1592
  31.3 5.1 %collective-permute-done.9.refs_3_ = bf16[32,2304]{1,0:T(8,128)(2,1)S(1)} collective-permute-done((bf16[32,2304]{1,0:T(8,128)(2,1)}, bf16[32,2304]{1,0:T(8,128)(2,1)S(1)}, u32[]{:S(2)}, u32[]{:S(2)}) %collective-permute-start.9) | collective-permute-done | bytes 147488 | tf_op jit(solution)/shard_map/ppermute | solution.py:1592
  36.4 5.3 %collective-permute-start.10 = (bf16[128,1280]{1,0:T(8,128)(2,1)}, bf16[128,1280]{1,0:T(8,128)(2,1)}, u32[]{:S(2)}, u32[]{:S(2)}) collective-permute-start(bf16[128,1280]{1,0:T(8,128)(2,1)} %copy-done.2), channel_id=1, source_target_pairs={{0,1},{1,0},{2,3},{3,2},{4,5},{5,4},{6,7},{7,6},{8,9},{9,8},{10,11... | collective-permute-start | bytes 983048 | tf_op jit(solution)/shard_map/ppermute | solution.py:1587
  45.4 5.3 %collective-permute-start.17 = (bf16[128,1280]{1,0:T(8,128)(2,1)S(1)}, bf16[128,1280]{1,0:T(8,128)(2,1)S(1)}, u32[]{:S(2)}, u32[]{:S(2)}) collective-permute-start(bf16[128,1280]{1,0:T(8,128)(2,1)S(1)} %pad_maximum_fusion.2.refs_11_.refs_13_), channel_id=1, source_target_pairs={{0,1},{1,0},{2,3},{3,2},{4,5},{5,4},{6,7},{7,6},{8,9},{9,8},{10,11... | collective-permute-start | bytes 983048 | tf_op jit(solution)/shard_map/ppermute | solution.py:1587
  56.7 6.7 %in_kernel.1 = (bf16[160,512]{1,0:T(8,128)(2,1)}, bf16[160,512]{1,0:T(8,128)(2,1)}, bf16[160,1024]{1,0:T(8,128)(2,1)}, f32[128,1024]{1,0:T(8,128)}, f32[128,1024...) custom-call(s32[2]{0:T(128)} %pad_add_fusion.refs_0_, ...), custom_call_target="tpu_custom_call" | custom-call | tf_op jit(solution)/shard_map/in_kernel/pallas_call | solution.py:1555
  64.2 4.7 %all-to-all-start = ((bf16[32,16,128]{2,1,0:T(8,128)(2,1)}), bf16[32,16,128]{2,1,0:T(8,128)(2,1)S(1)}, u32[]{:S(2)}, u32[]{:S(2)}) async-start(bf16[32,16,128]{2,1,0:T(8,128)(2,1)} %shard_map.341), calls=%async_computation | async-start | bytes 262144 | tf_op jit(solution)/shard_map/all_to_all | solution.py:1604
  69.7 7.3 %all-to-all-done.refs_2_ = bf16[32,16,128]{2,1,0:T(8,128)(2,1)S(1)} async-done(((bf16[32,16,128]{2,1,0:T(8,128)(2,1)}), bf16[32,16,128]{2,1,0:T(8,128)(2,1)S(1)}, u32[]{:S(2)}, u32[]{:S(2)}) %all-to-all-start) | async-done | bytes 131104 | tf_op jit(solution)/shard_map/all_to_all | solution.py:1604
  81.9 8.3 %all-to-all-done.1.refs_2_ = f32[32,8,128]{2,1,0:T(8,128)S(1)} async-done(((f32[32,8,128]{2,1,0:T(8,128)}), f32[32,8,128]{2,1,0:T(8,128)S(1)}, u32[]{:S(2)}, u32[]{:S(2)}) %all-to-all-start.1) | async-done | bytes 131104 | tf_op jit(solution)/shard_map/all_to_all | solution.py:1604
  90.8 5.5 %mix_kernel.1 = (f32[128,1024]{1,0:T(8,128)}, bf16[128,1024]{1,0:T(8,128)(2,1)}, f32[128,512]{1,0:T(8,128)}, bf16[128,512]{1,0:T(8,128)(2,1)}, bf16[16,96,128]{2,1,0:T(8,128)(2,1)}) custom-call(s32[2]{0:T(128)} %pad_add_fusion.refs_0_, bf16[160,512]{1,0:T(8,128)(2,1)} %get-tuple-element.87.refs_1_.refs_11_, f32[32,8,128]{2,1,0:T(8,128)} %copy-done.33, ...), custom_call_target="tpu_custom_call" | custom-call | tf_op jit(solution)/shard_map/mix_kernel/pallas_call | solution.py:1555
  97.4 3.7 %all-to-all-start.2 = ((bf16[16,96,128]{2,1,0:T(8,128)(2,1)}), bf16[16,96,128]{2,1,0:T(8,128)(2,1)S(1)}, u32[]{:S(2)}, u32[]{:S(2)}) async-start(bf16[16,96,128]{2,1,0:T(8,128)(2,1)} %shard_map.342), calls=%async_computation.2 | async-start | bytes 786432 | tf_op jit(solution)/shard_map/all_to_all | solution.py:1604
  103.3 8.6 %all-to-all-done.2.refs_2_ = bf16[16,96,128]{2,1,0:T(8,128)(2,1)S(1)} async-done(((bf16[16,96,128]{2,1,0:T(8,128)(2,1)}), bf16[16,96,128]{2,1,0:T(8,128)(2,1)S(1)}, u32[]{:S(2)}, u32[]{:S(2)}) %all-to-all-start.2) | async-done | bytes 393248 | tf_op jit(solution)/shard_map/all_to_all | solution.py:1604
  116.8 6.5 %attend_kernel.1 = (bf16[16,32,128]{2,1,0:T(8,128)(2,1)}, f32[1024,1]{1,0:T(8,128)}, f32[1024,64]{1,0:T(8,128)}) custom-call(s32[2]{0:T(128)} %pad_add_fusion.refs_0_, s32[2,32]{1,0:T(2,128)} %refs_1_.9, bf16[16,96,128]{2,1,0:T(8,128)(2,1)} %copy-done.5, bf16[16,96,128]{2,1,0:T(8,128)(2,1)} %copy-done.22), custom_call_target="tpu_custom_call" | custom-call | tf_op jit(solution)/shard_map/attend_kernel/pallas_call | solution.py:1555
  124.5 3.7 %all-to-all-start.3 = ((bf16[16,32,128]{2,1,0:T(8,128)(2,1)}), bf16[16,32,128]{2,1,0:T(8,128)(2,1)S(1)}, u32[]{:S(2)}, u32[]{:S(2)}) async-start(bf16[16,32,128]{2,1,0:T(8,128)(2,1)} %get-tuple-element.96), calls=%async_computation.3 | async-start | bytes 262144 | tf_op jit(solution)/shard_map/all_to_all | solution.py:1604
  128.3 6.7 %all-to-all-done.3.refs_1_ = bf16[16,32,128]{2,1,0:T(8,128)(2,1)S(1)} async-done(((bf16[16,32,128]{2,1,0:T(8,128)(2,1)}), bf16[16,32,128]{2,1,0:T(8,128)(2,1)S(1)}, u32[]{:S(2)}, u32[]{:S(2)}) %all-to-all-start.3) | async-done | bytes 131104 | tf_op jit(solution)/shard_map/all_to_all | solution.py:1604
  135.8 7.8 %mlp_kernel.1 = (f32[128,512]{1,0:T(8,128)}, f32[128,512]{1,0:T(8,128)}, bf16[256,512]{1,0:T(8,128)(2,1)}, bf16[128,3328]{1,0:T(8,128)(2,1)}, bf16[128,3328]{1,0...) custom-call(s32[2]{0:T(128)} %pad_add_fusion.refs_0_, ...), custom_call_target="tpu_custom_call" | custom-call | tf_op jit(solution)/shard_map/mlp_kernel/pallas_call | solution.py:1555
  145.2 3.5 %all-to-all-start.4 = ((bf16[16,32,128]{2,1,0:T(8,128)(2,1)}), bf16[16,32,128]{2,1,0:T(8,128)(2,1)S(1)}, u32[]{:S(2)}, u32[]{:S(2)}) async-start(bf16[16,32,128]{2,1,0:T(8,128)(2,1)} %get-tuple-element.102), calls=%async_computation.4 | async-start | bytes 262144 | tf_op jit(solution)/shard_map/all_to_all | solution.py:1604
  149.6 3.6 %third_grad_kernel.1 = (bf16[128,2304]{1,0:T(8,128)(2,1)}, bf16[128,2304]{1,0:T(8,128)(2,1)}, bf16[128,2304]{1,0:T(8,128)(2,1)}, bf16[128,2304]{1,0:T(8,128)(2,1)}) custom-call(bf16[128,3328]{1,0:T(8,128)(2,1)} %get-tuple-element.104.refs_0_, bf16[128,3328]{1,0:T(8,128)(2,1)} %copy-done.35, bf16[256,512]{1,0:T(8,128)(2,1)} %get-tuple-element.106.refs_2_), custom_call_target="tpu_custom_call" | custom-call | tf_op jit(solution)/shard_map/third_grad_kernel/pallas_call | solution.py:1555
  156.5 9.2 %attend_back_kernel.1 = (f32[16,96,128]{2,1,0:T(8,128)}, bf16[16,96,128]{2,1,0:T(8,128)(2,1)}) custom-call(s32[2]{0:T(128)} %pad_add_fusion.refs_0_, s32[2,32]{1,0:T(2,128)} %refs_1_.9, bf16[16,96,128]{2,1,0:T(8,128)(2,1)} %copy-done.5, bf16[16,96,128]{2,1,0:T(8,128)(2,1)} %copy-done.22, bf16[16,32,128]{2,1,0:T(8,128)(2,1)} %copy-done.51, ...), custom_call_target="tpu_custom_call" | custom-call | tf_op jit(solution)/shard_map/attend_back_kernel/pallas_call | solution.py:1555
  170.4 3.8 %all-to-all-start.5 = ((bf16[16,96,128]{2,1,0:T(8,128)(2,1)}), bf16[16,96,128]{2,1,0:T(8,128)(2,1)S(1)}, u32[]{:S(2)}, u32[]{:S(2)}) async-start(bf16[16,96,128]{2,1,0:T(8,128)(2,1)} %add_convert_fusion), calls=%async_computation.5 | async-start | bytes 786432 | tf_op jit(solution)/shard_map/all_to_all | solution.py:1604
  176.5 16.2 %collective-permute-done.31.refs_21_.refs_1_ = bf16[128,2304]{1,0:T(8,128)(2,1)S(1)} collective-permute-done((bf16[128,2304]{1,0:T(8,128)(2,1)S(1)}, bf16[128,2304]{1,0:T(8,128)(2,1)S(1)}, u32[]{:S(2)}, u32[]{:S(2)}) %collective-permute-start.31) | collective-permute-done | bytes 589856 | tf_op jit(solution)/shard_map/ppermute | solution.py:1592
  194.8 6.9 %mix_back_kernel.1 = (bf16[128,3328]{1,0:T(8,128)(2,1)}, bf16[128,3328]{1,0:T(8,128)(2,1)}, f32[128,1024]{1,0:T(8,128)}, bf16[128,1024]{1,0:T(8,128)(2,1)}, f32[...) custom-call(s32[2]{0:T(128)} %pad_add_fusion.refs_0_, ...), custom_call_target="tpu_custom_call" | custom-call | tf_op jit(solution)/shard_map/mix_back_kernel/pallas_call | solution.py:1555
  203.6 4.6 %all-to-all-start.6 = ((f32[32,8,128]{2,1,0:T(8,128)}), f32[32,8,128]{2,1,0:T(8,128)S(1)}, u32[]{:S(2)}, u32[]{:S(2)}) async-start(f32[32,8,128]{2,1,0:T(8,128)} %get-tuple-element.117), calls=%async_computation.6 | async-start | bytes 262144 | tf_op jit(solution)/shard_map/all_to_all | solution.py:1604
  209.2 3.3 %second_grad_kernel.1 = (bf16[128,1792]{1,0:T(8,128)(2,1)}, bf16[128,1792]{1,0:T(8,128)(2,1)}, bf16[128,1792]{1,0:T(8,128)(2,1)}, bf16[128,1792]{1,0:T(8,128)(2,1)}) custom-call(bf16[128,3328]{1,0:T(8,128)(2,1)} %get-tuple-element.118.refs_0_, bf16[128,3328]{1,0:T(8,128)(2,1)} %copy-done.34), custom_call_target="tpu_custom_call" | custom-call | tf_op jit(solution)/shard_map/second_grad_kernel/pallas_call | solution.py:1555
  212.5 6.9 %collective-permute-done.34.refs_5_.refs_3_ = bf16[128,2304]{1,0:T(8,128)(2,1)S(1)} collective-permute-done((bf16[128,2304]{1,0:T(8,128)(2,1)S(1)}, bf16[128,2304]{1,0:T(8,128)(2,1)S(1)}, u32[]{:S(2)}, u32[]{:S(2)}) %collective-permute-start.34) | collective-permute-done | bytes 589856 | tf_op jit(solution)/shard_map/ppermute | solution.py:1592
  222.4 4.6 %all-to-all-start.7 = ((f32[32,8,128]{2,1,0:T(8,128)}), f32[32,8,128]{2,1,0:T(8,128)S(1)}, u32[]{:S(2)}, u32[]{:S(2)}) async-start(f32[32,8,128]{2,1,0:T(8,128)} %backward_scan_kernel.1.refs_4_), calls=%async_computation.7 | async-start | bytes 262144 | tf_op jit(solution)/shard_map/all_to_all | solution.py:1604
  235.9 8.6 %in_back_kernel.1 = (bf16[176,1152]{1,0:T(8,128)(2,1)}, bf16[176,1152]{1,0:T(8,128)(2,1)}, f32[128,512]{1,0:T(8,128)}) custom-call(s32[2]{0:T(128)} %pad_add_fusion.refs_0_, f32[32,8,128]{2,1,0:T(8,128)} %copy-done.52, f32[32,8,128]{2,1,0:T(8,128)} %copy-done.33, f32[2,2,16,512]{3,2,1,0:T(8,128)} %get-tuple-element.122.refs_3_, ...), custom_call_target="tpu_custom_call" | custom-call | tf_op jit(solution)/shard_map/in_back_kernel/pallas_call | solution.py:1555
  245.3 6.3 %collective-permute-done.38.refs_5_.refs_7_ = bf16[128,1792]{1,0:T(8,128)(2,1)S(1)} collective-permute-done((bf16[128,1792]{1,0:T(8,128)(2,1)S(1)}, bf16[128,1792]{1,0:T(8,128)(2,1)S(1)}, u32[]{:S(2)}, u32[]{:S(2)}) %collective-permute-start.38) | collective-permute-done | bytes 458784 | tf_op jit(solution)/shard_map/ppermute | solution.py:1592
  262.2 4.5 %collective-permute-done.40.refs_2_ = bf16[128,640]{1,0:T(8,128)(2,1)S(1)} collective-permute-done((bf16[128,640]{1,0:T(8,128)(2,1)S(1)}, bf16[128,640]{1,0:T(8,128)(2,1)S(1)}, u32[]{:S(2)}, u32[]{:S(2)}) %collective-permute-start.40) | collective-permute-done | bytes 163872 | tf_op jit(solution)/shard_map/ppermute | solution.py:1592
  272.7 3.7 %all-to-all-start.8 = ((bf16[16,16,1024]{2,1,0:T(8,128)(2,1)}), bf16[16,16,1024]{2,1,0:T(8,128)(2,1)S(1)}, u32[]{:S(2)}, u32[]{:S(2)}) async-start(bf16[16,16,1024]{2,1,0:T(8,128)(2,1)} %shard_map.344), calls=%async_computation.8 | async-start | bytes 1048576 | tf_op jit(solution)/shard_map/all_to_all | solution.py:1604
  283.5 10.7 %all-to-all-done.8 = bf16[16,16,1024]{2,1,0:T(8,128)(2,1)S(1)} async-done(((bf16[16,16,1024]{2,1,0:T(8,128)(2,1)}), bf16[16,16,1024]{2,1,0:T(8,128)(2,1)S(1)}, u32[]{:S(2)}, u32[]{:S(2)}) %all-to-all-start.8) | async-done | bytes 524320 | tf_op jit(solution)/shard_map/all_to_all | solution.py:1604
  294.6 3.2 %collective-permute-start.42 = (bf16[2,2,64,512]{3,2,1,0:T(8,128)(2,1)S(1)}, bf16[2,2,64,512]{3,2,1,0:T(8,128)(2,1)S(1)}, u32[]{:S(2)}, u32[]{:S(2)}) collective-permute-start(bf16[2,2,64,512]{3,2,1,0:T(8,128)(2,1)S(1)} %maximum_maximum_fusion), channel_id=1, source_target_pairs={{0,1},{1,0},{2,3},{3,2},{4,5},{5,4},{6,7},{7,6},{8,9},{9,8},{10,11... | collective-permute-start | bytes 786440 | tf_op jit(solution)/shard_map/ppermute | solution.py:1587
  (314 shorter events, 107.3 us)
Async XLA Ops:
  10.7 31.7 %collective-permute-start = (f32[8,512]{1,0:T(8,128)S(1)}, f32[8,512]{1,0:T(8,128)S(1)}, u32[]{:S(2)}, u32[]{:S(2)}) collective-permute-start(f32[8,512]{1,0:T(8,128)S(1)} %concatenate.46.refs_4_.refs_8_.refs_14_), channel_id=1, source_target_pairs={{0,1},{1,0},{2,3},{3,2},{4,5},{5,4},{6,7},{7,6},{8,9},{9,8},{10,11... | collective-permute-start | bytes 49160 | tf_op jit(solution)/shard_map/ppermute | solution.py:1587
  19.1 22.6 %collective-permute-start.6 = (bf16[128,1280]{1,0:T(8,128)(2,1)S(1)}, bf16[128,1280]{1,0:T(8,128)(2,1)S(1)}, u32[]{:S(2)}, u32[]{:S(2)}) collective-permute-start(bf16[128,1280]{1,0:T(8,128)(2,1)S(1)} %pad_maximum_fusion.1.refs_1_.refs_6_.refs_20_), channel_id=1, source_target_pairs={{0,6},{2,4},{4,2},{6,0},{8,14},{10,12},{12,10},{14,8},{16,22},{18,... | collective-permute-start | bytes 983048 | tf_op jit(solution)/shard_map/ppermute | solution.py:1592
  28.9 14.2 %collective-permute-start.4 = (bf16[128,1280]{1,0:T(8,128)(2,1)}, bf16[128,1280]{1,0:T(8,128)(2,1)S(1)}, u32[]{:S(2)}, u32[]{:S(2)}) collective-permute-start(bf16[128,1280]{1,0:T(8,128)(2,1)} %copy-done.2), channel_id=1, source_target_pairs={{0,2},{2,0},{4,6},{6,4},{8,10},{10,8},{12,14},{14,12},{16,18},{18,... | collective-permute-start | bytes 983048 | tf_op jit(solution)/shard_map/ppermute | solution.py:1592
  31.0 13.3 %collective-permute-start.5 = (bf16[128,1280]{1,0:T(8,128)(2,1)}, bf16[128,1280]{1,0:T(8,128)(2,1)S(1)}, u32[]{:S(2)}, u32[]{:S(2)}) collective-permute-start(bf16[128,1280]{1,0:T(8,128)(2,1)} %copy-done.2), channel_id=1, source_target_pairs={{0,4},{2,6},{4,0},{6,2},{8,12},{10,14},{12,8},{14,10},{16,20},{18,... | collective-permute-start | bytes 983048 | tf_op jit(solution)/shard_map/ppermute | solution.py:1592
  43.0 20.4 %collective-permute-start.15 = (bf16[128,1280]{1,0:T(8,128)(2,1)S(1)}, bf16[128,1280]{1,0:T(8,128)(2,1)S(1)}, u32[]{:S(2)}, u32[]{:S(2)}) collective-permute-start(bf16[128,1280]{1,0:T(8,128)(2,1)S(1)} %pad_maximum_fusion.2.refs_11_.refs_13_), channel_id=1, source_target_pairs={{0,4},{2,6},{4,0},{6,2},{8,12},{10,14},{12,8},{14,10},{16,20},{18,... | collective-permute-start | bytes 983048 | tf_op jit(solution)/shard_map/ppermute | solution.py:1592
  44.3 24.9 %collective-permute-start.16 = (bf16[128,1280]{1,0:T(8,128)(2,1)S(1)}, bf16[128,1280]{1,0:T(8,128)(2,1)S(1)}, u32[]{:S(2)}, u32[]{:S(2)}) collective-permute-start(bf16[128,1280]{1,0:T(8,128)(2,1)S(1)} %pad_maximum_fusion.2.refs_11_.refs_13_), channel_id=1, source_target_pairs={{0,6},{2,4},{4,2},{6,0},{8,14},{10,12},{12,10},{14,8},{16,22},{18,... | collective-permute-start | bytes 983048 | tf_op jit(solution)/shard_map/ppermute | solution.py:1592
  45.4 24.0 %collective-permute-start.17 = (bf16[128,1280]{1,0:T(8,128)(2,1)S(1)}, bf16[128,1280]{1,0:T(8,128)(2,1)S(1)}, u32[]{:S(2)}, u32[]{:S(2)}) collective-permute-start(bf16[128,1280]{1,0:T(8,128)(2,1)S(1)} %pad_maximum_fusion.2.refs_11_.refs_13_), channel_id=1, source_target_pairs={{0,1},{1,0},{2,3},{3,2},{4,5},{5,4},{6,7},{7,6},{8,9},{9,8},{10,11... | collective-permute-start | bytes 983048 | tf_op jit(solution)/shard_map/ppermute | solution.py:1587
  54.2 42.1 %collective-permute-start.21 = (bf16[128,2304]{1,0:T(8,128)(2,1)S(1)}, bf16[128,2304]{1,0:T(8,128)(2,1)S(1)}, u32[]{:S(2)}, u32[]{:S(2)}) collective-permute-start(bf16[128,2304]{1,0:T(8,128)(2,1)S(1)} %pad_maximum_fusion.refs_19_.refs_6_), channel_id=1, source_target_pairs={{0,2},{2,0},{4,6},{6,4},{8,10},{10,8},{12,14},{14,12},{16,18},{18,... | collective-permute-start | bytes 1769480 | tf_op jit(solution)/shard_map/ppermute | solution.py:1592
  54.6 41.7 %collective-permute-start.22 = (bf16[128,2304]{1,0:T(8,128)(2,1)S(1)}, bf16[128,2304]{1,0:T(8,128)(2,1)S(1)}, u32[]{:S(2)}, u32[]{:S(2)}) collective-permute-start(bf16[128,2304]{1,0:T(8,128)(2,1)S(1)} %pad_maximum_fusion.refs_19_.refs_6_), channel_id=1, source_target_pairs={{0,4},{2,6},{4,0},{6,2},{8,12},{10,14},{12,8},{14,10},{16,20},{18,... | collective-permute-start | bytes 1769480 | tf_op jit(solution)/shard_map/ppermute | solution.py:1592
  64.2 12.9 %all-to-all-start = ((bf16[32,16,128]{2,1,0:T(8,128)(2,1)}), bf16[32,16,128]{2,1,0:T(8,128)(2,1)S(1)}, u32[]{:S(2)}, u32[]{:S(2)}) async-start(bf16[32,16,128]{2,1,0:T(8,128)(2,1)} %shard_map.341), calls=%async_computation | async-start | bytes 262144 | tf_op jit(solution)/shard_map/all_to_all | solution.py:1604
  68.9 13.0 %collective-permute-start.18 = (bf16[128,1280]{1,0:T(8,128)(2,1)S(1)}, bf16[128,1280]{1,0:T(8,128)(2,1)S(1)}, u32[]{:S(2)}, u32[]{:S(2)}) collective-permute-start(bf16[128,1280]{1,0:T(8,128)(2,1)S(1)} %copy-done.7), channel_id=1, source_target_pairs={{0,1},{1,0},{2,3},{3,2},{4,5},{5,4},{6,7},{7,6},{8,9},{9,8},{10,11... | collective-permute-start | bytes 983048 | tf_op jit(solution)/shard_map/ppermute | solution.py:1587
  97.4 14.5 %all-to-all-start.2 = ((bf16[16,96,128]{2,1,0:T(8,128)(2,1)}), bf16[16,96,128]{2,1,0:T(8,128)(2,1)S(1)}, u32[]{:S(2)}, u32[]{:S(2)}) async-start(bf16[16,96,128]{2,1,0:T(8,128)(2,1)} %shard_map.342), calls=%async_computation.2 | async-start | bytes 786432 | tf_op jit(solution)/shard_map/all_to_all | solution.py:1604
  101.1 22.2 %collective-permute-start.24 = (bf16[128,2304]{1,0:T(8,128)(2,1)S(1)}, bf16[128,2304]{1,0:T(8,128)(2,1)S(1)}, u32[]{:S(2)}, u32[]{:S(2)}) collective-permute-start(bf16[128,2304]{1,0:T(8,128)(2,1)S(1)} %copy-done.1), channel_id=1, source_target_pairs={{0,6},{2,4},{4,2},{6,0},{8,14},{10,12},{12,10},{14,8},{16,22},{18,... | collective-permute-start | bytes 1769480 | tf_op jit(solution)/shard_map/ppermute | solution.py:1592
  114.7 13.6 %collective-permute-start.25 = (bf16[128,2304]{1,0:T(8,128)(2,1)S(1)}, bf16[128,2304]{1,0:T(8,128)(2,1)S(1)}, u32[]{:S(2)}, u32[]{:S(2)}) collective-permute-start(bf16[128,2304]{1,0:T(8,128)(2,1)S(1)} %copy-done.1), channel_id=1, source_target_pairs={{0,1},{1,0},{2,3},{3,2},{4,5},{5,4},{6,7},{7,6},{8,9},{9,8},{10,11... | collective-permute-start | bytes 1769480 | tf_op jit(solution)/shard_map/ppermute | solution.py:1587
  114.7 13.6 %collective-permute-start.26 = (bf16[128,2304]{1,0:T(8,128)(2,1)}, bf16[128,2304]{1,0:T(8,128)(2,1)S(1)}, u32[]{:S(2)}, u32[]{:S(2)}) collective-permute-start(bf16[128,2304]{1,0:T(8,128)(2,1)} %copy-done.15), channel_id=1, source_target_pairs={{0,1},{1,0},{2,3},{3,2},{4,5},{5,4},{6,7},{7,6},{8,9},{9,8},{10,11... | collective-permute-start | bytes 1769480 | tf_op jit(solution)/shard_map/ppermute | solution.py:1587
  115.2 13.1 %collective-permute-start.27 = (bf16[128,2304]{1,0:T(8,128)(2,1)}, bf16[128,2304]{1,0:T(8,128)(2,1)}, u32[]{:S(2)}, u32[]{:S(2)}) collective-permute-start(bf16[128,2304]{1,0:T(8,128)(2,1)} %copy-done.16), channel_id=1, source_target_pairs={{0,1},{1,0},{2,3},{3,2},{4,5},{5,4},{6,7},{7,6},{8,9},{9,8},{10,11... | collective-permute-start | bytes 1769480 | tf_op jit(solution)/shard_map/ppermute | solution.py:1587
  170.4 23.5 %all-to-all-start.5 = ((bf16[16,96,128]{2,1,0:T(8,128)(2,1)}), bf16[16,96,128]{2,1,0:T(8,128)(2,1)S(1)}, u32[]{:S(2)}, u32[]{:S(2)}) async-start(bf16[16,96,128]{2,1,0:T(8,128)(2,1)} %add_convert_fusion), calls=%async_computation.5 | async-start | bytes 786432 | tf_op jit(solution)/shard_map/all_to_all | solution.py:1604
  174.2 18.5 %collective-permute-start.31 = (bf16[128,2304]{1,0:T(8,128)(2,1)S(1)}, bf16[128,2304]{1,0:T(8,128)(2,1)S(1)}, u32[]{:S(2)}, u32[]{:S(2)}) collective-permute-start(bf16[128,2304]{1,0:T(8,128)(2,1)S(1)} %copy-done.72), channel_id=1, source_target_pairs={{0,2},{2,0},{4,6},{6,4},{8,10},{10,8},{12,14},{14,12},{16,18},{18,... | collective-permute-start | bytes 1769480 | tf_op jit(solution)/shard_map/ppermute | solution.py:1592
  175.3 18.6 %collective-permute-start.32 = (bf16[128,2304]{1,0:T(8,128)(2,1)S(1)}, bf16[128,2304]{1,0:T(8,128)(2,1)S(1)}, u32[]{:S(2)}, u32[]{:S(2)}) collective-permute-start(bf16[128,2304]{1,0:T(8,128)(2,1)S(1)} %copy-done.71), channel_id=1, source_target_pairs={{0,4},{2,6},{4,0},{6,2},{8,12},{10,14},{12,8},{14,10},{16,20},{18,... | collective-permute-start | bytes 1769480 | tf_op jit(solution)/shard_map/ppermute | solution.py:1592
  202.4 16.9 %collective-permute-start.34 = (bf16[128,2304]{1,0:T(8,128)(2,1)S(1)}, bf16[128,2304]{1,0:T(8,128)(2,1)S(1)}, u32[]{:S(2)}, u32[]{:S(2)}) collective-permute-start(bf16[128,2304]{1,0:T(8,128)(2,1)S(1)} %copy-done.70), channel_id=1, source_target_pairs={{0,6},{2,4},{4,2},{6,0},{8,14},{10,12},{12,10},{14,8},{16,22},{18,... | collective-permute-start | bytes 1769480 | tf_op jit(solution)/shard_map/ppermute | solution.py:1592
  203.6 16.4 %all-to-all-start.6 = ((f32[32,8,128]{2,1,0:T(8,128)}), f32[32,8,128]{2,1,0:T(8,128)S(1)}, u32[]{:S(2)}, u32[]{:S(2)}) async-start(f32[32,8,128]{2,1,0:T(8,128)} %get-tuple-element.117), calls=%async_computation.6 | async-start | bytes 262144 | tf_op jit(solution)/shard_map/all_to_all | solution.py:1604
  222.4 12.8 %all-to-all-start.7 = ((f32[32,8,128]{2,1,0:T(8,128)}), f32[32,8,128]{2,1,0:T(8,128)S(1)}, u32[]{:S(2)}, u32[]{:S(2)}) async-start(f32[32,8,128]{2,1,0:T(8,128)} %backward_scan_kernel.1.refs_4_), calls=%async_computation.7 | async-start | bytes 262144 | tf_op jit(solution)/shard_map/all_to_all | solution.py:1604
  227.1 18.2 %collective-permute-start.36 = (bf16[128,1792]{1,0:T(8,128)(2,1)}, bf16[128,1792]{1,0:T(8,128)(2,1)S(1)}, u32[]{:S(2)}, u32[]{:S(2)}) collective-permute-start(bf16[128,1792]{1,0:T(8,128)(2,1)} %get-tuple-element.134), channel_id=1, source_target_pairs={{0,2},{2,0},{4,6},{6,4},{8,10},{10,8},{12,14},{14,12},{16,18},{18,... | collective-permute-start | bytes 1376264 | tf_op jit(solution)/shard_map/ppermute | solution.py:1592
  228.5 16.8 %collective-permute-start.37 = (bf16[128,1792]{1,0:T(8,128)(2,1)S(1)}, bf16[128,1792]{1,0:T(8,128)(2,1)S(1)}, u32[]{:S(2)}, u32[]{:S(2)}) collective-permute-start(bf16[128,1792]{1,0:T(8,128)(2,1)S(1)} %copy-done.74), channel_id=1, source_target_pairs={{0,4},{2,6},{4,0},{6,2},{8,12},{10,14},{12,8},{14,10},{16,20},{18,... | collective-permute-start | bytes 1376264 | tf_op jit(solution)/shard_map/ppermute | solution.py:1592
  229.7 21.9 %collective-permute-start.38 = (bf16[128,1792]{1,0:T(8,128)(2,1)S(1)}, bf16[128,1792]{1,0:T(8,128)(2,1)S(1)}, u32[]{:S(2)}, u32[]{:S(2)}) collective-permute-start(bf16[128,1792]{1,0:T(8,128)(2,1)S(1)} %copy-done.73), channel_id=1, source_target_pairs={{0,6},{2,4},{4,2},{6,0},{8,14},{10,12},{12,10},{14,8},{16,22},{18,... | collective-permute-start | bytes 1376264 | tf_op jit(solution)/shard_map/ppermute | solution.py:1592
  256.5 19.9 %collective-permute-start.46 = (bf16[32,2304]{1,0:T(8,128)(2,1)S(1)}, bf16[32,2304]{1,0:T(8,128)(2,1)S(1)}, u32[]{:S(2)}, u32[]{:S(2)}) collective-permute-start(bf16[32,2304]{1,0:T(8,128)(2,1)S(1)} %copy-done.80), channel_id=1, source_target_pairs={{0,8},{2,10},{4,12},{6,14},{8,0},{10,2},{12,4},{14,6},{16,24},{18,... | collective-permute-start | bytes 442376 | tf_op jit(solution)/shard_map/ppermute | solution.py:1592
  257.7 22.0 %collective-permute-start.47 = (bf16[32,2304]{1,0:T(8,128)(2,1)S(1)}, bf16[32,2304]{1,0:T(8,128)(2,1)S(1)}, u32[]{:S(2)}, u32[]{:S(2)}) collective-permute-start(bf16[32,2304]{1,0:T(8,128)(2,1)S(1)} %copy-done.79), channel_id=1, source_target_pairs={{0,16},{2,18},{4,20},{6,22},{8,24},{10,26},{12,28},{14,30},{16,0},... | collective-permute-start | bytes 442376 | tf_op jit(solution)/shard_map/ppermute | solution.py:1592
  259.5 20.8 %collective-permute-start.48 = (bf16[32,2304]{1,0:T(8,128)(2,1)S(1)}, bf16[32,2304]{1,0:T(8,128)(2,1)S(1)}, u32[]{:S(2)}, u32[]{:S(2)}) collective-permute-start(bf16[32,2304]{1,0:T(8,128)(2,1)S(1)} %copy-done.78), channel_id=1, source_target_pairs={{0,24},{2,26},{4,28},{6,30},{8,16},{10,18},{12,20},{14,22},{16,8},... | collective-permute-start | bytes 442376 | tf_op jit(solution)/shard_map/ppermute | solution.py:1592
  270.0 30.8 %collective-permute-start.43 = (bf16[32,2432]{1,0:T(8,128)(2,1)}, bf16[32,2432]{1,0:T(8,128)(2,1)S(1)}, u32[]{:S(2)}, u32[]{:S(2)}) collective-permute-start(bf16[32,2432]{1,0:T(8,128)(2,1)} %get-tuple-element.143), channel_id=1, source_target_pairs={{0,8},{2,10},{4,12},{6,14},{8,0},{10,2},{12,4},{14,6},{16,24},{18,... | collective-permute-start | bytes 466952 | tf_op jit(solution)/shard_map/ppermute | solution.py:1592
  270.5 30.4 %collective-permute-start.44 = (bf16[32,2432]{1,0:T(8,128)(2,1)}, bf16[32,2432]{1,0:T(8,128)(2,1)S(1)}, u32[]{:S(2)}, u32[]{:S(2)}) collective-permute-start(bf16[32,2432]{1,0:T(8,128)(2,1)} %get-tuple-element.144), channel_id=1, source_target_pairs={{0,16},{2,18},{4,20},{6,22},{8,24},{10,26},{12,28},{14,30},{16,0},... | collective-permute-start | bytes 466952 | tf_op jit(solution)/shard_map/ppermute | solution.py:1592
  272.7 21.4 %all-to-all-start.8 = ((bf16[16,16,1024]{2,1,0:T(8,128)(2,1)}), bf16[16,16,1024]{2,1,0:T(8,128)(2,1)S(1)}, u32[]{:S(2)}, u32[]{:S(2)}) async-start(bf16[16,16,1024]{2,1,0:T(8,128)(2,1)} %shard_map.344), calls=%async_computation.8 | async-start | bytes 1048576 | tf_op jit(solution)/shard_map/all_to_all | solution.py:1604
  276.5 24.4 %collective-permute-start.45 = (bf16[32,2432]{1,0:T(8,128)(2,1)S(1)}, bf16[32,2432]{1,0:T(8,128)(2,1)S(1)}, u32[]{:S(2)}, u32[]{:S(2)}) collective-permute-start(bf16[32,2432]{1,0:T(8,128)(2,1)S(1)} %copy-done.77), channel_id=1, source_target_pairs={{0,24},{2,26},{4,28},{6,30},{8,16},{10,18},{12,20},{14,22},{16,8},... | collective-permute-start | bytes 466952 | tf_op jit(solution)/shard_map/ppermute | solution.py:1592
  (107 other events, 724.0 us)
